TPU v7x, 32 devices: a whole 2x2x4 slice. The times are simulated.
32 devices in a mesh: dp: 2 (over core), fsdp: 16 (over z, y, x).
Axes of the slice: x: 2, y: 2, z: 4, core: 2. Of those that a mesh axis runs over, the one named last changes fastest.
Arguments:
- tokens_in: float32 [174080, 256], P(('dp', 'fsdp')), may hold values from -6 to 6
- cotangent: float32 [174080, 256], P(('dp', 'fsdp')), may hold values from -6 to 6
- crop_count: int32 [256], P(('dp', 'fsdp')), may hold values from 1 to 8
- wide_w: float32 [256, 2048], P('fsdp'), may hold values from -0.375 to 0.375
- wide_m: float32 [256, 2048], P('fsdp'), may hold values from -125.168686 to 125.168686
- wide_v: float32 [256, 2048], P('fsdp'), may hold values from 34.816 to 696.32
- wide_ema: float32 [256, 2048], P('fsdp'), may hold values from -0.375 to 0.375
- down_w: float32 [1024, 256], P('fsdp'), may hold values from -0.1875 to 0.1875
- down_m: float32 [1024, 256], P('fsdp'), may hold values from -125.168686 to 125.168686
- down_v: float32 [1024, 256], P('fsdp'), may hold values from 34.816 to 696.32
- down_ema: float32 [1024, 256], P('fsdp'), may hold values from -0.1875 to 0.1875
- small_p: float32 [5888], P('fsdp'), may hold values from -1 to 2, as said below
- small_m: float32 [5888], P('fsdp'), may hold values from -125.168686 to 125.168686
- small_v: float32 [5888], P('fsdp'), may hold values from 34.816 to 696.32
- small_ema: float32 [5888], P('fsdp'), may hold values from -1 to 2, as said below
Outputs:
- block_out: float32 [174080, 256], P(('dp', 'fsdp'))
- grad_in: float32 [174080, 256], P(('dp', 'fsdp'))
- wide_new: float32 [256, 2048], P('fsdp')
- wide_first: float32 [256, 2048], P('fsdp')
- wide_second: float32 [256, 2048], P('fsdp')
- wide_avg: float32 [256, 2048], P('fsdp')
- down_new: float32 [1024, 256], P('fsdp')
- down_first: float32 [1024, 256], P('fsdp')
- down_second: float32 [1024, 256], P('fsdp')
- down_avg: float32 [1024, 256], P('fsdp')
- small_new: float32 [5888], P('fsdp')
- small_first: float32 [5888], P('fsdp')
- small_second: float32 [5888], P('fsdp')
- small_avg: float32 [5888], P('fsdp')
- norms: float32 [2, 4], replicated
Inputs may be any that keep to these rules, and one draw needn't show every extreme that they name: Local crop slots from crop_count onward hold tokens whose output gets no cotangent. `small_p`: gains about one, other entries of either sign. `small_ema`: gains about one, other entries of either sign.
All inputs are finite; a program needn't handle non-finite values.
Results may differ from a plain program's by a relative error of at most 0.0086.
Values may be sent and summed in bfloat16 or wider, within the bound.
No kernel may reach another device: no remote copies, remote signals or barrier semaphores. Data moves between devices by JAX's collectives and lax.ppermute only.
A program may use at most 320 MiB of HBM per device.

v0:
```python
import jax
import jax.numpy as jnp
from jax import lax
from jax.sharding import PartitionSpec as P

D = 256
FF = 1024
HEAD = 32
STRIPE = 7
GRID_L = 14
GRID_S = 6
SMALL = 8
STEP = 10
TOK_IMG = 680


EPSILON = 1e-05
BETA_ONE = 0.9
BETA_TWO = 0.999
ADAM_EPS = 1e-06
DECAY = 0.05
RATE = 0.25
EMA_CEILING = 0.9999


def layer_norm(values, gain, shift):
    center = values - jnp.mean(values, axis=-1, keepdims=True)
    spread = jnp.mean(center * center, axis=-1, keepdims=True)
    return center * lax.rsqrt(spread + EPSILON) * gain + shift


def exact_gelu(values):
    return jax.nn.gelu(values, approximate=False)


def lepe_conv(values, kernel, offset):
    height, breadth = (values.shape[1], values.shape[2])
    padded = jnp.pad(values, ((0, 0), (1, 1), (1, 1), (0, 0)))
    result = jnp.zeros_like(values) + offset
    for row_shift in range(3):
        for col_shift in range(3):
            result = (
                result
                + kernel[row_shift, col_shift]
                * padded[:, row_shift : row_shift + height, col_shift : col_shift + breadth]
            )
    return result


def to_windows(crop_grid, stripe, vertical):
    number, height, breadth, channels = crop_grid.shape
    if vertical:
        reshaped = crop_grid.reshape(number, height, breadth // stripe, stripe, channels).transpose(
            0, 2, 1, 3, 4
        )
        return reshaped.reshape(number * (breadth // stripe), height, stripe, channels)
    return crop_grid.reshape(number * (height // stripe), stripe, breadth, channels)


def from_windows(windows, number, height, breadth, stripe, vertical):
    channels = windows.shape[-1]
    if vertical:
        reshaped = windows.reshape(number, breadth // stripe, height, stripe, channels).transpose(
            0, 2, 1, 3, 4
        )
        return reshaped.reshape(number, height, breadth, channels)
    return windows.reshape(number, height, breadth, channels)


def unpack(vector):
    bounds = [D, D, 3 * D, 9 * D, D, D, D, D, FF, D]
    pieces = []
    position = 0
    for extent in bounds:
        pieces.append(vector[position : position + extent])
        position = position + extent
    return pieces


def split_crops(flat):
    channels = flat.shape[-1]
    images = flat.reshape(-1, TOK_IMG, channels)
    large_count = 2 * GRID_L * GRID_L
    large_grid = images[:, :large_count].reshape(-1, GRID_L, GRID_L, channels)
    small_grid = images[:, large_count:].reshape(-1, GRID_S, GRID_S, channels)
    return (large_grid, small_grid)


def join_crops(large_grid, small_grid):
    channels = large_grid.shape[-1]
    image_count = large_grid.shape[0] // 2
    joined = jnp.concatenate(
        [
            large_grid.reshape(image_count, -1, channels),
            small_grid.reshape(image_count, -1, channels),
        ],
        axis=1,
    )
    return joined.reshape(-1, channels)


def head_views(queries, keys_in, values_in):
    number, height, breadth, channels = queries.shape
    length = height * breadth
    head_count = channels // HEAD
    return (
        queries.reshape(number, length, head_count, HEAD),
        keys_in.reshape(number, length, head_count, HEAD),
        values_in.reshape(number, length, head_count, HEAD),
    )


def stripe_forward(queries, keys_in, values_in, kernel, offset):
    query_heads, key_heads, value_heads = head_views(queries, keys_in, values_in)
    scores = jnp.einsum(
        "nlhd,nmhd->nhlm", query_heads, key_heads, preferred_element_type=jnp.float32
    ) * HEAD ** (-0.5)
    row_peak = jnp.max(scores, axis=-1, keepdims=True)
    exponent = jnp.exp(scores - row_peak)
    row_total = jnp.sum(exponent, axis=-1, keepdims=True)
    weights_soft = (exponent / row_total).astype(jnp.bfloat16)
    log_total = row_peak + jnp.log(row_total)
    mixture = jnp.einsum(
        "nhlm,nmhd->nlhd", weights_soft, value_heads, preferred_element_type=jnp.float32
    )
    return (
        mixture.reshape(queries.shape) + lepe_conv(values_in.astype(jnp.float32), kernel, offset),
        log_total,
    )


def stripe_backward(queries, keys_in, values_in, kernel, offset, log_total, grad_mixed):
    query_heads, key_heads, value_heads = head_views(queries, keys_in, values_in)
    scores = jnp.einsum(
        "nlhd,nmhd->nhlm", query_heads, key_heads, preferred_element_type=jnp.float32
    ) * HEAD ** (-0.5)
    weights_soft = jnp.exp(scores - log_total)
    grad_heads = grad_mixed.reshape(query_heads.shape)
    grad_soft = jnp.einsum(
        "nlhd,nmhd->nhlm", grad_heads, value_heads, preferred_element_type=jnp.float32
    )
    grad_values = jnp.einsum(
        "nhlm,nlhd->nmhd",
        weights_soft.astype(jnp.bfloat16),
        grad_heads,
        preferred_element_type=jnp.float32,
    )
    grad_scores = weights_soft * (
        grad_soft - jnp.sum(weights_soft * grad_soft, axis=-1, keepdims=True)
    )
    grad_raw = (grad_scores * HEAD ** (-0.5)).astype(jnp.bfloat16)
    grad_queries = jnp.einsum(
        "nhlm,nmhd->nlhd", grad_raw, key_heads, preferred_element_type=jnp.float32
    )
    grad_keys = jnp.einsum(
        "nhlm,nlhd->nmhd", grad_raw, query_heads, preferred_element_type=jnp.float32
    )
    unused, conv_back = jax.vjp(lepe_conv, values_in.astype(jnp.float32), kernel, offset)
    grad_conv, grad_kernel, grad_offset = conv_back(grad_mixed.astype(jnp.float32))
    return (
        grad_queries.reshape(queries.shape),
        grad_keys.reshape(queries.shape),
        grad_values.reshape(queries.shape) + grad_conv,
        grad_kernel,
        grad_offset,
    )


def crop_pieces(crop_grid, branch, half, stripe):
    vertical = branch == 1
    return [
        to_windows(
            crop_grid[..., column_base + branch * half : column_base + (branch + 1) * half],
            stripe,
            vertical,
        )
        for column_base in (0, 2 * half, 4 * half)
    ]


def crops_forward(crop_grid, kernel, offset):
    number, height, breadth, triple = crop_grid.shape
    half = triple // 6
    stripe = min(STRIPE, height)
    outputs = []
    totals = []
    for branch in range(2):
        pieces = crop_pieces(crop_grid, branch, half, stripe)
        mixture, log_total = stripe_forward(
            pieces[0],
            pieces[1],
            pieces[2],
            kernel[:, :, branch * half : (branch + 1) * half],
            offset[branch * half : (branch + 1) * half],
        )
        outputs.append(from_windows(mixture, number, height, breadth, stripe, branch == 1))
        totals.append(log_total)
    return (jnp.concatenate(outputs, axis=-1), totals)


def crops_backward(crop_grid, kernel, offset, totals, grad_grid):
    number, height, breadth, triple = crop_grid.shape
    half = triple // 6
    stripe = min(STRIPE, height)
    grad_parts = [[], [], []]
    kernel_parts = []
    offset_parts = []
    for branch in range(2):
        vertical = branch == 1
        pieces = crop_pieces(crop_grid, branch, half, stripe)
        grad_window = to_windows(
            grad_grid[..., branch * half : (branch + 1) * half], stripe, vertical
        )
        results = stripe_backward(
            pieces[0],
            pieces[1],
            pieces[2],
            kernel[:, :, branch * half : (branch + 1) * half],
            offset[branch * half : (branch + 1) * half],
            totals[branch],
            grad_window,
        )
        for member in range(3):
            grad_parts[member].append(
                from_windows(results[member], number, height, breadth, stripe, vertical)
            )
        kernel_parts.append(results[3])
        offset_parts.append(results[4])
    grad_qkv = jnp.concatenate(grad_parts[0] + grad_parts[1] + grad_parts[2], axis=-1)
    return (
        grad_qkv,
        jnp.concatenate(kernel_parts, axis=-1),
        jnp.concatenate(offset_parts, axis=-1),
    )


def crop_mask(counts):
    slots = jnp.arange(SMALL, dtype=jnp.int32)
    live_slots = (slots[None, :] < counts[:, None]).astype(jnp.float32)
    small_part = jnp.repeat(live_slots, GRID_S * GRID_S, axis=1)
    large_part = jnp.ones((counts.shape[0], 2 * GRID_L * GRID_L), jnp.float32)
    return jnp.concatenate([large_part, small_part], axis=1)


def moments(grad, first, second):
    first_new = BETA_ONE * first + (1.0 - BETA_ONE) * grad
    second_new = BETA_TWO * second + (1.0 - BETA_TWO) * grad * grad
    direction = (
        first_new
        / (1.0 - BETA_ONE**STEP)
        / (jnp.sqrt(second_new / (1.0 - BETA_TWO**STEP)) + ADAM_EPS)
    )
    return (first_new, second_new, direction)


def matrix_squares(wide, down):
    column_sq = jnp.sum(wide * wide, axis=0)
    return jnp.stack(
        [
            jnp.sum(column_sq[: 3 * D]),
            jnp.sum(column_sq[3 * D : 4 * D]),
            jnp.sum(column_sq[4 * D :]),
            jnp.sum(down * down),
        ]
    )


def on_device(
    tokens_in,
    cotangent,
    crop_count,
    wide_w,
    wide_m,
    wide_v,
    wide_ema,
    down_w,
    down_m,
    down_v,
    down_ema,
    small_p,
    small_m,
    small_v,
    small_ema,
):
    weight_sq = matrix_squares(wide_w, down_w)
    shipped = (
        wide_w.astype(jnp.bfloat16),
        down_w.astype(jnp.bfloat16),
        small_p.astype(jnp.bfloat16),
    )
    wide_all, down_all, small_all = (
        lax.all_gather(shipped[0], "fsdp", axis=0, tiled=True),
        lax.all_gather(shipped[1], "fsdp", axis=0, tiled=True),
        lax.all_gather(shipped[2], "fsdp", axis=0, tiled=True),
    )
    (
        gain_one,
        shift_one,
        bias_qkv,
        kernel_flat,
        kernel_bias,
        bias_out,
        gain_two,
        shift_two,
        bias_up,
        bias_down,
    ) = unpack(small_all.astype(jnp.float32))
    kernel = kernel_flat.reshape(3, 3, D)
    normed = layer_norm(tokens_in, gain_one, shift_one).astype(jnp.bfloat16)
    projected = (
        jnp.dot(normed, wide_all[:, : 3 * D], preferred_element_type=jnp.float32) + bias_qkv
    ).astype(jnp.bfloat16)
    large_grid, small_grid = split_crops(projected)
    large_mixed, large_totals = crops_forward(large_grid, kernel, kernel_bias)
    small_mixed, small_totals = crops_forward(small_grid, kernel, kernel_bias)
    mixed_low = join_crops(large_mixed, small_mixed).astype(jnp.bfloat16)
    residual = (
        tokens_in
        + jnp.dot(mixed_low, wide_all[:, 3 * D : 4 * D], preferred_element_type=jnp.float32)
        + bias_out
    )
    second = layer_norm(residual, gain_two, shift_two).astype(jnp.bfloat16)
    hidden = jnp.dot(second, wide_all[:, 4 * D :], preferred_element_type=jnp.float32) + bias_up
    activated = exact_gelu(hidden).astype(jnp.bfloat16)
    block_out = (
        residual + jnp.dot(activated, down_all, preferred_element_type=jnp.float32) + bias_down
    )
    back_wide, back_down, back_small = (
        lax.all_gather(shipped[0], "fsdp", axis=0, tiled=True),
        lax.all_gather(shipped[1], "fsdp", axis=0, tiled=True),
        lax.all_gather(shipped[2], "fsdp", axis=0, tiled=True),
    )
    back_pieces = unpack(back_small.astype(jnp.float32))
    back_kernel = back_pieces[3].reshape(3, 3, D)
    live = crop_mask(crop_count).reshape(-1)
    grad_out = cotangent * live[:, None]
    grad_low = grad_out.astype(jnp.bfloat16)
    grad_bias_down = jnp.sum(grad_low.astype(jnp.float32), axis=0)
    grad_down = jnp.dot(activated.T, grad_low, preferred_element_type=jnp.float32)
    grad_act = jnp.dot(grad_low, back_down.T, preferred_element_type=jnp.float32)
    unused, gelu_back = jax.vjp(exact_gelu, hidden)
    grad_hidden = gelu_back(grad_act)[0].astype(jnp.bfloat16)
    grad_bias_up = jnp.sum(grad_hidden.astype(jnp.float32), axis=0)
    grad_up = jnp.dot(second.T, grad_hidden, preferred_element_type=jnp.float32)
    grad_second = jnp.dot(grad_hidden, back_wide[:, 4 * D :].T, preferred_element_type=jnp.float32)
    unused, norm_two_back = jax.vjp(layer_norm, residual, back_pieces[6], back_pieces[7])
    grad_resid_part, grad_gain_two, grad_shift_two = norm_two_back(grad_second)
    grad_resid = grad_out + grad_resid_part
    grad_resid_low = grad_resid.astype(jnp.bfloat16)
    grad_bias_out = jnp.sum(grad_resid_low.astype(jnp.float32), axis=0)
    grad_proj = jnp.dot(mixed_low.T, grad_resid_low, preferred_element_type=jnp.float32)
    grad_mixed = jnp.dot(
        grad_resid_low, back_wide[:, 3 * D : 4 * D].T, preferred_element_type=jnp.float32
    ).astype(jnp.bfloat16)
    grad_large, grad_small_crops = split_crops(grad_mixed)
    large_qkv, large_kernel, large_offset = crops_backward(
        large_grid, back_kernel, back_pieces[4], large_totals, grad_large
    )
    small_qkv, small_kernel, small_offset = crops_backward(
        small_grid, back_kernel, back_pieces[4], small_totals, grad_small_crops
    )
    grad_qkv = join_crops(large_qkv, small_qkv).astype(jnp.bfloat16)
    grad_bias_qkv = jnp.sum(grad_qkv.astype(jnp.float32), axis=0)
    grad_wqkv = jnp.dot(normed.T, grad_qkv, preferred_element_type=jnp.float32)
    grad_normed = jnp.dot(grad_qkv, back_wide[:, : 3 * D].T, preferred_element_type=jnp.float32)
    unused, norm_one_back = jax.vjp(layer_norm, tokens_in, back_pieces[0], back_pieces[1])
    grad_tokens_part, grad_gain_one, grad_shift_one = norm_one_back(grad_normed)
    grad_tokens = grad_resid + grad_tokens_part
    small_terms = jnp.concatenate(
        [
            grad_gain_one,
            grad_shift_one,
            grad_bias_qkv,
            (large_kernel + small_kernel).reshape(-1),
            large_offset + small_offset,
            grad_bias_out,
            grad_gain_two,
            grad_shift_two,
            grad_bias_up,
            grad_bias_down,
        ]
    )
    wide_terms = jnp.concatenate([grad_wqkv, grad_proj, grad_up], axis=1)
    shard_wide, shard_down, shard_small = (
        lax.psum_scatter(wide_terms, "fsdp", scatter_dimension=0, tiled=True),
        lax.psum_scatter(grad_down, "fsdp", scatter_dimension=0, tiled=True),
        lax.psum_scatter(small_terms, "fsdp", scatter_dimension=0, tiled=True),
    )
    shard_wide, shard_down, shard_small = lax.psum((shard_wide, shard_down, shard_small), "dp")
    wide_first, wide_second, wide_dir = moments(shard_wide, wide_m, wide_v)
    down_first, down_second, down_dir = moments(shard_down, down_m, down_v)
    small_first, small_second, small_dir = moments(shard_small, small_m, small_v)
    wide_upd = wide_dir + DECAY * wide_w
    down_upd = down_dir + DECAY * down_w
    update_sq = matrix_squares(wide_upd, down_upd)
    weight_total, update_total = lax.psum((weight_sq, update_sq), "fsdp")
    weight_norm = jnp.sqrt(weight_total)
    update_norm = jnp.sqrt(update_total)
    ratio = weight_norm / update_norm
    column_ratio = jnp.concatenate(
        [
            ratio[0] * jnp.ones((3 * D,), jnp.float32),
            ratio[1] * jnp.ones((D,), jnp.float32),
            ratio[2] * jnp.ones((FF,), jnp.float32),
        ]
    )
    wide_new = wide_w - RATE * column_ratio * wide_upd
    down_new = down_w - RATE * ratio[3] * down_upd
    small_new = small_p - RATE * small_dir
    ema_keep = min(EMA_CEILING, (1.0 + STEP) / (10.0 + STEP))
    wide_avg = ema_keep * wide_ema + (1.0 - ema_keep) * wide_new
    down_avg = ema_keep * down_ema + (1.0 - ema_keep) * down_new
    small_avg = ema_keep * small_ema + (1.0 - ema_keep) * small_new
    norms = jnp.stack([weight_norm, update_norm])
    return (
        block_out,
        grad_tokens,
        wide_new,
        wide_first,
        wide_second,
        wide_avg,
        down_new,
        down_first,
        down_second,
        down_avg,
        small_new,
        small_first,
        small_second,
        small_avg,
        norms,
    )


def solution(mesh):
    in_specs = (
        P(("dp", "fsdp"), None),
        P(("dp", "fsdp"), None),
        P(("dp", "fsdp")),
        P("fsdp", None),
        P("fsdp", None),
        P("fsdp", None),
        P("fsdp", None),
        P("fsdp", None),
        P("fsdp", None),
        P("fsdp", None),
        P("fsdp", None),
        P("fsdp"),
        P("fsdp"),
        P("fsdp"),
        P("fsdp"),
    )
    out_specs = (
        P(("dp", "fsdp"), None),
        P(("dp", "fsdp"), None),
        P("fsdp", None),
        P("fsdp", None),
        P("fsdp", None),
        P("fsdp", None),
        P("fsdp", None),
        P("fsdp", None),
        P("fsdp", None),
        P("fsdp", None),
        P("fsdp"),
        P("fsdp"),
        P("fsdp"),
        P("fsdp"),
        P(),
    )
    return jax.shard_map(
        on_device, mesh=mesh, in_specs=in_specs, out_specs=out_specs, check_vma=False
    )
```

profile of v0, /device:TPU:0, one launch (start us, length us, event | category | flops | bytes accessed | tf_op | source)
XLA Modules:
  0.0 1149.0 jit_solution(494440846947114332)
XLA Ops:
  12.5 78.8 %all-reduce.77 = bf16[5888]{0:T(1024)(128)(2,1)S(1)} all-reduce(bf16[5888]{0:T(1024)(128)(2,1)S(1)} %dynamic-update-slice), channel_id=1, replica_groups=mesh['dp'=2,'fsdp'=16] {'fsdp'}, use_global_device_ids=true, to_apply=%add.77 | all-reduce | flops 5888 | bytes 23552
  103.4 41.1 %all_gather.14 = bf16[1024,256]{1,0:T(8,128)(2,1)} all-gather(bf16[64,256]{1,0:T(8,128)(2,1)S(1)} %convert_element_type.186), channel_id=1, replica_groups=mesh['dp'=2,'fsdp'=16] {'fsdp'}, dimensions={0}, use_global_device_ids=true | all-gather | bytes 557056 | tf_op jit(solution)/shard_map/all_gather | solution.py:293
  148.5 6.7 add_convert_fusion.1
  159.8 8.2 reshape.487
  168.0 5.8 slice_convert_fusion.2
  176.3 7.1 reshape.495
  189.2 6.2 reshape_reshape.41
  195.4 5.6 copy.304
  200.9 5.9 reshape_reshape.42
  206.9 5.6 copy.302
  212.4 5.9 reshape_reshape.43
  218.4 5.6 copy.303
  224.0 5.5 reshape_reshape.40
  234.8 5.5 reshape_reshape.39
  245.7 5.5 reshape_reshape.38
  251.2 5.8 copy.290
  266.9 6.6 copy.292
  273.5 5.9 reshape.488
  295.5 6.6 copy.306
  318.6 5.6 copy.322
  326.6 5.8 copy.321
  334.8 5.6 copy.323
  342.8 5.6 copy.313
  350.7 5.6 copy.312
  358.7 5.6 copy.314
  374.8 5.8 copy.316
  394.7 5.8 copy.325
  418.3 9.3 fusion.172
  427.7 62.2 %convert_reduce_fusion = (f32[1024]{0:T(1024)}, bf16[5440,1024]{1,0:T(8,128)(2,1)S(1)}, f32[5440,1024]{1,0:T(8,128)}) fusion(f32[5440,1024]{1,0:T(8,128)} %fusion.172, f32[1024]{0:T(1024)S(1)} %copy-done.126, bf16[5440,256]{1,0:T(8,128)(2,1)S(1)} %copy-done.28, bf16[1024,256]{1,0:T(8,128)(2,1)S(1)} %copy-done.100), kind=kOutput, calls=%fused_computation.6 | convolution fusion | flops 3269917696 | bytes 59023360 | tf_op jit(solution)/shard_map/dot_general | solution.py:340
  489.9 9.3 multiply_reduce_fusion.4
  499.3 7.4 fusion.227
  506.8 5.5 convert_reduce_fusion.5
  532.6 5.4 fusion.236
  538.1 12.1 %fusion.122 = bf16[64,36,4,32]{1,3,2,0:T(8,128)(2,1)} fusion(bf16[64,36,4,32]{1,3,2,0:T(8,128)(2,1)} %copy.313, f32[64,4,36,36]{2,3,1,0:T(8,128)} %fusion.236, f32[64,4,36,36]{2,3,1,0:T(8,128)} %copy-done.6, f32[64,4,36]{2,1,0:T(4,128)S(1)} %bitcast.317), kind=kOutput, calls=%fused_computation.200 | convolution fusion | flops 24228900 | bytes 3870720 | tf_op jit(solution)/shard_map/nhlm,nmhd->nlhd/dot_general | solution.py:152
  550.2 11.9 %fusion.125 = bf16[64,36,4,32]{1,3,2,0:T(8,128)(2,1)} fusion(bf16[64,36,4,32]{1,3,2,0:T(8,128)(2,1)} %copy.312, f32[64,4,36,36]{2,3,1,0:T(8,128)} %fusion.236, f32[64,4,36,36]{2,3,1,0:T(8,128)} %copy-done.6, f32[64,4,36]{2,1,0:T(4,128)S(1)} %bitcast.318), kind=kOutput, calls=%fused_computation.201 | convolution fusion | flops 24228900 | bytes 3870720 | tf_op jit(solution)/shard_map/nhlm,nlhd->nmhd/dot_general | solution.py:155
  562.1 6.0 fusion.110
  574.2 5.5 fusion.237
  579.8 12.2 %fusion.116 = bf16[64,36,4,32]{1,3,2,0:T(8,128)(2,1)} fusion(bf16[64,36,4,32]{1,3,2,0:T(8,128)(2,1)} %copy.322, f32[64,4,36,36]{2,3,1,0:T(8,128)} %fusion.237, f32[64,4,36,36]{2,3,1,0:T(8,128)} %copy-done.5, f32[64,4,36]{2,1,0:T(4,128)S(1)} %bitcast.320), kind=kOutput, calls=%fused_computation.198 | convolution fusion | flops 24228900 | bytes 3870720 | tf_op jit(solution)/shard_map/nhlm,nmhd->nlhd/dot_general | solution.py:152
  592.0 11.9 %fusion.119 = bf16[64,36,4,32]{1,3,2,0:T(8,128)(2,1)} fusion(bf16[64,36,4,32]{1,3,2,0:T(8,128)(2,1)} %copy.321, f32[64,4,36,36]{2,3,1,0:T(8,128)} %fusion.237, f32[64,4,36,36]{2,3,1,0:T(8,128)} %copy-done.5, f32[64,4,36]{2,1,0:T(4,128)S(1)} %bitcast.321), kind=kOutput, calls=%fused_computation.199 | convolution fusion | flops 24228900 | bytes 3870720 | tf_op jit(solution)/shard_map/nhlm,nlhd->nmhd/dot_general | solution.py:155
  603.9 6.0 fusion.113
  612.4 5.6 copy.327
  618.1 6.5 fusion.234
  627.9 13.5 %fusion.142 = bf16[32,98,4,32]{1,3,2,0:T(8,128)(2,1)} fusion(bf16[32,98,4,32]{1,3,2,0:T(8,128)(2,1)} %copy.289, f32[32,4,98,98]{2,3,1,0:T(8,128)} %fusion.234, f32[32,4,98,98]{2,3,1,0:T(8,128)} %copy-done.4, f32[32,4,98]{2,1,0:T(4,128)S(1)} %bitcast.328), kind=kOutput, calls=%fused_computation.213 | convolution fusion | flops 89752416 | bytes 11490304 | tf_op jit(solution)/shard_map/nhlm,nmhd->nlhd/dot_general | solution.py:152
  641.4 13.2 %fusion.145 = bf16[32,98,4,32]{1,3,2,0:T(8,128)(2,1)} fusion(bf16[32,98,4,32]{1,3,2,0:T(8,128)(2,1)S(1)} %copy-done.60, f32[32,4,98,98]{2,3,1,0:T(8,128)} %fusion.234, f32[32,4,98,98]{2,3,1,0:T(8,128)} %copy-done.4, f32[32,4,98]{2,1,0:T(4,128)S(1)} %bitcast.329), kind=kOutput, calls=%fused_computation.214 | convolution fusion | flops 89752416 | bytes 11490304 | tf_op jit(solution)/shard_map/nhlm,nlhd->nmhd/dot_general | solution.py:155
  657.2 6.1 copy.334
  663.3 6.4 fusion.235
  673.1 13.5 %fusion.136 = bf16[32,98,4,32]{1,3,2,0:T(8,128)(2,1)} fusion(bf16[32,98,4,32]{1,3,2,0:T(8,128)(2,1)} %copy.303, f32[32,4,98,98]{2,3,1,0:T(8,128)} %fusion.235, f32[32,4,98,98]{2,3,1,0:T(8,128)} %copy-done.3, f32[32,4,98]{2,1,0:T(4,128)S(1)} %bitcast.331), kind=kOutput, calls=%fused_computation.211 | convolution fusion | flops 89752416 | bytes 11490304 | tf_op jit(solution)/shard_map/nhlm,nmhd->nlhd/dot_general | solution.py:152
  686.7 13.1 %fusion.139 = bf16[32,98,4,32]{1,3,2,0:T(8,128)(2,1)} fusion(bf16[32,98,4,32]{1,3,2,0:T(8,128)(2,1)S(1)} %copy-done.58, f32[32,4,98,98]{2,3,1,0:T(8,128)} %fusion.235, f32[32,4,98,98]{2,3,1,0:T(8,128)} %copy-done.3, f32[32,4,98]{2,1,0:T(4,128)S(1)} %bitcast.332), kind=kOutput, calls=%fused_computation.212 | convolution fusion | flops 89752416 | bytes 11490304 | tf_op jit(solution)/shard_map/nhlm,nlhd->nmhd/dot_general | solution.py:155
  700.0 6.3 fusion.154
  716.1 15.3 %multiply_convert_fusion = bf16[5440,1024]{1,0:T(8,128)(2,1)S(1)} fusion(f32[5440,1024]{1,0:T(8,128)} %get-tuple-element.82, f32[5440,1024]{1,0:T(8,128)} %fusion.172, f32[1024]{0:T(1024)S(1)} %copy-done.126), kind=kLoop, calls=%fused_computation.8 | loop fusion | flops 22282240 | bytes 55709696 | tf_op jit(solution)/shard_map/convert_element_type | solution.py:324
  782.0 5.6 copy.349
  787.7 6.0 reshape.506
  793.7 5.6 copy.362
  799.4 6.0 reshape.507
  884.7 14.9 %convert_reduce_fusion.1 = (f32[768]{0:T(1024)S(1)}, bf16[8,680,768]{1,0,2:T(8,128)(2,1)}) fusion(bf16[8,288,768]{1,0,2:T(8,128)(2,1)S(1)} %constant_dynamic-update-slice_fusion.6, bf16[8,392,768]{1,0,2:T(8,128)(2,1)} %constant_dynamic-update-slice_fusion), kind=kLoop, calls=%fused_computation.23 | loop fusion | flops 25066752 | bytes 16714752 | tf_op jit(solution)/shard_map/reduce_sum | solution.py:363
  899.6 13.3 %copy.397 = bf16[8,680,768]{2,1,0:T(8,128)(2,1)} copy(bf16[8,680,768]{1,0,2:T(8,128)(2,1)} %get-tuple-element.87) | data formatting | bytes 16711680 | tf_op jit(solution)/shard_map/convert_element_type | solution.py:362
  913.0 8.2 fusion.221
  926.6 9.1 fusion.220
  937.6 9.6 multiply_reduce_fusion.5
  958.6 7.4 fusion.226
  970.0 45.5 %reduce-scatter.3.cloned.1.call-done = f32[16,2048]{1,0:T(8,128)} async-done(((f32[256,2048]{1,0:T(8,128)}), f32[16,2048]{1,0:T(8,128)}) %reduce-scatter.3.cloned.1.call-update) | async-done | bytes 131088 | tf_op jit(solution)/shard_map/reduce_scatter | solution.py:385
  1018.1 15.2 %all-reduce.83.cloned.1.call-done = (f32[64,256]{1,0:T(8,128)}, f32[16,2048]{1,0:T(8,128)}) async-done(((f32[64,256]{1,0:T(8,128)}, f32[16,2048]{1,0:T(8,128)}), (f32[64,256]{1,0:T(8,128)}, f32[16,2048]{1,0:T(8,128)})) %all-reduce.83.cloned.1.call-update) | async-done | bytes 196624 | tf_op jit(solution)/shard_map/psum | solution.py:389
  1045.0 11.5 %fusion.11 = f32[5440,256]{1,0:T(8,128)} fusion(f32[5440,256]{1,0:T(8,128)} %copy-done, bf16[5440,1024]{1,0:T(8,128)(2,1)} %copy-done.7, bf16[1024,256]{1,0:T(8,128)(2,1)} %all_gather.14, f32[256]{0:T(256)S(1)} %copy-done.196), kind=kOutput, calls=%fused_computation.69 | convolution fusion | flops 2854912000 | bytes 22807552 | tf_op jit(solution)/shard_map/dot_general | solution.py:326
  1056.5 77.0 %all-reduce.79 = (f32[4]{0:T(128)S(1)}, f32[4]{0:T(128)S(1)}, f32[5888]{0:T(1024)S(1)}) all-reduce(f32[4]{0:T(128)S(1)} %pad_maximum_fusion.5, f32[4]{0:T(128)S(1)} %pad_maximum_fusion.4, f32[5888]{0:T(1024)S(1)} %copy-done.123), channel_id=1, replica_groups=mesh['dp'=2,'fsdp'=16] {'fsdp'}, use_global_device_ids=true, to_apply=%region_35.36 | all-reduce | flops 5896 | bytes 47168 | tf_op jit(solution)/shard_map/psum | solution.py:396
  (635 shorter events, 361.1 us)
Async XLA Ops:
  7.2 141.3 %all-gather.2.cloned.1.call-start = ((), (), s32[]{:S(2)}) async-start(), calls=%async_computation.2 | async-start | bytes 1114112 | tf_op jit(solution)/shard_map/all_gather | solution.py:292
  8.8 961.2 %reduce-scatter.5.cloned.1.call-start = ((), (), s32[]{:S(2)}) async-start(), calls=%async_computation.4 | async-start | bytes 1114112 | tf_op jit(solution)/shard_map/reduce_scatter | solution.py:386
  92.2 52.3 %copy-start.109 = (f32[5440]{0:T(1024)}, f32[5440]{0:T(1024)S(1)}, u32[]{:S(2)}) copy-start(f32[5440]{0:T(1024)S(1)} %mul.1153) | copy-start | bytes 65284
  97.7 50.8 %copy-start.124 = (f32[256]{0:T(256)}, f32[256]{0:T(256)S(1)}, u32[]{:S(2)}) copy-start(f32[256]{0:T(256)S(1)} %get-tuple-element.155) | copy-start | bytes 3076
  97.7 50.8 %copy-start.161 = (f32[256]{0:T(256)}, f32[256]{0:T(256)S(1)}, u32[]{:S(2)}) copy-start(f32[256]{0:T(256)S(1)} %get-tuple-element.156) | copy-start | bytes 3076
  98.3 305.3 %copy-start.131 = (f32[128]{0:T(128)}, f32[128]{0:T(128)S(1)}, u32[]{:S(2)}) copy-start(f32[128]{0:T(128)S(1)} %get-tuple-element.159) | copy-start | bytes 1540
  98.3 305.3 %copy-start.133 = (f32[128]{0:T(128)}, f32[128]{0:T(128)S(1)}, u32[]{:S(2)}) copy-start(f32[128]{0:T(128)S(1)} %get-tuple-element.169) | copy-start | bytes 1540
  98.3 305.3 %copy-start.135 = (f32[128]{0:T(128)}, f32[128]{0:T(128)S(1)}, u32[]{:S(2)}) copy-start(f32[128]{0:T(128)S(1)} %get-tuple-element.173) | copy-start | bytes 1540
  98.3 305.3 %copy-start.137 = (f32[128]{0:T(128)}, f32[128]{0:T(128)S(1)}, u32[]{:S(2)}) copy-start(f32[128]{0:T(128)S(1)} %get-tuple-element.175) | copy-start | bytes 1540
  98.3 305.3 %copy-start.139 = (f32[128]{0:T(128)}, f32[128]{0:T(128)S(1)}, u32[]{:S(2)}) copy-start(f32[128]{0:T(128)S(1)} %get-tuple-element.176) | copy-start | bytes 1540
  98.3 305.3 %copy-start.155 = (f32[128]{0:T(128)}, f32[128]{0:T(128)S(1)}, u32[]{:S(2)}) copy-start(f32[128]{0:T(128)S(1)} %get-tuple-element.170) | copy-start | bytes 1540
  98.3 305.3 %copy-start.157 = (f32[128]{0:T(128)}, f32[128]{0:T(128)S(1)}, u32[]{:S(2)}) copy-start(f32[128]{0:T(128)S(1)} %get-tuple-element.171) | copy-start | bytes 1540
  98.4 305.3 %copy-start.159 = (f32[128]{0:T(128)}, f32[128]{0:T(128)S(1)}, u32[]{:S(2)}) copy-start(f32[128]{0:T(128)S(1)} %get-tuple-element.172) | copy-start | bytes 1540
  98.4 308.3 %copy-start.127 = (f32[128]{0:T(128)}, f32[128]{0:T(128)S(1)}, u32[]{:S(2)}) copy-start(f32[128]{0:T(128)S(1)} %get-tuple-element.167) | copy-start | bytes 1540
  98.4 308.3 %copy-start.129 = (f32[128]{0:T(128)}, f32[128]{0:T(128)S(1)}, u32[]{:S(2)}) copy-start(f32[128]{0:T(128)S(1)} %get-tuple-element.168) | copy-start | bytes 1540
  98.4 308.3 %copy-start.141 = (f32[128]{0:T(128)}, f32[128]{0:T(128)S(1)}, u32[]{:S(2)}) copy-start(f32[128]{0:T(128)S(1)} %get-tuple-element.160) | copy-start | bytes 1540
  98.4 308.3 %copy-start.143 = (f32[128]{0:T(128)}, f32[128]{0:T(128)S(1)}, u32[]{:S(2)}) copy-start(f32[128]{0:T(128)S(1)} %get-tuple-element.161) | copy-start | bytes 1540
  98.4 308.3 %copy-start.145 = (f32[128]{0:T(128)}, f32[128]{0:T(128)S(1)}, u32[]{:S(2)}) copy-start(f32[128]{0:T(128)S(1)} %get-tuple-element.162) | copy-start | bytes 1540
  98.4 308.3 %copy-start.147 = (f32[128]{0:T(128)}, f32[128]{0:T(128)S(1)}, u32[]{:S(2)}) copy-start(f32[128]{0:T(128)S(1)} %get-tuple-element.163) | copy-start | bytes 1540
  98.4 308.3 %copy-start.149 = (f32[128]{0:T(128)}, f32[128]{0:T(128)S(1)}, u32[]{:S(2)}) copy-start(f32[128]{0:T(128)S(1)} %get-tuple-element.164) | copy-start | bytes 1540
  98.4 308.3 %copy-start.151 = (f32[128]{0:T(128)}, f32[128]{0:T(128)S(1)}, u32[]{:S(2)}) copy-start(f32[128]{0:T(128)S(1)} %get-tuple-element.165) | copy-start | bytes 1540
  98.4 308.3 %copy-start.153 = (f32[128]{0:T(128)}, f32[128]{0:T(128)S(1)}, u32[]{:S(2)}) copy-start(f32[128]{0:T(128)S(1)} %get-tuple-element.166) | copy-start | bytes 1540
  98.5 50.1 %copy-start.82 = (f32[5440]{0:T(1024)}, f32[5440]{0:T(1024)S(1)}, u32[]{:S(2)}) copy-start(f32[5440]{0:T(1024)S(1)} %broadcast_multiply_fusion.19) | copy-start | bytes 65284
  98.5 46.1 %copy-start.13 = (f32[5440,256]{1,0:T(8,128)S(1)}, f32[5440,256]{1,0:T(8,128)}, u32[]{:S(2)}) copy-start(f32[5440,256]{1,0:T(8,128)} %param.16) | copy-start | bytes 16711684
  103.4 45.1 %copy-start.101 = (f32[5440]{0:T(1024)}, f32[5440]{0:T(1024)S(1)}, u32[]{:S(2)}) copy-start(f32[5440]{0:T(1024)S(1)} %fusion.181) | copy-start | bytes 65284
  176.3 130.8 %copy-start.14 = (f32[16,2,14,7,128]{4,1,0,3,2:T(2,128)}, f32[16,2,14,7,128]{4,1,0,3,2:T(2,128)S(1)}, u32[]{:S(2)}) copy-start(f32[16,2,14,7,128]{4,1,0,3,2:T(2,128)S(1)} %copy.307) | copy-start | bytes 4816900
  185.5 93.9 %copy-start.16 = (f32[32,7,14,128]{3,0,2,1:T(8,128)}, f32[32,7,14,128]{3,0,2,1:T(8,128)S(1)}, u32[]{:S(2)}) copy-start(f32[32,7,14,128]{3,0,2,1:T(8,128)S(1)} %copy.293) | copy-start | bytes 4816900
  315.8 87.9 %copy-start.18 = (f32[64,6,6,128]{3,2,1,0:T(8,128)}, f32[64,6,6,128]{3,2,1,0:T(8,128)S(1)}, u32[]{:S(2)}) copy-start(f32[64,6,6,128]{3,2,1,0:T(8,128)S(1)} %get-tuple-element.103) | copy-start | bytes 3538948
  315.8 90.9 %copy-start.20 = (f32[64,6,6,128]{3,2,1,0:T(8,128)}, f32[64,6,6,128]{3,2,1,0:T(8,128)S(1)}, u32[]{:S(2)}) copy-start(f32[64,6,6,128]{3,2,1,0:T(8,128)S(1)} %get-tuple-element.104) | copy-start | bytes 3538948
  427.6 62.2 %copy-start.1 = (f32[5440,256]{1,0:T(8,128)S(1)}, f32[5440,256]{1,0:T(8,128)}, u32[]{:S(2)}) copy-start(f32[5440,256]{1,0:T(8,128)} %copy-done) | copy-start | bytes 16711684
  427.7 62.2 %copy-start.80 = (f32[5440]{0:T(1024)S(1)}, f32[5440]{0:T(1024)}, u32[]{:S(2)}) copy-start(f32[5440]{0:T(1024)} %copy-done.79) | copy-start | bytes 65284
  427.7 62.2 %copy-start.85 = (f32[5440]{0:T(1024)S(1)}, f32[5440]{0:T(1024)}, u32[]{:S(2)}) copy-start(f32[5440]{0:T(1024)} %copy-done.84) | copy-start | bytes 65284
  427.7 62.2 %copy-start.88 = (bf16[256,2048]{1,0:T(8,128)(2,1)S(1)}, bf16[256,2048]{1,0:T(8,128)(2,1)}, u32[]{:S(2)}) copy-start(bf16[256,2048]{1,0:T(8,128)(2,1)} %all-gather.2.cloned.1.call-done) | copy-start | bytes 3145732
  427.7 62.2 %copy-start.119 = (f32[256]{0:T(256)S(1)}, f32[256]{0:T(256)}, u32[]{:S(2)}) copy-start(f32[256]{0:T(256)} %get-tuple-element.152) | copy-start | bytes 3076
  627.9 13.6 %copy-start.60 = (bf16[32,98,4,32]{1,3,2,0:T(8,128)(2,1)S(1)}, bf16[32,98,4,32]{1,3,2,0:T(8,128)(2,1)}, u32[]{:S(2)}) copy-start(bf16[32,98,4,32]{1,3,2,0:T(8,128)(2,1)} %copy.288) | copy-start | bytes 2408452
  673.1 13.5 %copy-start.58 = (bf16[32,98,4,32]{1,3,2,0:T(8,128)(2,1)S(1)}, bf16[32,98,4,32]{1,3,2,0:T(8,128)(2,1)}, u32[]{:S(2)}) copy-start(bf16[32,98,4,32]{1,3,2,0:T(8,128)(2,1)} %copy.302) | copy-start | bytes 2408452
  716.1 19.5 %copy-start.29 = (bf16[5440,256]{1,0:T(8,128)(2,1)S(1)}, bf16[5440,256]{1,0:T(8,128)(2,1)}, u32[]{:S(2)}) copy-start(bf16[5440,256]{1,0:T(8,128)(2,1)} %get-tuple-element.79) | copy-start | bytes 8355844
  739.9 275.6 %reduce-scatter.3.cloned.1.call-start = ((), (), s32[]{:S(2)}) async-start(), calls=%async_computation.3 | async-start | bytes 2228224 | tf_op jit(solution)/shard_map/reduce_scatter | solution.py:385
  899.6 13.4 %copy-start.125 = (f32[256]{0:T(256)S(1)}, f32[256]{0:T(256)}, u32[]{:S(2)}) copy-start(f32[256]{0:T(256)} %copy-done.124) | copy-start | bytes 3076
  899.6 13.4 %copy-start.162 = (f32[256]{0:T(256)S(1)}, f32[256]{0:T(256)}, u32[]{:S(2)}) copy-start(f32[256]{0:T(256)} %copy-done.161) | copy-start | bytes 3076
  899.6 26.9 %slice-start = ((s8[5570560]{0:T(1024)(128)(4,1)}), s8[1376256]{0:T(1024)(128)(4,1)S(1)}, s32[]{:S(2)}) async-start(s8[5570560]{0:T(1024)(128)(4,1)} %bitcast.264), calls=%async_computation.6 | async-start | bytes 2752512
  913.0 13.6 %slice-start.1 = ((s8[5570560]{0:T(1024)(128)(4,1)}), s8[4194304]{0:T(1024)(128)(4,1)S(1)}, s32[]{:S(2)}) async-start(s8[5570560]{0:T(1024)(128)(4,1)} %bitcast.264), calls=%async_computation.7 | async-start | bytes 8388608
  937.5 15.8 %copy-start.168 = (f32[128]{0:T(128)S(1)}, f32[128]{0:T(128)}, u32[]{:S(2)}) copy-start(f32[128]{0:T(128)} %get-tuple-element.58) | copy-start | bytes 1540
  937.6 17.1 %copy-start.166 = (f32[256]{0:T(256)S(1)}, f32[256]{0:T(256)}, u32[]{:S(2)}) copy-start(f32[256]{0:T(256)} %get-tuple-element.83) | copy-start | bytes 3076
  937.6 18.4 %copy-start.198 = (f32[256]{0:T(256)S(1)}, f32[256]{0:T(256)}, u32[]{:S(2)}) copy-start(f32[256]{0:T(256)} %get-tuple-element.15) | copy-start | bytes 3076
  937.6 19.6 %copy-start.197 = (f32[256]{0:T(256)S(1)}, f32[256]{0:T(256)}, u32[]{:S(2)}) copy-start(f32[256]{0:T(256)} %get-tuple-element.21) | copy-start | bytes 3076
  937.6 20.9 %copy-start.112 = (f32[5440]{0:T(1024)S(1)}, f32[5440]{0:T(1024)}, u32[]{:S(2)}) copy-start(f32[5440]{0:T(1024)} %copy-done.111) | copy-start | bytes 65284
  937.6 95.7 %all-reduce.83.cloned.1.call-start = ((), (), s32[]{:S(2)}) async-start(), calls=%async_computation.5 | async-start | bytes 393216 | tf_op jit(solution)/shard_map/psum | solution.py:389
  966.0 49.5 %copy-start.167 = (f32[1024]{0:T(1024)S(1)}, f32[1024]{0:T(1024)}, u32[]{:S(2)}) copy-start(f32[1024]{0:T(1024)} %get-tuple-element.80) | copy-start | bytes 12292
  966.0 50.8 %copy-start.165 = (f32[256]{0:T(256)S(1)}, f32[256]{0:T(256)}, u32[]{:S(2)}) copy-start(f32[256]{0:T(256)} %get-tuple-element.78) | copy-start | bytes 3076
  966.0 67.2 %copy-start.76 = (f32[16,2048]{1,0:T(8,128)S(1)}, f32[16,2048]{1,0:T(8,128)}, u32[]{:S(2)}) copy-start(f32[16,2048]{1,0:T(8,128)} %param.18) | copy-start | bytes 393220
  966.1 67.2 %copy-start.115 = (f32[16,2048]{1,0:T(8,128)S(1)}, f32[16,2048]{1,0:T(8,128)}, u32[]{:S(2)}) copy-start(f32[16,2048]{1,0:T(8,128)} %param.19) | copy-start | bytes 393220
  966.1 71.9 %copy-start.93 = (f32[64,256]{1,0:T(8,128)S(1)}, f32[64,256]{1,0:T(8,128)}, u32[]{:S(2)}) copy-start(f32[64,256]{1,0:T(8,128)} %param.22) | copy-start | bytes 196612
  966.1 78.8 %copy-start.196 = (f32[256]{0:T(256)S(1)}, f32[256]{0:T(256)}, u32[]{:S(2)}) copy-start(f32[256]{0:T(256)} %get-tuple-element.151) | copy-start | bytes 3076
  1034.4 106.8 %copy-start.94 = (f32[16,2048]{1,0:T(8,128)}, f32[16,2048]{1,0:T(8,128)S(1)}, u32[]{:S(2)}) copy-start(f32[16,2048]{1,0:T(8,128)S(1)} %get-tuple-element.88) | copy-start | bytes 393220
  1034.4 106.8 %copy-start.95 = (f32[16,2048]{1,0:T(8,128)}, f32[16,2048]{1,0:T(8,128)S(1)}, u32[]{:S(2)}) copy-start(f32[16,2048]{1,0:T(8,128)S(1)} %get-tuple-element.89) | copy-start | bytes 393220
  1039.6 100.9 %copy-start.107 = (f32[64,256]{1,0:T(8,128)}, f32[64,256]{1,0:T(8,128)S(1)}, u32[]{:S(2)}) copy-start(f32[64,256]{1,0:T(8,128)S(1)} %get-tuple-element.90) | copy-start | bytes 196612
  1039.6 100.9 %copy-start.108 = (f32[64,256]{1,0:T(8,128)}, f32[64,256]{1,0:T(8,128)S(1)}, u32[]{:S(2)}) copy-start(f32[64,256]{1,0:T(8,128)S(1)} %get-tuple-element.91) | copy-start | bytes 196612
  1044.9 94.9 %copy-start.164 = (f32[368]{0:T(512)S(1)}, f32[368]{0:T(512)}, u32[]{:S(2)}) copy-start(f32[368]{0:T(512)} %param.26) | copy-start | bytes 4420
  1044.9 94.9 %copy-start.193 = (f32[368]{0:T(512)S(1)}, f32[368]{0:T(512)}, u32[]{:S(2)}) copy-start(f32[368]{0:T(512)} %param.29) | copy-start | bytes 4420
  1044.9 94.9 %copy-start.194 = (f32[368]{0:T(512)S(1)}, f32[368]{0:T(512)}, u32[]{:S(2)}) copy-start(f32[368]{0:T(512)} %param.27) | copy-start | bytes 4420
  1044.9 94.9 %copy-start.195 = (f32[368]{0:T(512)S(1)}, f32[368]{0:T(512)}, u32[]{:S(2)}) copy-start(f32[368]{0:T(512)} %param.28) | copy-start | bytes 4420
  1044.9 95.6 %copy-start.117 = (f32[64,256]{1,0:T(8,128)S(1)}, f32[64,256]{1,0:T(8,128)}, u32[]{:S(2)}) copy-start(f32[64,256]{1,0:T(8,128)} %param.25) | copy-start | bytes 196612
  1045.0 96.3 %copy-start.116 = (f32[16,2048]{1,0:T(8,128)S(1)}, f32[16,2048]{1,0:T(8,128)}, u32[]{:S(2)}) copy-start(f32[16,2048]{1,0:T(8,128)} %param.21) | copy-start | bytes 393220
  (149 other events, 968.7 us)
Sparse Core Ops, SparseCore 0:
  11.3 58.1 all-gather.1
  740.0 75.3 reduce-scatter.4
  937.4 78.0 reduce-scatter.2
  1017.8 15.3 all-reduce.82
where the time goes:
time: 1160 us; the launch traced here: 1150 us
  local copies, waits for them, and re-layouts  395 us (34%)
  matrix products  311 us (27%)
  blocking collectives  199 us (17%)
  other arithmetic  163 us (14%)
  waiting for transfers between devices  60.8 us (5%)
  between operations  19 us (2%)
    unnamed x1, blocking collectives  78.8 us
    psum x1, blocking collectives, on_device(): weight_total, update_total = lax.psum((weight_sq, update_sq), 'fsdp')  77 us
    dot_general x1, matrix products, on_device(): jnp.dot(grad_low, back_down.T, preferred_element_type=jnp.float32)  62.2 us
    dot_general x4, matrix products, stripe_backward(): jnp.einsum('nhlm,nmhd->nlhd', grad_raw, key_heads, preferred_element_type...  51.4 us
    dot_general x4, matrix products, stripe_backward(): jnp.einsum('nhlm,nlhd->nmhd', grad_raw, query_heads, preferred_element_ty...  50.1 us
    reduce_scatter x1, waiting for transfers between devices, on_device(): lax.psum_scatter(wide_terms, 'fsdp', scatter_dimension=0, tiled=True)  45.5 us
    unnamed x440, local copies, waits for them, and re-layouts  42 us
    all_gather x1, blocking collectives, on_device(): lax.all_gather(shipped[1], 'fsdp', axis=0, tiled=True)  41.1 us
  transfers between devices with their start and end apart: 4, of which 2 were waited for; matrix products, arithmetic and copies ran while one was open for 21% of the time, Pallas kernels for 0%

commit v1 on v0

v1 whole, which is shorter than its diff:
```python
import functools

import jax
import jax.numpy as jnp
import numpy as np
from jax import lax
from jax.experimental import pallas as pl
from jax.experimental.pallas import tpu as pltpu
from jax.sharding import PartitionSpec as P

D = 256
FF = 1024
HEAD = 32
STRIPE = 7
GRID_L = 14
GRID_S = 6
SMALL = 8
STEP = 10
TOK_IMG = 680

EPSILON = 1e-05
BETA_ONE = 0.9
BETA_TWO = 0.999
ADAM_EPS = 1e-06
DECAY = 0.05
RATE = 0.25
EMA_CEILING = 0.9999

ROWS = 688
BIG = 2 * GRID_L * GRID_L
PAIRS = 7
WIN = 128
QROWS = 112
HALF = 128
HEADS = 4
SCALE = HEAD**-0.5
LOG2E = 1.4426950408889634
LN2 = 0.6931471805599453
CHUNKS = ((0, 176), (176, 352), (352, 528), (528, 688))
BLOCKS = ((0, 208), (192, 400), (384, 512), (496, 608), (608, 688))
FIRST = (0, 196, 392, 500, 608)
GROUP = (3, 3, 2)
VMEM = 62 * 1024 * 1024

BF = jnp.bfloat16
F32 = jnp.float32


def window_tokens(block, branch):
    if block < 2:
        index = np.full((2, WIN), -1)
        for window in range(2):
            for r in range(GRID_L):
                for c in range(GRID_L):
                    if branch == 0:
                        w, at = divmod(r * GRID_L + c, STRIPE * GRID_L)
                    else:
                        w, at = c // STRIPE, r * STRIPE + c % STRIPE
                    index[w, at] = FIRST[block] + r * GRID_L + c
        return index.reshape(-1)
    count = GROUP[block - 2] * GRID_S * GRID_S
    index = np.full((WIN,), -1)
    index[:count] = FIRST[block] + np.arange(count)
    return index


def select_matrix(block, branch):
    low, high = BLOCKS[block]
    index = window_tokens(block, branch)
    return (index[:, None] == np.arange(low, high)[None, :]).astype(np.float32)


def tap_matrix(kind):
    shape = ((STRIPE, GRID_L), (GRID_L, STRIPE), (GRID_S, GRID_S))[kind]
    copies = (1, 1, 3)[kind]
    size = shape[0] * shape[1]
    out = np.zeros((9, QROWS, WIN), np.float32)
    for copy in range(copies):
        for r in range(shape[0]):
            for c in range(shape[1]):
                for tap in range(9):
                    rr, cc = r + tap // 3 - 1, c + tap % 3 - 1
                    if 0 <= rr < shape[0] and 0 <= cc < shape[1]:
                        out[tap, copy * size + r * shape[1] + c, copy * size + rr * shape[1] + cc] = 1
    return out


def mask_operands():
    size = GRID_S * GRID_S
    rows = np.zeros((3, QROWS, HALF), np.float32)
    keys = np.zeros((3, WIN, HALF), np.float32)
    rows[0, :, 0] = 1
    keys[0, STRIPE * GRID_L :, 0] = -1e30
    for kind, crops in ((1, 3), (2, 2)):
        for at in range(QROWS):
            rows[kind, at, at // size if at < crops * size else 0] = 1
        for at in range(WIN):
            for crop in range(crops):
                if at >= crops * size or at // size != crop:
                    keys[kind, at, crop] = -1e30
    return rows, np.tile(keys, (1, HEADS, 1))


def bf(array):
    return jnp.asarray(array, BF)


def dot(left, right):
    return jnp.dot(left, right, preferred_element_type=F32)


def dot_nt(left, right):
    return lax.dot_general(left, right, (((1,), (1,)), ((), ())), preferred_element_type=F32)


def dot_tn(left, right):
    return lax.dot_general(left, right, (((0,), (0,)), ((), ())), preferred_element_type=F32)


def normalise(values):
    center = values - jnp.mean(values, axis=-1, keepdims=True)
    spread = jnp.mean(center * center, axis=-1, keepdims=True)
    scale = lax.rsqrt(spread + EPSILON)
    return center * scale, scale


def norm_back(grad_hat, hat, scale):
    mean_grad = jnp.mean(grad_hat, axis=-1, keepdims=True)
    mean_dot = jnp.mean(grad_hat * hat, axis=-1, keepdims=True)
    return scale * (grad_hat - mean_grad - hat * mean_dot)


def rows_of(ref, low, high):
    if high <= TOK_IMG:
        return ref[low:high, :]
    tail = jnp.zeros((high - TOK_IMG, ref.shape[1]), F32)
    return jnp.concatenate([ref[low:TOK_IMG, :], tail], axis=0)


def store_rows(ref, low, high, values):
    last = min(high, TOK_IMG)
    ref[low:last, :] = values[: last - low]


def fold(values):
    return jnp.sum(values.reshape(values.shape[0] // 8, 8, values.shape[1]), axis=0)


def head_lanes(head):
    lanes = lax.broadcasted_iota(jnp.int32, (1, HALF), 1)
    return jnp.where(lanes // HEAD == head, 1.0, 0.0).astype(BF)


def by_head(values):
    return jnp.concatenate([values * head_lanes(h) for h in range(HEADS)], axis=0)


def head_block(rows):
    return jnp.concatenate(
        [jnp.broadcast_to(head_lanes(h), (rows, HALF)) for h in range(HEADS)], axis=0
    )


def attend_kernel(
    x_ref,
    w_ref,
    s_ref,
    k_ref,
    p0h_ref,
    p0v_ref,
    p1h_ref,
    p1v_ref,
    pg0_ref,
    pg1_ref,
    pg2_ref,
    tap_ref,
    mrow_ref,
    mkey_ref,
    a_ref,
    att_ref,
    win_ref,
    e_ref,
    il_ref,
    o_ref,
    qkv_scr,
    attw_scr,
    attf_scr,
):
    gain, shift = s_ref[0:1, :], s_ref[1:2, :]
    for low, high in CHUNKS:
        hat, _ = normalise(rows_of(x_ref, low, high))
        a = (hat * gain + shift).astype(BF)
        a_ref[0, low:high, :] = a
        qkv = dot(a, w_ref[...])
        for part in range(3):
            piece = qkv[:, part * D : (part + 1) * D] + s_ref[2 + part : 3 + part, :]
            if part == 0:
                piece = piece * (SCALE * LOG2E)
            piece = piece.astype(BF)
            for branch in range(2):
                qkv_scr[branch, low:high, part * HALF : (part + 1) * HALF] = piece[
                    :, branch * HALF : (branch + 1) * HALF
                ]
    attf_scr[...] = jnp.zeros_like(attf_scr)
    attw_scr[...] = jnp.zeros_like(attw_scr)
    crops = ((p0h_ref, p0v_ref), (p1h_ref, p1v_ref))
    groups = (pg0_ref, pg1_ref, pg2_ref)
    for branch in range(2):
        for crop in range(2):
            low, high = BLOCKS[crop]
            got = dot(crops[crop][branch][...], qkv_scr[branch, low:high, :]).astype(BF)
            at = 4 * branch + 2 * crop
            win_ref[0, at] = got[:WIN]
            win_ref[0, at + 1] = got[WIN:]
        for group in range(3):
            low, high = BLOCKS[2 + group]
            got = dot(groups[group][...], qkv_scr[branch, low:high, :]).astype(BF)
            win_ref[0, 8 + 2 * group + branch] = got

    ones = head_block(WIN)

    def one_pair(pair, carry):
        kind = jnp.minimum(pair // 2, 2)
        mask_kind = jnp.maximum(pair - 4, 0)
        mask_kind = jnp.where(pair < 4, 0, jnp.where(pair < 6, 1, 2))
        taps = []
        mixed = []
        for member in range(2):
            at = 2 * pair + member
            branch = jnp.where(pair < 2, 0, jnp.where(pair < 4, 1, member))
            q = win_ref[0, at, :QROWS, 0:HALF]
            k = win_ref[0, at, :, HALF : 2 * HALF]
            v = win_ref[0, at, :, 2 * HALF :]
            left = jnp.concatenate([q, mrow_ref[mask_kind]], axis=1)
            right = jnp.concatenate([by_head(k), mkey_ref[mask_kind]], axis=1)
            scores = dot_nt(left, right)
            exps = []
            for h in range(HEADS):
                part = scores[:, h * WIN : (h + 1) * WIN]
                peak = jnp.max(part, axis=-1, keepdims=True)
                exps.append(jnp.exp2(part - peak).astype(BF))
            e = jnp.concatenate(exps, axis=1)
            e_ref[0, at] = e
            both = dot(e, jnp.concatenate([by_head(v), ones], axis=1))
            inv = 1.0 / both[:, HALF:]
            o = both[:, :HALF] * inv
            il_ref[0, at] = inv
            o_ref[0, at] = o.astype(BF)
            kernel = k_ref[branch]
            mixed.append(o + kernel[9:10])
            taps.append(
                jnp.concatenate(
                    [
                        v * kernel[tap : tap + 1].astype(BF) for tap in range(9)
                    ],
                    axis=0,
                )
            )
        conv = dot(tap_ref[kind], jnp.concatenate(taps, axis=1))
        for member in range(2):
            piece = mixed[member] + conv[:, member * HALF : (member + 1) * HALF]
            attw_scr[2 * pair + member, :QROWS, :] = piece.astype(BF)
        return carry

    lax.fori_loop(0, PAIRS, one_pair, 0)

    for branch in range(2):
        lanes = slice(branch * HALF, (branch + 1) * HALF)
        for crop in range(2):
            low, high = BLOCKS[crop]
            at = 4 * branch + 2 * crop
            rows = attw_scr[at : at + 2].reshape(2 * WIN, HALF)
            attf_scr[low:high, lanes] += dot_tn(crops[crop][branch][...], rows)
        for group in range(3):
            low, high = BLOCKS[2 + group]
            attf_scr[low:high, lanes] += dot_tn(
                groups[group][...], attw_scr[8 + 2 * group + branch]
            )
    att_ref[0] = attf_scr[...].astype(BF)


def gelu_parts(u):
    size = jnp.abs(u)
    t = 1.0 / (1.0 + (0.3275911 * 2**-0.5) * size)
    decay = jnp.exp2((-0.5 * LOG2E) * (u * u))
    poly = 0.5 * 1.061405429
    for term in (-1.453152027, 1.421413741, -0.284496736, 0.254829592):
        poly = poly * t + 0.5 * term
    tail = poly * t * decay
    phi = jnp.where(u >= 0, 1.0 - tail, tail)
    slope = phi + (u * 0.3989422804014327) * decay
    return phi, slope


def feed_kernel(
    cnt_ref,
    x_ref,
    c_ref,
    att_ref,
    w_ref,
    down_ref,
    s_ref,
    out_ref,
    dx_ref,
    datt_ref,
    gup_ref,
    gdn_ref,
    gout_ref,
    sums_ref,
    bup_ref,
    h2_scr,
    u_scr,
    dg_scr,
    g_scr,
    du_scr,
    dy_scr,
    dz_scr,
    x1_scr,
):
    image = pl.program_id(0)

    @pl.when(image == 0)
    def _():
        for ref in (gup_ref, gdn_ref, gout_ref, sums_ref, bup_ref):
            ref[...] = jnp.zeros_like(ref)

    bound = BIG + GRID_S * GRID_S * cnt_ref[image]
    bias_out, gain, shift = s_ref[15:16, :], s_ref[16:17, :], s_ref[17:18, :]
    w_out, w_up = w_ref[:, 3 * D : 4 * D], w_ref[:, 4 * D :]
    for low, high in CHUNKS:
        att = att_ref[0, low:high, :]
        x1 = rows_of(x_ref, low, high) + dot(att, w_out) + bias_out
        x1_scr[low:high, :] = x1
        hat, scale = normalise(x1)
        h2 = (hat * gain + shift).astype(BF)
        h2_scr[low:high, :] = h2
        u_scr[low:high, :] = dot(h2, w_up)
        row = low + lax.broadcasted_iota(jnp.int32, (high - low, 1), 0)
        dy = jnp.where(row < bound, rows_of(c_ref, low, high), 0.0)
        dyr = dy.astype(BF)
        dy_scr[low:high, :] = dyr
        sums_ref[0] += fold(dyr.astype(F32))
        dg_scr[low:high, :] = dot_nt(dyr, down_ref[...])
        for part in range(4):
            lanes = slice(part * D, (part + 1) * D)
            bias = s_ref[18 + part : 19 + part, :]
            total = jnp.zeros((8, D), F32)
            for at in range(low, high, 16):
                u = u_scr[at : at + 16, lanes] + bias
                phi, slope = gelu_parts(u)
                g_scr[at : at + 16, lanes] = (u * phi).astype(BF)
                du = dg_scr[at : at + 16, lanes] * slope
                total = total + fold(du)
                du_scr[at : at + 16, lanes] = du.astype(BF)
            bup_ref[:, lanes] += total
        block = x1_scr[low:high, :] + dot(g_scr[low:high, :], down_ref[...]) + s_ref[22:23, :]
        store_rows(out_ref, low, high, block)
        dh2 = dot_nt(du_scr[low:high, :], w_up)
        hat, scale = normalise(x1_scr[low:high, :])
        sums_ref[1] += fold(dh2 * hat)
        sums_ref[2] += fold(dh2)
        row = low + lax.broadcasted_iota(jnp.int32, (high - low, 1), 0)
        dy = jnp.where(row < bound, rows_of(c_ref, low, high), 0.0)
        dx = dy + norm_back(dh2 * gain, hat, scale)
        store_rows(dx_ref, low, high, dx)
        dz = dx.astype(BF)
        dz_scr[low:high, :] = dz
        sums_ref[3] += fold(dz.astype(F32))
        datt = dot_nt(dz, w_out)
        sums_ref[4] += fold(datt)
        datt_ref[0, low:high, :] = datt.astype(BF)
    gup_ref[...] += dot_tn(h2_scr[...], du_scr[...])
    gdn_ref[...] += dot_tn(dy_scr[...], g_scr[...])
    gout_ref[...] += dot_tn(att_ref[0], dz_scr[...])


def back_kernel(
    datt_ref,
    win_ref,
    e_ref,
    il_ref,
    o_ref,
    a_ref,
    k_ref,
    p0h_ref,
    p0v_ref,
    p1h_ref,
    p1v_ref,
    pg0_ref,
    pg1_ref,
    pg2_ref,
    tap_ref,
    rows_ref,
    dqkv_ref,
    g_ref,
    kern_ref,
    sums_ref,
    dw_scr,
    dqkvw_scr,
    dqkvf_scr,
):
    image = pl.program_id(0)

    @pl.when(image == 0)
    def _():
        for ref in (g_ref, kern_ref, sums_ref):
            ref[...] = jnp.zeros_like(ref)

    crops = ((p0h_ref, p0v_ref), (p1h_ref, p1v_ref))
    groups = (pg0_ref, pg1_ref, pg2_ref)
    for branch in range(2):
        lanes = slice(branch * HALF, (branch + 1) * HALF)
        for crop in range(2):
            low, high = BLOCKS[crop]
            got = dot(crops[crop][branch][...], datt_ref[0, low:high, lanes]).astype(BF)
            at = 4 * branch + 2 * crop
            dw_scr[at] = got[:WIN]
            dw_scr[at + 1] = got[WIN:]
        for group in range(3):
            low, high = BLOCKS[2 + group]
            got = dot(groups[group][...], datt_ref[0, low:high, lanes]).astype(BF)
            dw_scr[8 + 2 * group + branch] = got
    dqkvw_scr[...] = jnp.zeros_like(dqkvw_scr)
    dqkvf_scr[...] = jnp.zeros_like(dqkvf_scr)
    minus = -head_block(WIN)

    def one_pair(pair, carry):
        kind = jnp.minimum(pair // 2, 2)
        taps, values, grads, dvs = [], [], [], []
        for member in range(2):
            at = 2 * pair + member
            branch = jnp.where(pair < 2, 0, jnp.where(pair < 4, 1, member))
            q = win_ref[0, at, :QROWS, 0:HALF]
            k = win_ref[0, at, :, HALF : 2 * HALF]
            v = win_ref[0, at, :, 2 * HALF :]
            dwin = dw_scr[at]
            dwf = dwin[:QROWS].astype(F32)
            dn = dwf * il_ref[0, at]
            z = (dn * o_ref[0, at].astype(F32)).astype(BF)
            dn = dn.astype(BF)
            left = jnp.concatenate([dn, z], axis=1)
            right = jnp.concatenate([by_head(v), minus], axis=1)
            ds = (dot_nt(left, right) * e_ref[0, at].astype(F32)).astype(BF)
            dq = dot(ds, by_head(k)) * SCALE
            dqkvw_scr[at, :QROWS, 0:HALF] = dq.astype(BF)
            dks, dvt = [], []
            for h in range(HEADS):
                lanes = slice(h * WIN, (h + 1) * WIN)
                own = slice(h * HEAD, (h + 1) * HEAD)
                dks.append(dot_tn(q, ds[:, lanes])[own])
                dvt.append(dot_tn(dn, e_ref[0, at, :, lanes])[own])
            dk = jnp.concatenate(dks, axis=0).T * LN2
            dqkvw_scr[at, :, HALF : 2 * HALF] = dk.astype(BF)
            dvs.append(jnp.concatenate(dvt, axis=0).T)
            kernel = k_ref[branch]
            taps.append(
                jnp.concatenate(
                    [
                        dwin * kernel[8 - tap : 9 - tap].astype(BF) for tap in range(9)
                    ],
                    axis=0,
                )
            )
            values.append(v)
            grads.append(dwf)
        conv = dot(tap_ref[kind], jnp.concatenate(taps, axis=1))
        for member in range(2):
            piece = dvs[member][:QROWS] + conv[:, member * HALF : (member + 1) * HALF]
            dqkvw_scr[2 * pair + member, :QROWS, 2 * HALF :] = piece.astype(BF)
        both = jnp.concatenate(values, axis=1)
        grad = jnp.concatenate(grads, axis=1)
        for tap in range(9):
            moved = dot(rows_ref[kind, tap], both)
            kern_ref[kind, tap] += fold(moved * grad)
        return carry

    lax.fori_loop(0, PAIRS, one_pair, 0)

    for branch in range(2):
        for crop in range(2):
            low, high = BLOCKS[crop]
            at = 4 * branch + 2 * crop
            rows = dqkvw_scr[at : at + 2].reshape(2 * WIN, 3 * HALF)
            dqkvf_scr[branch, low:high, :] += dot_tn(crops[crop][branch][...], rows)
        for group in range(3):
            low, high = BLOCKS[2 + group]
            dqkvf_scr[branch, low:high, :] += dot_tn(
                groups[group][...], dqkvw_scr[8 + 2 * group + branch]
            )
    for part in range(3):
        for branch in range(2):
            value = dqkvf_scr[branch, :, part * HALF : (part + 1) * HALF]
            lanes = slice(part * D + branch * HALF, part * D + (branch + 1) * HALF)
            sums_ref[:, lanes] += fold(value)
            dqkv_ref[0, :, lanes] = value.astype(BF)
    g_ref[...] += dot_tn(a_ref[0], dqkv_ref[0])


def input_kernel(x_ref, dqkv_ref, dx_ref, w_ref, s_ref, out_ref, sums_ref):
    @pl.when(pl.program_id(0) == 0)
    def _():
        sums_ref[...] = jnp.zeros_like(sums_ref)

    for low, high in CHUNKS:
        dh = dot_nt(dqkv_ref[0, low:high, :], w_ref[...])
        hat, scale = normalise(rows_of(x_ref, low, high))
        sums_ref[0] += fold(dh * hat)
        sums_ref[1] += fold(dh)
        grad = rows_of(dx_ref, low, high) + norm_back(dh * s_ref[0:1, :], hat, scale)
        store_rows(out_ref, low, high, grad)


def whole(shape):
    return pl.BlockSpec(shape, lambda i, *_: (0,) * len(shape))


def image_of(shape):
    return pl.BlockSpec((1,) + shape, lambda i, *_: (i,) + (0,) * len(shape))


def tokens():
    return pl.BlockSpec((TOK_IMG, D), lambda i, *_: (i, 0))


def params():
    return pltpu.CompilerParams(
        vmem_limit_bytes=VMEM, dimension_semantics=("arbitrary",)
    )


def sds(shape, dtype):
    return jax.ShapeDtypeStruct(shape, dtype)


def small_tables(small):
    rows = small.reshape(-1, D)
    taps = rows[5:15].reshape(10, 2, HALF).transpose(1, 0, 2)
    return jnp.pad(rows, ((0, 1), (0, 0))), jnp.pad(taps, ((0, 0), (0, 6), (0, 0)))


def matrices():
    selects = [bf(select_matrix(b, br)) for b in range(2) for br in range(2)]
    selects += [bf(select_matrix(2 + g, 0)) for g in range(3)]
    taps = np.stack([tap_matrix(kind) for kind in range(3)])
    side = bf(taps.transpose(0, 2, 1, 3).reshape(3, QROWS, 9 * WIN))
    return selects, side, bf(taps)


def run_attend(tokens_in, w_qkv, table, kernels, selects, side):
    images = tokens_in.shape[0] // TOK_IMG
    mrow, mkey = mask_operands()
    consts = [table, kernels, *selects, side, bf(mrow), bf(mkey)]
    outs = [
        ((ROWS, D), BF),
        ((ROWS, D), BF),
        ((2 * PAIRS, WIN, 3 * HALF), BF),
        ((2 * PAIRS, QROWS, HEADS * WIN), BF),
        ((2 * PAIRS, QROWS, HALF), F32),
        ((2 * PAIRS, QROWS, HALF), BF),
    ]
    return pl.pallas_call(
        attend_kernel,
        grid=(images,),
        in_specs=[tokens(), whole(w_qkv.shape)] + [whole(c.shape) for c in consts],
        out_specs=[image_of(shape) for shape, _ in outs],
        out_shape=[sds((images,) + shape, dtype) for shape, dtype in outs],
        scratch_shapes=[
            pltpu.VMEM((2, ROWS, 3 * HALF), BF),
            pltpu.VMEM((2 * PAIRS, WIN, HALF), BF),
            pltpu.VMEM((ROWS, D), F32),
        ],
        compiler_params=params(),
        name="attend",
    )(tokens_in, w_qkv, *consts)


def run_feed(counts, tokens_in, cotangent, att, wide, down, table):
    images = tokens_in.shape[0] // TOK_IMG
    return pl.pallas_call(
        feed_kernel,
        grid_spec=pltpu.PrefetchScalarGridSpec(
            num_scalar_prefetch=1,
            grid=(images,),
            in_specs=[
                tokens(),
                tokens(),
                image_of((ROWS, D)),
                whole(wide.shape),
                whole(down.shape),
                whole(table.shape),
            ],
            out_specs=[
                tokens(),
                tokens(),
                image_of((ROWS, D)),
                whole((D, FF)),
                whole((D, FF)),
                whole((D, D)),
                whole((5, 8, D)),
                whole((8, FF)),
            ],
            scratch_shapes=[
                pltpu.VMEM((ROWS, D), BF),
                pltpu.VMEM((ROWS, FF), F32),
                pltpu.VMEM((ROWS, FF), F32),
                pltpu.VMEM((ROWS, FF), BF),
                pltpu.VMEM((ROWS, FF), BF),
                pltpu.VMEM((ROWS, D), BF),
                pltpu.VMEM((ROWS, D), BF),
                pltpu.VMEM((ROWS, D), F32),
            ],
        ),
        out_shape=[
            sds(tokens_in.shape, F32),
            sds(tokens_in.shape, F32),
            sds((images, ROWS, D), BF),
            sds((D, FF), F32),
            sds((D, FF), F32),
            sds((D, D), F32),
            sds((5, 8, D), F32),
            sds((8, FF), F32),
        ],
        compiler_params=params(),
        name="feed",
    )(counts, tokens_in, cotangent, att, wide, down, table)


def run_back(datt, win, e, il, o, a, kernels, selects, side, taps):
    images = datt.shape[0]
    consts = [kernels, *selects, side, taps]
    blocks = [datt, win, e, il, o, a]
    return pl.pallas_call(
        back_kernel,
        grid=(images,),
        in_specs=[image_of(b.shape[1:]) for b in blocks] + [whole(c.shape) for c in consts],
        out_specs=[
            image_of((ROWS, 3 * D)),
            whole((D, 3 * D)),
            whole((3, 9, 8, D)),
            whole((8, 3 * D)),
        ],
        out_shape=[
            sds((images, ROWS, 3 * D), BF),
            sds((D, 3 * D), F32),
            sds((3, 9, 8, D), F32),
            sds((8, 3 * D), F32),
        ],
        scratch_shapes=[
            pltpu.VMEM((2 * PAIRS, WIN, HALF), BF),
            pltpu.VMEM((2 * PAIRS, WIN, 3 * HALF), BF),
            pltpu.VMEM((2, ROWS, 3 * HALF), F32),
        ],
        compiler_params=params(),
        name="back",
    )(*blocks, *consts)


def run_input(tokens_in, dqkv, dx, w_qkv, table):
    images = dqkv.shape[0]
    return pl.pallas_call(
        input_kernel,
        grid=(images,),
        in_specs=[
            tokens(),
            image_of((ROWS, 3 * D)),
            tokens(),
            whole(w_qkv.shape),
            whole(table.shape),
        ],
        out_specs=[tokens(), whole((2, 8, D))],
        out_shape=[sds(tokens_in.shape, F32), sds((2, 8, D), F32)],
        compiler_params=params(),
        name="input_grad",
    )(tokens_in, dqkv, dx, w_qkv, table)


def moments(grad, first, second):
    first_new = BETA_ONE * first + (1.0 - BETA_ONE) * grad
    second_new = BETA_TWO * second + (1.0 - BETA_TWO) * grad * grad
    direction = (
        first_new
        / (1.0 - BETA_ONE**STEP)
        / (jnp.sqrt(second_new / (1.0 - BETA_TWO**STEP)) + ADAM_EPS)
    )
    return (first_new, second_new, direction)


def matrix_squares(wide, down):
    column_sq = jnp.sum(wide * wide, axis=0)
    return jnp.stack(
        [
            jnp.sum(column_sq[: 3 * D]),
            jnp.sum(column_sq[3 * D : 4 * D]),
            jnp.sum(column_sq[4 * D :]),
            jnp.sum(down * down),
        ]
    )


def on_device(
    tokens_in,
    cotangent,
    crop_count,
    wide_w,
    wide_m,
    wide_v,
    wide_ema,
    down_w,
    down_m,
    down_v,
    down_ema,
    small_p,
    small_m,
    small_v,
    small_ema,
):
    weight_sq = matrix_squares(wide_w, down_w)
    wide_all = lax.all_gather(wide_w.astype(BF), "fsdp", axis=0, tiled=True)
    down_all = lax.all_gather(down_w.astype(BF), "fsdp", axis=0, tiled=True)
    small_all = lax.all_gather(small_p.astype(BF), "fsdp", axis=0, tiled=True)
    table, kernels = small_tables(small_all.astype(F32))
    w_qkv = wide_all[:, : 3 * D]
    selects, side, taps = matrices()
    a, att, win, e, il, o = run_attend(tokens_in, w_qkv, table, kernels, selects, side)
    block_out, dx, datt, g_up, g_down_t, g_out, sums, b_up = run_feed(
        crop_count, tokens_in, cotangent, att, wide_all, down_all, table
    )
    dqkv, g_qkv, kern, b_qkv = run_back(datt, win, e, il, o, a, kernels, selects, side, taps)
    grad_in, sums_in = run_input(tokens_in, dqkv, dx, w_qkv, table)
    sums = jnp.sum(sums, axis=1)
    sums_in = jnp.sum(sums_in, axis=1)
    kern = jnp.sum(kern, axis=2)
    side_h = kern[0, :, :HALF] + kern[0, :, HALF:] + kern[2, :, :HALF]
    side_v = kern[1, :, :HALF] + kern[1, :, HALF:] + kern[2, :, HALF:]
    small_terms = jnp.concatenate(
        [
            sums_in[0],
            sums_in[1],
            jnp.sum(b_qkv, axis=0),
            jnp.concatenate([side_h, side_v], axis=1).reshape(-1),
            sums[4],
            sums[3],
            sums[1],
            sums[2],
            jnp.sum(b_up, axis=0),
            sums[0],
        ]
    )
    wide_terms = jnp.concatenate([g_qkv, g_out, g_up], axis=1)
    shard_wide, shard_down, shard_small = (
        lax.psum_scatter(wide_terms, "fsdp", scatter_dimension=0, tiled=True),
        lax.psum_scatter(g_down_t.T, "fsdp", scatter_dimension=0, tiled=True),
        lax.psum_scatter(small_terms, "fsdp", scatter_dimension=0, tiled=True),
    )
    shard_wide, shard_down, shard_small = lax.psum((shard_wide, shard_down, shard_small), "dp")
    wide_first, wide_second, wide_dir = moments(shard_wide, wide_m, wide_v)
    down_first, down_second, down_dir = moments(shard_down, down_m, down_v)
    small_first, small_second, small_dir = moments(shard_small, small_m, small_v)
    wide_upd = wide_dir + DECAY * wide_w
    down_upd = down_dir + DECAY * down_w
    update_sq = matrix_squares(wide_upd, down_upd)
    weight_total, update_total = lax.psum((weight_sq, update_sq), "fsdp")
    weight_norm = jnp.sqrt(weight_total)
    update_norm = jnp.sqrt(update_total)
    ratio = weight_norm / update_norm
    column_ratio = jnp.concatenate(
        [
            ratio[0] * jnp.ones((3 * D,), jnp.float32),
            ratio[1] * jnp.ones((D,), jnp.float32),
            ratio[2] * jnp.ones((FF,), jnp.float32),
        ]
    )
    wide_new = wide_w - RATE * column_ratio * wide_upd
    down_new = down_w - RATE * ratio[3] * down_upd
    small_new = small_p - RATE * small_dir
    ema_keep = min(EMA_CEILING, (1.0 + STEP) / (10.0 + STEP))
    wide_avg = ema_keep * wide_ema + (1.0 - ema_keep) * wide_new
    down_avg = ema_keep * down_ema + (1.0 - ema_keep) * down_new
    small_avg = ema_keep * small_ema + (1.0 - ema_keep) * small_new
    norms = jnp.stack([weight_norm, update_norm])
    return (
        block_out,
        grad_in,
        wide_new,
        wide_first,
        wide_second,
        wide_avg,
        down_new,
        down_first,
        down_second,
        down_avg,
        small_new,
        small_first,
        small_second,
        small_avg,
        norms,
    )


def solution(mesh):
    tok, row, vec = P(("dp", "fsdp"), None), P("fsdp", None), P("fsdp")
    in_specs = (tok, tok, P(("dp", "fsdp"))) + (row,) * 8 + (vec,) * 4
    out_specs = (tok, tok) + (row,) * 8 + (vec,) * 4 + (P(),)
    return jax.shard_map(
        on_device, mesh=mesh, in_specs=in_specs, out_specs=out_specs, check_vma=False
    )
```

time: 1160 us -> 536 us (0.46)
  local copies, waits for them, and re-layouts: 395 us -> 10 us
  matrix products: 311 us -> 0 us
  Pallas kernels: 0 us -> 206 us
  other arithmetic: 163 us -> 19.1 us
  waiting for transfers between devices: 60.8 us -> 84.2 us
    dot_general x36 -> x0, matrix products: 311 us -> none  [the longest x1 62.2 us: on_device(): jnp.dot(grad_low, back_down.T, preferred_element_type=jnp.float32)]
    pallas_call x0 -> x4, Pallas kernels: none -> 206 us  [the longest x1 70.4 us: run_back(): pl.pallas_call(back_kernel, grid=(images,), in_specs=[image_of(b.shape[1:...]
    another operation x23 -> x0, local copies, waits for them, and re-layouts: 112 us -> none  [the longest x5 28.6 us: head_views(): values_in.reshape(number, length, head_count, HEAD)]
    transpose x22 -> x0, local copies, waits for them, and re-layouts: 80.8 us -> none  [the longest x4 24.9 us: stripe_forward(): jnp.einsum('nhlm,nmhd->nlhd', weights_soft, value_heads, preferred_elemen...]
    reduce_sum x19 -> x5, other arithmetic: 80 us -> 0.84 us  [the longest x1 0.73 us: on_device(): sums_in = jnp.sum(sums_in, axis=1)]
    reshape x21 -> x2, local copies, waits for them, and re-layouts: 74.5 us -> 0.01 us  [the longest x1 0.01 us: small_tables(): rows = small.reshape(-1, D)]
    concatenate x24 -> x1, local copies, waits for them, and re-layouts: 37.7 us -> 0.01 us  [on_device(): jnp.concatenate([sums_in[0], sums_in[1], jnp.sum(b_qkv, axis=0), jnp.conc...]
    unnamed x440 -> x58, local copies, waits for them, and re-layouts: 42 us -> 4.38 us
  transfers between devices with their start and end apart: 4 -> 4, of which waited for: 2 -> 2; matrix products, arithmetic and copies ran while one was open for 21% -> 2% of each run, Pallas kernels for 0% -> 16%
where the time goes in v1:
time: 536 us; the launch traced here: 535 us
  Pallas kernels  206 us (38%)
  blocking collectives  199 us (37%)
  waiting for transfers between devices  84.2 us (16%)
  other arithmetic  19.1 us (4%)
  between operations  16.2 us (3%)
  local copies, waits for them, and re-layouts  10 us (2%)
    unnamed x1, blocking collectives  78.8 us
    psum x1, blocking collectives, on_device(): weight_total, update_total = lax.psum((weight_sq, update_sq), 'fsdp')  77 us
    pallas_call x1, Pallas kernels, run_back(): pl.pallas_call(back_kernel, grid=(images,), in_specs=[image_of(b.shape[1:...  70.4 us
    reduce_scatter x1, waiting for transfers between devices, on_device(): lax.psum_scatter(wide_terms, 'fsdp', scatter_dimension=0, tiled=True)  66.7 us
    pallas_call x1, Pallas kernels, run_attend(): pl.pallas_call(attend_kernel, grid=(images,), in_specs=[tokens(), whole(w...  61.5 us
    pallas_call x1, Pallas kernels, run_feed(): pl.pallas_call(feed_kernel, grid_spec=pltpu.PrefetchScalarGridSpec(num_sc...  60.4 us
    all_gather x1, blocking collectives, on_device(): down_all = lax.all_gather(down_w.astype(BF), 'fsdp', axis=0, tiled=True)  40.9 us
    psum x1, waiting for transfers between devices, on_device(): lax.psum((shard_wide, shard_down, shard_small), 'dp')  17.4 us
  transfers between devices with their start and end apart: 4, of which 2 were waited for; matrix products, arithmetic and copies ran while one was open for 2% of the time, Pallas kernels for 16%

profile of v1, /device:TPU:0, one launch (start us, length us, event | category | flops | bytes accessed | tf_op | source)
XLA Modules:
  0.0 534.9 jit_solution(16657285447757432798)
XLA Ops:
  7.2 0.0 all-gather.2.cloned.1.call-start
  7.2 1.5 convert_element_type.16
  8.8 0.0 all-gather.2.cloned.1.call-update
  8.8 0.0 reduce-scatter.7.cloned.1.call-start
  8.9 0.7 convert_element_type.17
  9.5 1.3 fusion.10
  11.5 0.3 dynamic-update-slice
  11.8 78.8 %all-reduce.2 = bf16[5888]{0:T(1024)(128)(2,1)S(1)} all-reduce(bf16[5888]{0:T(1024)(128)(2,1)S(1)} %dynamic-update-slice), channel_id=1, replica_groups=mesh['dp'=2,'fsdp'=16] {'fsdp'}, use_global_device_ids=true, to_apply=%add.2 | all-reduce | flops 5888 | bytes 23552
  90.6 0.6 pad.8.s_ref
  91.2 0.6 pad.9.k_ref
  91.9 0.8 convert_element_type.19
  92.7 40.9 %all_gather.11.down_ref = bf16[1024,256]{1,0:T(8,128)(2,1)} all-gather(bf16[64,256]{1,0:T(8,128)(2,1)S(1)} %convert_element_type.19), channel_id=1, replica_groups=mesh['dp'=2,'fsdp'=16] {'fsdp'}, dimensions={0}, use_global_device_ids=true | all-gather | bytes 557056 | tf_op jit(solution)/shard_map/all_gather | solution.py:719
  133.6 1.8 slice.112.w_ref
  135.4 61.5 %attend.1 = (bf16[8,688,256]{2,1,0:T(8,128)(2,1)}, bf16[8,688,256]{2,1,0:T(8,128)(2,1)}, bf16[8,14,128,384]{3,2,1,0:T(8,128)(2,1)}, bf16[8,14,112,512]{3,2,1,0:T...) custom-call(f32[5440,256]{1,0:T(8,128)} %x_ref.5, bf16[256,768]{1,0:T(8,128)(2,1)} %slice.112.w_ref, ...), custom_call_target="tpu_custom_call" | custom-call | tf_op jit(solution)/shard_map/attend/pallas_call | solution.py:561
  196.9 60.4 %feed.1 = (f32[5440,256]{1,0:T(8,128)}, f32[5440,256]{1,0:T(8,128)}, bf16[8,688,256]{2,1,0:T(8,128)(2,1)}, f32[256,1024]{1,0:T(8,128)}, f32[256,1024]{1,0:T(8,12...) custom-call(s32[8]{0:T(128)} %cnt_ref.1, f32[5440,256]{1,0:T(8,128)} %x_ref.5, ...), custom_call_target="tpu_custom_call" | custom-call | tf_op jit(solution)/shard_map/feed/pallas_call | solution.py:579
  257.2 2.5 copy.72
  259.8 0.0 reduce-scatter.7.cloned.1.call-update
  259.8 0.2 reduce-scatter.5.cloned.1.call-start
  260.1 70.4 %back.1 = (bf16[8,688,768]{2,1,0:T(8,128)(2,1)}, f32[256,768]{1,0:T(8,128)}, f32[3,9,8,256]{3,2,1,0:T(8,128)}, f32[8,768]{1,0:T(8,128)}) custom-call(bf16[8,688,256]{2,1,0:T(8,128)(2,1)} %get-tuple-element.37.datt_ref, bf16[8,14,128,384]{3,2,1,0:T(8,128)(2,1)} %get-tuple-element.38.win_ref, bf16[8,14,112,512]{3,2,1,0:T(8,128)(2,1)} %get-tuple-element.39.e_ref, ...), custom_call_target="tpu_custom_call" | custom-call | tf_op jit(solution)/shard_map/back/pallas_call | solution.py:632
  330.5 2.8 pad_maximum_fusion
  333.2 0.0 reduce-scatter.5.cloned.1.call-update
  333.2 0.0 all-reduce.8.cloned.1.call-start
  333.3 0.1 reduce_sum.147
  333.4 0.0 copy-start.17
  333.4 0.0 copy-start.15
  333.4 0.0 copy-start.16
  333.5 0.0 copy-start
  333.5 0.0 copy-start.9
  333.5 0.0 copy-start.10
  333.5 0.0 copy-start.2
  333.5 0.0 copy-start.12
  333.5 0.0 copy-start.13
  333.5 0.0 copy-start.14
  333.5 0.0 copy-start.11
  333.6 0.0 copy-start.18
  333.6 0.0 copy-start.19
  333.6 0.0 copy-start.20
  333.6 0.0 copy-start.21
  333.6 13.8 %input_grad.1 = (f32[5440,256]{1,0:T(8,128)}, f32[2,8,256]{2,1,0:T(8,128)}) custom-call(f32[5440,256]{1,0:T(8,128)} %x_ref.5, bf16[8,688,768]{2,1,0:T(8,128)(2,1)} %get-tuple-element.43.dqkv_ref, f32[5440,256]{1,0:T(8,128)} %get-tuple-element.44.dx_ref, bf16[256,768]{1,0:T(8,128)(2,1)} %slice.112.w_ref, f32[24,256]{1,0:T(8,128)} %pad.8.s_ref), custom_call_target="tpu_custom_call" | custom-call | tf_op jit(solution)/shard_map/input_grad/pallas_call | solution.py:660
  347.4 0.7 reduce_sum.145
  348.3 0.0 reduce-scatter.7.cloned.1.call-done
  348.3 66.7 %reduce-scatter.5.cloned.1.call-done = f32[16,2048]{1,0:T(8,128)} async-done(((f32[256,2048]{1,0:T(8,128)}), f32[16,2048]{1,0:T(8,128)}) %reduce-scatter.5.cloned.1.call-update) | async-done | bytes 131088 | tf_op jit(solution)/shard_map/reduce_scatter | solution.py:751
  415.1 0.0 all-reduce.8.cloned.1.call-update
  415.1 17.4 %all-reduce.8.cloned.1.call-done = (f32[64,256]{1,0:T(8,128)}, f32[16,2048]{1,0:T(8,128)}) async-done(((f32[64,256]{1,0:T(8,128)}, f32[16,2048]{1,0:T(8,128)}), (f32[64,256]{1,0:T(8,128)}, f32[16,2048]{1,0:T(8,128)})) %all-reduce.8.cloned.1.call-update) | async-done | bytes 196624 | tf_op jit(solution)/shard_map/psum | solution.py:755
  432.5 1.0 multiply_reduce_fusion.1
  433.5 0.0 copy-start.3
  433.6 0.0 copy-start.4
  433.6 0.6 slice_reduce_fusion.1
  434.2 0.6 slice_reduce_fusion.4
  434.8 0.6 slice_reduce_fusion
  435.4 1.5 multiply_reduce_fusion.3
  436.9 2.7 pad_maximum_fusion.3
  439.6 2.7 pad_maximum_fusion.4
  442.9 77.0 %all-reduce.4 = (f32[4]{0:T(128)S(1)}, f32[4]{0:T(128)S(1)}, f32[5888]{0:T(1024)S(1)}) all-reduce(f32[4]{0:T(128)S(1)} %pad_maximum_fusion.4, f32[4]{0:T(128)S(1)} %pad_maximum_fusion.3, f32[5888]{0:T(1024)S(1)} %constant_dynamic-update-slice_fusion), channel_id=1, replica_groups=mesh['dp'=2,'fsdp'=16] {'fsdp'}, use_global_device_ids=true, to_apply=%region_15.16 | all-reduce | flops 5896 | bytes 47168 | tf_op jit(solution)/shard_map/psum | solution.py:762
  519.9 0.6 fusion.11
  520.5 0.1 dynamic-slice.2
  520.6 2.4 psum.39
  523.0 0.6 pad_maximum_fusion.2
  524.3 0.6 mul.212
  524.9 0.6 mul.214
  525.6 0.6 mul.213
  526.2 0.7 multiply_add_fusion.3
  527.0 0.8 multiply_add_fusion
  527.8 0.6 multiply_add_fusion.6
  (54 shorter events, 0.2 us)
Async XLA Ops:
  7.2 126.4 %all-gather.2.cloned.1.call-start = ((), (), s32[]{:S(2)}) async-start(), calls=%async_computation.2 | async-start | bytes 1114112 | tf_op jit(solution)/shard_map/all_gather | solution.py:718
  8.8 339.5 %reduce-scatter.7.cloned.1.call-start = ((), (), s32[]{:S(2)}) async-start(), calls=%async_computation.4 | async-start | bytes 1114112 | tf_op jit(solution)/shard_map/reduce_scatter | solution.py:752
  259.8 155.2 %reduce-scatter.5.cloned.1.call-start = ((), (), s32[]{:S(2)}) async-start(), calls=%async_computation.3 | async-start | bytes 2228224 | tf_op jit(solution)/shard_map/reduce_scatter | solution.py:751
  260.0 70.4 %copy-start.1 = (f32[256,1024]{1,0:T(8,128)S(1)}, f32[256,1024]{1,0:T(8,128)}, u32[]{:S(2)}) copy-start(f32[256,1024]{1,0:T(8,128)} %get-tuple-element.48) | copy-start | bytes 3145732
  260.1 70.4 %copy-start.5 = (f32[256,256]{1,0:T(8,128)S(1)}, f32[256,256]{1,0:T(8,128)}, u32[]{:S(2)}) copy-start(f32[256,256]{1,0:T(8,128)} %get-tuple-element.47) | copy-start | bytes 786436
  330.4 2.9 copy-start.8
  333.2 99.2 %all-reduce.8.cloned.1.call-start = ((), (), s32[]{:S(2)}) async-start(), calls=%async_computation.5 | async-start | bytes 393216 | tf_op jit(solution)/shard_map/psum | solution.py:755
  333.4 14.7 %copy-start.17 = (f32[8,768]{1,0:T(8,128)S(1)}, f32[8,768]{1,0:T(8,128)}, u32[]{:S(2)}) copy-start(f32[8,768]{1,0:T(8,128)} %get-tuple-element.51) | copy-start | bytes 73732
  333.4 14.7 %copy-start.15 = (f32[5,8,256]{2,1,0:T(8,128)S(1)}, f32[5,8,256]{2,1,0:T(8,128)}, u32[]{:S(2)}) copy-start(f32[5,8,256]{2,1,0:T(8,128)} %get-tuple-element.53) | copy-start | bytes 122884
  333.4 14.7 %copy-start.16 = (f32[8,1024]{1,0:T(8,128)S(1)}, f32[8,1024]{1,0:T(8,128)}, u32[]{:S(2)}) copy-start(f32[8,1024]{1,0:T(8,128)} %get-tuple-element.54) | copy-start | bytes 98308
  333.5 99.0 %copy-start = (f32[16,2048]{1,0:T(8,128)S(1)}, f32[16,2048]{1,0:T(8,128)}, u32[]{:S(2)}) copy-start(f32[16,2048]{1,0:T(8,128)} %param.29) | copy-start | bytes 393220
  333.5 99.0 %copy-start.9 = (f32[16,2048]{1,0:T(8,128)S(1)}, f32[16,2048]{1,0:T(8,128)}, u32[]{:S(2)}) copy-start(f32[16,2048]{1,0:T(8,128)} %param.30) | copy-start | bytes 393220
  333.5 99.0 %copy-start.10 = (f32[16,2048]{1,0:T(8,128)S(1)}, f32[16,2048]{1,0:T(8,128)}, u32[]{:S(2)}) copy-start(f32[16,2048]{1,0:T(8,128)} %param.31) | copy-start | bytes 393220
  333.5 101.9 %copy-start.2 = (f32[64,256]{1,0:T(8,128)S(1)}, f32[64,256]{1,0:T(8,128)}, u32[]{:S(2)}) copy-start(f32[64,256]{1,0:T(8,128)} %param.33) | copy-start | bytes 196612
  333.5 101.9 %copy-start.12 = (f32[64,256]{1,0:T(8,128)S(1)}, f32[64,256]{1,0:T(8,128)}, u32[]{:S(2)}) copy-start(f32[64,256]{1,0:T(8,128)} %param.34) | copy-start | bytes 196612
  333.5 101.9 %copy-start.13 = (f32[64,256]{1,0:T(8,128)S(1)}, f32[64,256]{1,0:T(8,128)}, u32[]{:S(2)}) copy-start(f32[64,256]{1,0:T(8,128)} %param.35) | copy-start | bytes 196612
  333.5 192.7 %copy-start.14 = (f32[64,256]{1,0:T(8,128)S(1)}, f32[64,256]{1,0:T(8,128)}, u32[]{:S(2)}) copy-start(f32[64,256]{1,0:T(8,128)} %param.36) | copy-start | bytes 196612
  333.5 193.4 %copy-start.11 = (f32[16,2048]{1,0:T(8,128)S(1)}, f32[16,2048]{1,0:T(8,128)}, u32[]{:S(2)}) copy-start(f32[16,2048]{1,0:T(8,128)} %param.32) | copy-start | bytes 393220
  333.6 194.2 %copy-start.18 = (f32[368]{0:T(512)S(1)}, f32[368]{0:T(512)}, u32[]{:S(2)}) copy-start(f32[368]{0:T(512)} %param.37) | copy-start | bytes 4420
  333.6 194.2 %copy-start.19 = (f32[368]{0:T(512)S(1)}, f32[368]{0:T(512)}, u32[]{:S(2)}) copy-start(f32[368]{0:T(512)} %param.40) | copy-start | bytes 4420
  333.6 194.2 %copy-start.20 = (f32[368]{0:T(512)S(1)}, f32[368]{0:T(512)}, u32[]{:S(2)}) copy-start(f32[368]{0:T(512)} %param.38) | copy-start | bytes 4420
  333.6 194.2 %copy-start.21 = (f32[368]{0:T(512)S(1)}, f32[368]{0:T(512)}, u32[]{:S(2)}) copy-start(f32[368]{0:T(512)} %param.39) | copy-start | bytes 4420
  433.5 94.8 %copy-start.3 = (f32[16,2048]{1,0:T(8,128)}, f32[16,2048]{1,0:T(8,128)S(1)}, u32[]{:S(2)}) copy-start(f32[16,2048]{1,0:T(8,128)S(1)} %get-tuple-element.117) | copy-start | bytes 393220
  433.6 94.8 %copy-start.4 = (f32[16,2048]{1,0:T(8,128)}, f32[16,2048]{1,0:T(8,128)S(1)}, u32[]{:S(2)}) copy-start(f32[16,2048]{1,0:T(8,128)S(1)} %get-tuple-element.118) | copy-start | bytes 393220
  436.9 91.5 %copy-start.6 = (f32[64,256]{1,0:T(8,128)}, f32[64,256]{1,0:T(8,128)S(1)}, u32[]{:S(2)}) copy-start(f32[64,256]{1,0:T(8,128)S(1)} %get-tuple-element.119) | copy-start | bytes 196612
  436.9 91.5 %copy-start.7 = (f32[64,256]{1,0:T(8,128)}, f32[64,256]{1,0:T(8,128)S(1)}, u32[]{:S(2)}) copy-start(f32[64,256]{1,0:T(8,128)S(1)} %get-tuple-element.120) | copy-start | bytes 196612
Sparse Core Ops, SparseCore 0:
  11.3 58.1 all-gather.1
  259.9 75.4 reduce-scatter.6
  337.8 77.1 reduce-scatter.4
  417.4 15.0 all-reduce.7

commit v2 on v1

--- a/solution.py
+++ b/solution.py
@@ -303,9 +303,8 @@
     out_ref,
     dx_ref,
     datt_ref,
-    gup_ref,
+    glate_ref,
     gdn_ref,
-    gout_ref,
     sums_ref,
     bup_ref,
     h2_scr,
@@ -316,17 +315,20 @@
     dy_scr,
     dz_scr,
     x1_scr,
+    gup_scr,
+    gdn_scr,
+    gout_scr,
 ):
     image = pl.program_id(0)
 
     @pl.when(image == 0)
     def _():
-        for ref in (gup_ref, gdn_ref, gout_ref, sums_ref, bup_ref):
+        for ref in (gup_scr, gdn_scr, gout_scr, sums_ref, bup_ref):
             ref[...] = jnp.zeros_like(ref)
 
     bound = BIG + GRID_S * GRID_S * cnt_ref[image]
     bias_out, gain, shift = s_ref[15:16, :], s_ref[16:17, :], s_ref[17:18, :]
-    w_out, w_up = w_ref[:, 3 * D : 4 * D], w_ref[:, 4 * D :]
+    w_out, w_up = w_ref[:, :D], w_ref[:, D : D + FF]
     for low, high in CHUNKS:
         att = att_ref[0, low:high, :]
         x1 = rows_of(x_ref, low, high) + dot(att, w_out) + bias_out
@@ -369,9 +371,15 @@
         datt = dot_nt(dz, w_out)
         sums_ref[4] += fold(datt)
         datt_ref[0, low:high, :] = datt.astype(BF)
-    gup_ref[...] += dot_tn(h2_scr[...], du_scr[...])
-    gdn_ref[...] += dot_tn(dy_scr[...], g_scr[...])
-    gout_ref[...] += dot_tn(att_ref[0], dz_scr[...])
+    gup_scr[...] += dot_tn(h2_scr[...], du_scr[...])
+    gdn_scr[...] += dot_tn(dy_scr[...], g_scr[...])
+    gout_scr[...] += dot_tn(att_ref[0], dz_scr[...])
+
+    @pl.when(image == pl.num_programs(0) - 1)
+    def _():
+        gdn_ref[...] = gdn_scr[...].T.astype(BF)
+        glate_ref[:, :D] = gout_scr[...].astype(BF)
+        glate_ref[:, D:] = gup_scr[...].astype(BF)
 
 
 def back_kernel(
@@ -381,6 +389,10 @@
     il_ref,
     o_ref,
     a_ref,
+    x_ref,
+    dx_ref,
+    w_ref,
+    s_ref,
     k_ref,
     p0h_ref,
     p0v_ref,
@@ -391,19 +403,21 @@
     pg2_ref,
     tap_ref,
     rows_ref,
-    dqkv_ref,
+    out_ref,
     g_ref,
     kern_ref,
+    bias_ref,
     sums_ref,
     dw_scr,
     dqkvw_scr,
     dqkvf_scr,
+    dqkv_scr,
 ):
     image = pl.program_id(0)
 
     @pl.when(image == 0)
     def _():
-        for ref in (g_ref, kern_ref, sums_ref):
+        for ref in (g_ref, kern_ref, bias_ref, sums_ref):
             ref[...] = jnp.zeros_like(ref)
 
     crops = ((p0h_ref, p0v_ref), (p1h_ref, p1v_ref))
@@ -491,18 +505,11 @@
         for branch in range(2):
             value = dqkvf_scr[branch, :, part * HALF : (part + 1) * HALF]
             lanes = slice(part * D + branch * HALF, part * D + (branch + 1) * HALF)
-            sums_ref[:, lanes] += fold(value)
-            dqkv_ref[0, :, lanes] = value.astype(BF)
-    g_ref[...] += dot_tn(a_ref[0], dqkv_ref[0])
-
-
-def input_kernel(x_ref, dqkv_ref, dx_ref, w_ref, s_ref, out_ref, sums_ref):
-    @pl.when(pl.program_id(0) == 0)
-    def _():
-        sums_ref[...] = jnp.zeros_like(sums_ref)
-
+            bias_ref[:, lanes] += fold(value)
+            dqkv_scr[:, lanes] = value.astype(BF)
+    g_ref[...] += dot_tn(a_ref[0], dqkv_scr[...])
     for low, high in CHUNKS:
-        dh = dot_nt(dqkv_ref[0, low:high, :], w_ref[...])
+        dh = dot_nt(dqkv_scr[low:high, :], w_ref[...])
         hat, scale = normalise(rows_of(x_ref, low, high))
         sums_ref[0] += fold(dh * hat)
         sums_ref[1] += fold(dh)
@@ -593,9 +600,8 @@
                 tokens(),
                 tokens(),
                 image_of((ROWS, D)),
-                whole((D, FF)),
-                whole((D, FF)),
-                whole((D, D)),
+                whole((D, D + FF)),
+                whole((FF, D)),
                 whole((5, 8, D)),
                 whole((8, FF)),
             ],
@@ -608,15 +614,17 @@
                 pltpu.VMEM((ROWS, D), BF),
                 pltpu.VMEM((ROWS, D), BF),
                 pltpu.VMEM((ROWS, D), F32),
+                pltpu.VMEM((D, FF), F32),
+                pltpu.VMEM((D, FF), F32),
+                pltpu.VMEM((D, D), F32),
             ],
         ),
         out_shape=[
             sds(tokens_in.shape, F32),
             sds(tokens_in.shape, F32),
             sds((images, ROWS, D), BF),
-            sds((D, FF), F32),
-            sds((D, FF), F32),
-            sds((D, D), F32),
+            sds((D, D + FF), BF),
+            sds((FF, D), BF),
             sds((5, 8, D), F32),
             sds((8, FF), F32),
         ],
@@ -625,53 +633,27 @@
     )(counts, tokens_in, cotangent, att, wide, down, table)
 
 
-def run_back(datt, win, e, il, o, a, kernels, selects, side, taps):
-    images = datt.shape[0]
-    consts = [kernels, *selects, side, taps]
-    blocks = [datt, win, e, il, o, a]
+def run_back(blocks, tokens_in, dx, w_qkv, table, kernels, selects, side, taps):
+    images = blocks[0].shape[0]
+    consts = [w_qkv, table, kernels, *selects, side, taps]
+    outs = [(D, 3 * D), (3, 9, 8, D), (8, 3 * D), (2, 8, D)]
     return pl.pallas_call(
         back_kernel,
         grid=(images,),
-        in_specs=[image_of(b.shape[1:]) for b in blocks] + [whole(c.shape) for c in consts],
-        out_specs=[
-            image_of((ROWS, 3 * D)),
-            whole((D, 3 * D)),
-            whole((3, 9, 8, D)),
-            whole((8, 3 * D)),
-        ],
-        out_shape=[
-            sds((images, ROWS, 3 * D), BF),
-            sds((D, 3 * D), F32),
-            sds((3, 9, 8, D), F32),
-            sds((8, 3 * D), F32),
-        ],
+        in_specs=[image_of(b.shape[1:]) for b in blocks]
+        + [tokens(), tokens()]
+        + [whole(c.shape) for c in consts],
+        out_specs=[tokens()] + [whole(shape) for shape in outs],
+        out_shape=[sds(tokens_in.shape, F32)] + [sds(shape, F32) for shape in outs],
         scratch_shapes=[
             pltpu.VMEM((2 * PAIRS, WIN, HALF), BF),
             pltpu.VMEM((2 * PAIRS, WIN, 3 * HALF), BF),
             pltpu.VMEM((2, ROWS, 3 * HALF), F32),
+            pltpu.VMEM((ROWS, 3 * D), BF),
         ],
         compiler_params=params(),
         name="back",
-    )(*blocks, *consts)
-
-
-def run_input(tokens_in, dqkv, dx, w_qkv, table):
-    images = dqkv.shape[0]
-    return pl.pallas_call(
-        input_kernel,
-        grid=(images,),
-        in_specs=[
-            tokens(),
-            image_of((ROWS, 3 * D)),
-            tokens(),
-            whole(w_qkv.shape),
-            whole(table.shape),
-        ],
-        out_specs=[tokens(), whole((2, 8, D))],
-        out_shape=[sds(tokens_in.shape, F32), sds((2, 8, D), F32)],
-        compiler_params=params(),
-        name="input_grad",
-    )(tokens_in, dqkv, dx, w_qkv, table)
+    )(*blocks, tokens_in, dx, *consts)
 
 
 def moments(grad, first, second):
@@ -685,19 +667,120 @@
     return (first_new, second_new, direction)
 
 
-def matrix_squares(wide, down):
-    column_sq = jnp.sum(wide * wide, axis=0)
-    return jnp.stack(
-        [
-            jnp.sum(column_sq[: 3 * D]),
-            jnp.sum(column_sq[3 * D : 4 * D]),
-            jnp.sum(column_sq[4 * D :]),
-            jnp.sum(down * down),
-        ]
-    )
+MATRICES = (slice(0, 3 * D), slice(3 * D, 4 * D), slice(4 * D, 4 * D + FF))
+
+
+def lane_sums(values):
+    column = jnp.sum(values * values, axis=0, keepdims=True)
+    parts = [column[:, at : at + HALF] for at in range(0, column.shape[1], HALF)]
+    return functools.reduce(jnp.add, parts)
+
+
+def moment_kernel(
+    gq_ref,
+    gq_other_ref,
+    gl_ref,
+    gl_other_ref,
+    ww_ref,
+    wm_ref,
+    wv_ref,
+    dw_ref,
+    dm_ref,
+    dv_ref,
+    wf_ref,
+    ws_ref,
+    wu_ref,
+    df_ref,
+    ds_ref,
+    du_ref,
+    sq_ref,
+):
+    for lanes, own, other in (
+        (slice(0, 3 * D), gq_ref[:, : 3 * D], gq_other_ref[:, : 3 * D]),
+        (slice(3 * D, 4 * D + FF), gl_ref[:, : D + FF], gl_other_ref[:, : D + FF]),
+    ):
+        first, second, way = moments(own + other, wm_ref[:, lanes], wv_ref[:, lanes])
+        wf_ref[:, lanes] = first
+        ws_ref[:, lanes] = second
+        wu_ref[:, lanes] = way + DECAY * ww_ref[:, lanes]
+    count = ww_ref.shape[0]
+    for part in range(FF // D):
+        lanes = slice(D + FF + part * D, D + FF + (part + 1) * D)
+        own = slice(part * count, (part + 1) * count)
+        grad = gl_ref[:, lanes] + gl_other_ref[:, lanes]
+        first, second, way = moments(grad, dm_ref[own, :], dv_ref[own, :])
+        df_ref[own, :] = first
+        ds_ref[own, :] = second
+        du_ref[own, :] = way + DECAY * dw_ref[own, :]
+    for base, wide, down in ((0, ww_ref, dw_ref), (4, wu_ref, du_ref)):
+        for at, lanes in enumerate(MATRICES):
+            sq_ref[base + at : base + at + 1, :] = lane_sums(wide[:, lanes])
+        sq_ref[base + 3 : base + 4, :] = lane_sums(down[...])
+
+
+def update_kernel(
+    sq_ref,
+    ww_ref,
+    wu_ref,
+    we_ref,
+    dw_ref,
+    du_ref,
+    de_ref,
+    wn_ref,
+    wa_ref,
+    dn_ref,
+    da_ref,
+    norm_ref,
+):
+    total = jnp.sum(sq_ref[...], axis=1, keepdims=True)
+    norm = jnp.sqrt(total)
+    norm_ref[...] = jnp.broadcast_to(norm, norm_ref.shape)
+    ratio = norm[0:4] / norm[4:8]
+    keep = min(EMA_CEILING, (1.0 + STEP) / (10.0 + STEP))
+    for at, lanes in enumerate(MATRICES):
+        new = ww_ref[:, lanes] - (RATE * ratio[at : at + 1]) * wu_ref[:, lanes]
+        wn_ref[:, lanes] = new
+        wa_ref[:, lanes] = keep * we_ref[:, lanes] + (1.0 - keep) * new
+    new = dw_ref[...] - (RATE * ratio[3:4]) * du_ref[...]
+    dn_ref[...] = new
+    da_ref[...] = keep * de_ref[...] + (1.0 - keep) * new
+
+
+def plain(kernel, name, out_shape, *operands):
+    return pl.pallas_call(kernel, out_shape=out_shape, compiler_params=pltpu.CompilerParams(
+        vmem_limit_bytes=VMEM), name=name)(*operands)
+
+
+def to_other(values):
+    return lax.ppermute(values, "dp", [(0, 1), (1, 0)])
+
+
+def side_by_side(wide, down):
+    rows = wide.shape[0]
+    blocks = [down[at : at + rows] for at in range(0, down.shape[0], rows)]
+    return jnp.concatenate([wide] + blocks, axis=1)
+
+
+def gather(values, count):
+    copies = jnp.broadcast_to(values[None], (count,) + values.shape)
+    return lax.all_to_all(copies, "fsdp", 0, 0).reshape(-1, values.shape[1])
+
+
+def scatter_sum(values, count):
+    terms = values.reshape(count, -1, values.shape[1])
+    return jnp.sum(lax.all_to_all(terms, "fsdp", 0, 0).astype(F32), axis=0)
+
+
+def add_all(values, count):
+    step = 1
+    while step < count:
+        values = values + lax.ppermute(values, "fsdp", [(i, i ^ step) for i in range(count)])
+        step *= 2
+    return values
 
 
 def on_device(
+    count,
     tokens_in,
     cotangent,
     crop_count,
@@ -714,19 +797,27 @@
     small_v,
     small_ema,
 ):
-    weight_sq = matrix_squares(wide_w, down_w)
-    wide_all = lax.all_gather(wide_w.astype(BF), "fsdp", axis=0, tiled=True)
-    down_all = lax.all_gather(down_w.astype(BF), "fsdp", axis=0, tiled=True)
-    small_all = lax.all_gather(small_p.astype(BF), "fsdp", axis=0, tiled=True)
-    table, kernels = small_tables(small_all.astype(F32))
-    w_qkv = wide_all[:, : 3 * D]
+    rows = wide_w.shape[0]
+    narrow = small_p.shape[0] // rows
+    wide_low = wide_w.astype(BF)
+    small_low = jnp.pad(small_p.astype(BF).reshape(rows, narrow), ((0, 0), (0, HALF - narrow)))
+    first = jnp.concatenate([wide_low[:, : 3 * D], small_low], axis=1)
+    first = gather(first, count)
+    late_all = gather(side_by_side(wide_low[:, 3 * D :], down_w.astype(BF)), count)
+    down_all = late_all[:, D + FF :].reshape(count, rows, FF // D, D)
+    down_all = down_all.transpose(0, 2, 1, 3).reshape(FF, D)
+    w_qkv = first[:, : 3 * D]
+    table, kernels = small_tables(first[:, 3 * D : 3 * D + narrow].astype(F32).reshape(-1))
     selects, side, taps = matrices()
     a, att, win, e, il, o = run_attend(tokens_in, w_qkv, table, kernels, selects, side)
-    block_out, dx, datt, g_up, g_down_t, g_out, sums, b_up = run_feed(
-        crop_count, tokens_in, cotangent, att, wide_all, down_all, table
+    block_out, dx, datt, g_late, g_down, sums, b_up = run_feed(
+        crop_count, tokens_in, cotangent, att, late_all, down_all, table
     )
-    dqkv, g_qkv, kern, b_qkv = run_back(datt, win, e, il, o, a, kernels, selects, side, taps)
-    grad_in, sums_in = run_input(tokens_in, dqkv, dx, w_qkv, table)
+    g_down = g_down.reshape(count, FF // D, rows, D).transpose(0, 2, 1, 3).reshape(D, FF)
+    late = scatter_sum(jnp.concatenate([g_late, g_down], axis=1), count)
+    grad_in, g_qkv, kern, b_qkv, sums_in = run_back(
+        [datt, win, e, il, o, a], tokens_in, dx, w_qkv, table, kernels, selects, side, taps
+    )
     sums = jnp.sum(sums, axis=1)
     sums_in = jnp.sum(sums_in, axis=1)
     kern = jnp.sum(kern, axis=2)
@@ -745,39 +836,32 @@
             jnp.sum(b_up, axis=0),
             sums[0],
         ]
+    ).reshape(D, narrow)
+    small_terms = jnp.pad(small_terms, ((0, 0), (0, HALF - narrow)))
+    last = jnp.concatenate([g_qkv, small_terms], axis=1).astype(BF)
+    last = scatter_sum(last, count)
+    last_other = to_other(last)
+    late_other = to_other(late)
+    wide_like, down_like = sds(wide_w.shape, F32), sds(down_w.shape, F32)
+    wide_first, wide_second, wide_upd, down_first, down_second, down_upd, squares = plain(
+        moment_kernel,
+        "moment",
+        [wide_like] * 3 + [down_like] * 3 + [sds((8, HALF), F32)],
+        *(last, last_other, late, late_other),
+        *(wide_w, wide_m, wide_v, down_w, down_m, down_v),
     )
-    wide_terms = jnp.concatenate([g_qkv, g_out, g_up], axis=1)
-    shard_wide, shard_down, shard_small = (
-        lax.psum_scatter(wide_terms, "fsdp", scatter_dimension=0, tiled=True),
-        lax.psum_scatter(g_down_t.T, "fsdp", scatter_dimension=0, tiled=True),
-        lax.psum_scatter(small_terms, "fsdp", scatter_dimension=0, tiled=True),
+    squares = add_all(squares, count)
+    wide_new, wide_avg, down_new, down_avg, norms = plain(
+        update_kernel,
+        "update",
+        [wide_like] * 2 + [down_like] * 2 + [sds((8, HALF), F32)],
+        *(squares, wide_w, wide_upd, wide_ema, down_w, down_upd, down_ema),
     )
-    shard_wide, shard_down, shard_small = lax.psum((shard_wide, shard_down, shard_small), "dp")
-    wide_first, wide_second, wide_dir = moments(shard_wide, wide_m, wide_v)
-    down_first, down_second, down_dir = moments(shard_down, down_m, down_v)
+    shard_small = (last + last_other)[:, 3 * D : 3 * D + narrow].reshape(-1)
     small_first, small_second, small_dir = moments(shard_small, small_m, small_v)
-    wide_upd = wide_dir + DECAY * wide_w
-    down_upd = down_dir + DECAY * down_w
-    update_sq = matrix_squares(wide_upd, down_upd)
-    weight_total, update_total = lax.psum((weight_sq, update_sq), "fsdp")
-    weight_norm = jnp.sqrt(weight_total)
-    update_norm = jnp.sqrt(update_total)
-    ratio = weight_norm / update_norm
-    column_ratio = jnp.concatenate(
-        [
-            ratio[0] * jnp.ones((3 * D,), jnp.float32),
-            ratio[1] * jnp.ones((D,), jnp.float32),
-            ratio[2] * jnp.ones((FF,), jnp.float32),
-        ]
-    )
-    wide_new = wide_w - RATE * column_ratio * wide_upd
-    down_new = down_w - RATE * ratio[3] * down_upd
     small_new = small_p - RATE * small_dir
     ema_keep = min(EMA_CEILING, (1.0 + STEP) / (10.0 + STEP))
-    wide_avg = ema_keep * wide_ema + (1.0 - ema_keep) * wide_new
-    down_avg = ema_keep * down_ema + (1.0 - ema_keep) * down_new
     small_avg = ema_keep * small_ema + (1.0 - ema_keep) * small_new
-    norms = jnp.stack([weight_norm, update_norm])
     return (
         block_out,
         grad_in,
@@ -793,7 +877,7 @@
         small_first,
         small_second,
         small_avg,
-        norms,
+        norms[:, 0].reshape(2, 4),
     )
 
 
@@ -802,5 +886,9 @@
     in_specs = (tok, tok, P(("dp", "fsdp"))) + (row,) * 8 + (vec,) * 4
     out_specs = (tok, tok) + (row,) * 8 + (vec,) * 4 + (P(),)
     return jax.shard_map(
-        on_device, mesh=mesh, in_specs=in_specs, out_specs=out_specs, check_vma=False
+        functools.partial(on_device, mesh.shape["fsdp"]),
+        mesh=mesh,
+        in_specs=in_specs,
+        out_specs=out_specs,
+        check_vma=False,
     )

time: 536 us -> 296 us (0.55)
  blocking collectives: 199 us -> 0 us
  waiting for transfers between devices: 84.2 us -> 36.9 us
  starting transfers between devices: 0.34 us -> 29.3 us
  between operations: 16.2 us -> 0.98 us
  other arithmetic: 19.1 us -> 12 us
    psum x2 -> x0, blocking collectives: 79.5 us -> none  [the longest x1 77 us: on_device(): weight_total, update_total = lax.psum((weight_sq, update_sq), 'fsdp')]
    unnamed x1 -> x0, blocking collectives: 78.8 us -> none
    reduce_scatter x2 -> x0, waiting for transfers between devices: 66.7 us -> none  [the longest x1 66.7 us: on_device(): lax.psum_scatter(wide_terms, 'fsdp', scatter_dimension=0, tiled=True)]
    all_gather x1 -> x0, blocking collectives: 40.9 us -> none  [on_device(): down_all = lax.all_gather(down_w.astype(BF), 'fsdp', axis=0, tiled=True)]
    all_to_all x0 -> x4, starting transfers between devices: none -> 25.9 us  [the longest x2 13.8 us: scatter_sum(): return jnp.sum(lax.all_to_all(terms, 'fsdp', 0, 0).astype(F32), axis=0)]
    all_to_all x0 -> x4, waiting for transfers between devices: none -> 24.8 us  [the longest x2 13 us: gather(): return lax.all_to_all(copies, 'fsdp', 0, 0).reshape(-1, values.shape[1])]
    psum x1 -> x0, waiting for transfers between devices: 17.4 us -> none  [on_device(): lax.psum((shard_wide, shard_down, shard_small), 'dp')]
    ppermute x0 -> x6, waiting for transfers between devices: none -> 12 us  [the longest x4 10.8 us: add_all(): lax.ppermute(values, 'fsdp', [(i, i ^ step) for i in range(count)])]
  transfers between devices with their start and end apart: 4 -> 10, of which waited for: 2 -> 7; matrix products, arithmetic and copies ran while one was open for 2% -> 4% of each run, Pallas kernels for 16% -> 47%
where the time goes in v2:
time: 296 us; the launch traced here: 295 us
  Pallas kernels  203 us (69%)
  waiting for transfers between devices  36.9 us (12%)
  starting transfers between devices  29.3 us (10%)
  local copies, waits for them, and re-layouts  12.5 us (4%)
  other arithmetic  12 us (4%)
    pallas_call x1, Pallas kernels, run_back(): pl.pallas_call(back_kernel, grid=(images,), in_specs=[image_of(b.shape[1:...  75.6 us
    pallas_call x1, Pallas kernels, run_feed(): pl.pallas_call(feed_kernel, grid_spec=pltpu.PrefetchScalarGridSpec(num_sc...  61.7 us
    pallas_call x1, Pallas kernels, run_attend(): pl.pallas_call(attend_kernel, grid=(images,), in_specs=[tokens(), whole(w...  61.5 us
    all_to_all x2, starting transfers between devices, scatter_sum(): return jnp.sum(lax.all_to_all(terms, 'fsdp', 0, 0).astype(F32), axis=0)  13.8 us
    all_to_all x2, waiting for transfers between devices, gather(): return lax.all_to_all(copies, 'fsdp', 0, 0).reshape(-1, values.shape[1])  13 us
    all_to_all x2, starting transfers between devices, gather(): return lax.all_to_all(copies, 'fsdp', 0, 0).reshape(-1, values.shape[1])  12.1 us
    all_to_all x2, waiting for transfers between devices, scatter_sum(): return jnp.sum(lax.all_to_all(terms, 'fsdp', 0, 0).astype(F32), axis=0)  11.8 us
    ppermute x4, waiting for transfers between devices, add_all(): lax.ppermute(values, 'fsdp', [(i, i ^ step) for i in range(count)])  10.8 us
  transfers between devices with their start and end apart: 10, of which 7 were waited for; matrix products, arithmetic and copies ran while one was open for 4% of the time, Pallas kernels for 47%

profile of v2, /device:TPU:0, one launch (start us, length us, event | category | flops | bytes accessed | tf_op | source)
XLA Modules:
  0.0 294.6 jit_solution(1844598891059552410)
XLA Ops:
  0.6 0.9 convert_element_type.26
  1.6 0.7 convert_element_type.27
  2.3 0.1 reshape.80
  2.4 0.8 broadcast_in_dim.4
  3.2 8.3 %all-to-all-start = ((bf16[16,16,896]{2,1,0:T(8,128)(2,1)}), bf16[16,16,896]{2,1,0:T(8,128)(2,1)S(1)}, u32[]{:S(2)}, u32[]{:S(2)}) async-start(bf16[16,16,896]{2,1,0:T(8,128)(2,1)} %broadcast_in_dim.4), calls=%async_computation | async-start | bytes 917504 | tf_op jit(solution)/shard_map/all_to_all | solution.py:766
  11.5 0.8 convert_element_type.28
  12.4 13.0 %all-to-all-done = bf16[16,16,896]{2,1,0:T(8,128)(2,1)S(1)} async-done(((bf16[16,16,896]{2,1,0:T(8,128)(2,1)}), bf16[16,16,896]{2,1,0:T(8,128)(2,1)S(1)}, u32[]{:S(2)}, u32[]{:S(2)}) %all-to-all-start) | async-done | bytes 458784 | tf_op jit(solution)/shard_map/all_to_all | solution.py:766
  25.4 1.1 broadcast_in_dim.5
  26.4 3.8 %all-to-all-start.1 = ((bf16[16,16,2304]{2,1,0:T(8,128)(2,1)}), bf16[16,16,2304]{2,1,0:T(8,128)(2,1)S(1)}, u32[]{:S(2)}, u32[]{:S(2)}) async-start(bf16[16,16,2304]{2,1,0:T(8,128)(2,1)} %broadcast_in_dim.5), calls=%async_computation.1 | async-start | bytes 2359296 | tf_op jit(solution)/shard_map/all_to_all | solution.py:766
  30.2 0.8 slice.108.w_ref
  31.0 0.2 reshape.90
  31.2 0.6 pad.18.s_ref
  31.9 0.6 pad.19.k_ref
  32.5 61.5 %attend.1 = (bf16[8,688,256]{2,1,0:T(8,128)(2,1)}, bf16[8,688,256]{2,1,0:T(8,128)(2,1)}, bf16[8,14,128,384]{3,2,1,0:T(8,128)(2,1)}, bf16[8,14,112,512]{3,2,1,0:T...) custom-call(f32[5440,256]{1,0:T(8,128)} %x_ref.5, bf16[256,768]{1,0:T(8,128)(2,1)} %slice.108.w_ref, ...), custom_call_target="tpu_custom_call" | custom-call | tf_op jit(solution)/shard_map/attend/pallas_call | solution.py:568
  94.1 0.4 reshape.84
  94.5 0.9 copy.43
  95.3 61.7 %feed.1 = (f32[5440,256]{1,0:T(8,128)}, f32[5440,256]{1,0:T(8,128)}, bf16[8,688,256]{2,1,0:T(8,128)(2,1)}, bf16[256,1280]{1,0:T(8,128)(2,1)}, bf16[1024,256]{1,0...) custom-call(s32[8]{0:T(128)} %cnt_ref.1, f32[5440,256]{1,0:T(8,128)} %x_ref.5, f32[5440,256]{1,0:T(8,128)} %c_ref.1, ...), custom_call_target="tpu_custom_call" | custom-call | tf_op jit(solution)/shard_map/feed/pallas_call | solution.py:586
  157.0 1.3 copy.47
  158.3 0.4 concatenate.39
  158.7 2.2 pad_maximum_fusion
  160.9 6.9 %all-to-all-start.3 = ((bf16[16,16,2304]{2,1,0:T(8,128)(2,1)}), bf16[16,16,2304]{2,1,0:T(8,128)(2,1)S(1)}, u32[]{:S(2)}, u32[]{:S(2)}) async-start(bf16[16,16,2304]{2,1,0:T(8,128)(2,1)} %pad_maximum_fusion), calls=%async_computation.3 | async-start | bytes 2359296 | tf_op jit(solution)/shard_map/all_to_all | solution.py:771
  167.8 75.6 %back.1 = (f32[5440,256]{1,0:T(8,128)}, f32[256,768]{1,0:T(8,128)}, f32[3,9,8,256]{3,2,1,0:T(8,128)}, f32[8,768]{1,0:T(8,128)}, f32[2,8,256]{2,1,0:T(8,128)}) custom-call(bf16[8,688,256]{2,1,0:T(8,128)(2,1)} %get-tuple-element.47.datt_ref, bf16[8,14,128,384]{3,2,1,0:T(8,128)(2,1)} %get-tuple-element.48.win_ref, ...), custom_call_target="tpu_custom_call" | custom-call | tf_op jit(solution)/shard_map/back/pallas_call | solution.py:640
  243.4 1.2 convert.51
  244.7 1.0 reduce_sum.65
  245.7 0.7 reduce_sum.63
  246.5 0.8 reduce_sum.64
  247.3 0.2 dynamic-update-slice
  247.6 0.2 dynamic-update-slice.1
  247.8 0.2 dynamic-update-slice.2
  248.0 0.3 dynamic-update-slice.3
  248.3 0.2 dynamic-update-slice.4
  248.5 0.2 dynamic-update-slice.5
  248.7 0.2 dynamic-update-slice.6
  248.9 0.2 dynamic-update-slice.7
  249.1 0.2 dynamic-update-slice.8
  249.3 0.2 dynamic-update-slice.9
  249.5 0.2 reshape.87
  249.8 0.8 pad_maximum_fusion.1
  250.6 6.9 %all-to-all-start.2 = ((bf16[16,16,896]{2,1,0:T(8,128)(2,1)}), bf16[16,16,896]{2,1,0:T(8,128)(2,1)S(1)}, u32[]{:S(2)}, u32[]{:S(2)}) async-start(bf16[16,16,896]{2,1,0:T(8,128)(2,1)} %pad_maximum_fusion.1), calls=%async_computation.2 | async-start | bytes 917504 | tf_op jit(solution)/shard_map/all_to_all | solution.py:771
  257.5 0.2 convert_reduce_fusion.gl_ref
  257.6 0.1 collective-permute-start.1
  257.7 11.8 %all-to-all-done.2 = bf16[16,16,896]{2,1,0:T(8,128)(2,1)S(1)} async-done(((bf16[16,16,896]{2,1,0:T(8,128)(2,1)}), bf16[16,16,896]{2,1,0:T(8,128)(2,1)S(1)}, u32[]{:S(2)}, u32[]{:S(2)}) %all-to-all-start.2) | async-done | bytes 458784 | tf_op jit(solution)/shard_map/all_to_all | solution.py:771
  269.5 0.1 convert_reduce_fusion.1.gq_ref
  269.6 0.1 collective-permute-start
  269.7 1.2 collective-permute-done.gq_other_ref
  271.0 0.6 copy-done.4
  271.6 0.6 copy-done.3
  272.2 2.1 moment.1
  274.3 0.6 collective-permute-start.2
  274.9 3.3 %collective-permute-done.2 = f32[8,128]{1,0:T(8,128)S(1)} collective-permute-done((f32[8,128]{1,0:T(8,128)}, f32[8,128]{1,0:T(8,128)S(1)}, u32[]{:S(2)}, u32[]{:S(2)}) %collective-permute-start.2) | collective-permute-done | bytes 4128 | tf_op jit(solution)/shard_map/ppermute | solution.py:777
  278.1 0.7 add.64
  278.8 0.9 collective-permute-start.3
  279.8 2.7 collective-permute-done.3
  282.4 1.2 collective-permute-start.4
  283.6 0.7 slice_add_fusion
  284.3 0.1 reshape.89
  284.4 1.6 collective-permute-done.4
  286.1 0.6 collective-permute-start.5
  286.7 0.6 multiply_add_fusion
  287.3 3.3 %collective-permute-done.5 = f32[8,128]{1,0:T(8,128)S(1)} collective-permute-done((f32[8,128]{1,0:T(8,128)S(1)}, f32[8,128]{1,0:T(8,128)S(1)}, u32[]{:S(2)}, u32[]{:S(2)}) %collective-permute-start.5) | collective-permute-done | bytes 4128 | tf_op jit(solution)/shard_map/ppermute | solution.py:777
  290.6 0.6 add.67.sq_ref
  291.2 2.0 update.1
  293.1 0.8 slice_reduce_fusion
  293.9 0.6 reshape_squeeze.3
  (46 shorter events, 0.3 us)
Async XLA Ops:
  3.2 22.2 %all-to-all-start = ((bf16[16,16,896]{2,1,0:T(8,128)(2,1)}), bf16[16,16,896]{2,1,0:T(8,128)(2,1)S(1)}, u32[]{:S(2)}, u32[]{:S(2)}) async-start(bf16[16,16,896]{2,1,0:T(8,128)(2,1)} %broadcast_in_dim.4), calls=%async_computation | async-start | bytes 917504 | tf_op jit(solution)/shard_map/all_to_all | solution.py:766
  26.4 67.5 %all-to-all-start.1 = ((bf16[16,16,2304]{2,1,0:T(8,128)(2,1)}), bf16[16,16,2304]{2,1,0:T(8,128)(2,1)S(1)}, u32[]{:S(2)}, u32[]{:S(2)}) async-start(bf16[16,16,2304]{2,1,0:T(8,128)(2,1)} %broadcast_in_dim.5), calls=%async_computation.1 | async-start | bytes 2359296 | tf_op jit(solution)/shard_map/all_to_all | solution.py:766
  94.0 1.3 copy-start
  160.9 89.7 %all-to-all-start.3 = ((bf16[16,16,2304]{2,1,0:T(8,128)(2,1)}), bf16[16,16,2304]{2,1,0:T(8,128)(2,1)S(1)}, u32[]{:S(2)}, u32[]{:S(2)}) async-start(bf16[16,16,2304]{2,1,0:T(8,128)(2,1)} %pad_maximum_fusion), calls=%async_computation.3 | async-start | bytes 2359296 | tf_op jit(solution)/shard_map/all_to_all | solution.py:771
  167.8 79.4 %copy-start.5 = (f32[5,8,256]{2,1,0:T(8,128)S(1)}, f32[5,8,256]{2,1,0:T(8,128)}, u32[]{:S(2)}) copy-start(f32[5,8,256]{2,1,0:T(8,128)} %get-tuple-element.59) | copy-start | bytes 122884
  167.8 79.4 %copy-start.6 = (f32[8,1024]{1,0:T(8,128)S(1)}, f32[8,1024]{1,0:T(8,128)}, u32[]{:S(2)}) copy-start(f32[8,1024]{1,0:T(8,128)} %get-tuple-element.60) | copy-start | bytes 98308
  244.6 42.1 %copy-start.7 = (f32[368]{0:T(512)S(1)}, f32[368]{0:T(512)}, u32[]{:S(2)}) copy-start(f32[368]{0:T(512)} %param.37) | copy-start | bytes 4420
  244.6 42.1 %copy-start.8 = (f32[368]{0:T(512)S(1)}, f32[368]{0:T(512)}, u32[]{:S(2)}) copy-start(f32[368]{0:T(512)} %param.40) | copy-start | bytes 4420
  244.6 42.0 %copy-start.9 = (f32[368]{0:T(512)S(1)}, f32[368]{0:T(512)}, u32[]{:S(2)}) copy-start(f32[368]{0:T(512)} %param.38) | copy-start | bytes 4420
  244.7 42.0 %copy-start.10 = (f32[368]{0:T(512)S(1)}, f32[368]{0:T(512)}, u32[]{:S(2)}) copy-start(f32[368]{0:T(512)} %param.39) | copy-start | bytes 4420
  250.6 19.0 %all-to-all-start.2 = ((bf16[16,16,896]{2,1,0:T(8,128)(2,1)}), bf16[16,16,896]{2,1,0:T(8,128)(2,1)S(1)}, u32[]{:S(2)}, u32[]{:S(2)}) async-start(bf16[16,16,896]{2,1,0:T(8,128)(2,1)} %pad_maximum_fusion.1), calls=%async_computation.2 | async-start | bytes 917504 | tf_op jit(solution)/shard_map/all_to_all | solution.py:771
  257.6 13.3 %copy-start.1 = (f32[16,2304]{1,0:T(8,128)}, f32[16,2304]{1,0:T(8,128)S(1)}, u32[]{:S(2)}) copy-start(f32[16,2304]{1,0:T(8,128)S(1)} %convert_reduce_fusion.gl_ref) | copy-start | bytes 442372
  257.6 13.3 %collective-permute-start.1 = (f32[16,2304]{1,0:T(8,128)S(1)}, f32[16,2304]{1,0:T(8,128)S(1)}, u32[]{:S(2)}, u32[]{:S(2)}) collective-permute-start(f32[16,2304]{1,0:T(8,128)S(1)} %convert_reduce_fusion.gl_ref), channel_id=1, source_target_pairs={{0,16},{16,0},{1,17},{17,1},{2,18},{18,2},{3,19},{19,3},{4,20},{20... | collective-permute-start | bytes 442376 | tf_op jit(solution)/shard_map/ppermute | solution.py:755
  269.6 1.3 copy-start.2
  269.6 1.3 collective-permute-start
  270.9 0.6 copy-start.4
  271.6 0.7 copy-start.3
  274.3 3.8 %collective-permute-start.2 = (f32[8,128]{1,0:T(8,128)}, f32[8,128]{1,0:T(8,128)S(1)}, u32[]{:S(2)}, u32[]{:S(2)}) collective-permute-start(f32[8,128]{1,0:T(8,128)} %get-tuple-element.63), channel_id=1, source_target_pairs={{0,1},{1,0},{2,3},{3,2},{4,5},{5,4},{6,7},{7,6},{8,9},{9,8},{10,11... | collective-permute-start | bytes 12296 | tf_op jit(solution)/shard_map/ppermute | solution.py:777
  278.8 3.6 %collective-permute-start.3 = (f32[8,128]{1,0:T(8,128)S(1)}, f32[8,128]{1,0:T(8,128)S(1)}, u32[]{:S(2)}, u32[]{:S(2)}) collective-permute-start(f32[8,128]{1,0:T(8,128)S(1)} %add.64), channel_id=1, source_target_pairs={{0,2},{1,3},{2,0},{3,1},{4,6},{5,7},{6,4},{7,5},{8,10},{9,11},{10,... | collective-permute-start | bytes 12296 | tf_op jit(solution)/shard_map/ppermute | solution.py:777
  282.4 3.6 %collective-permute-start.4 = (f32[8,128]{1,0:T(8,128)S(1)}, f32[8,128]{1,0:T(8,128)S(1)}, u32[]{:S(2)}, u32[]{:S(2)}) collective-permute-start(f32[8,128]{1,0:T(8,128)S(1)} %add.65), channel_id=1, source_target_pairs={{0,4},{1,5},{2,6},{3,7},{4,0},{5,1},{6,2},{7,3},{8,12},{9,13},{10,... | collective-permute-start | bytes 12296 | tf_op jit(solution)/shard_map/ppermute | solution.py:777
  286.1 4.5 %collective-permute-start.5 = (f32[8,128]{1,0:T(8,128)S(1)}, f32[8,128]{1,0:T(8,128)S(1)}, u32[]{:S(2)}, u32[]{:S(2)}) collective-permute-start(f32[8,128]{1,0:T(8,128)S(1)} %add.66), channel_id=1, source_target_pairs={{0,8},{1,9},{2,10},{3,11},{4,12},{5,13},{6,14},{7,15},{8,0},{9,1},... | collective-permute-start | bytes 12296 | tf_op jit(solution)/shard_map/ppermute | solution.py:777

commit v3 on v2

v3 whole, which is shorter than its diff:
```python
import functools

import jax
import jax.numpy as jnp
import numpy as np
from jax import lax
from jax.experimental import pallas as pl
from jax.experimental.pallas import tpu as pltpu
from jax.sharding import PartitionSpec as P

D = 256
FF = 1024
HEAD = 32
STRIPE = 7
GRID_L = 14
GRID_S = 6
SMALL = 8
STEP = 10
TOK_IMG = 680

EPSILON = 1e-05
BETA_ONE = 0.9
BETA_TWO = 0.999
ADAM_EPS = 1e-06
DECAY = 0.05
RATE = 0.25
EMA_CEILING = 0.9999

ROWS = 688
BIG = 2 * GRID_L * GRID_L
PAIRS = 7
WIN = 128
QROWS = 112
HALF = 128
HEADS = 4
SCALE = HEAD**-0.5
LOG2E = 1.4426950408889634
LN2 = 0.6931471805599453
CHUNKS = ((0, 240), (240, 464), (464, 688))
LONG = 744
EDGE = 16
COPIES = (3, 3, 2)
TAPS = tuple((dy, dx) for dy in (-1, 0, 1) for dx in (-1, 0, 1))
ORDER = (0, 2, 1, 3, 4, 5, 6)
VMEM = 62 * 1024 * 1024

BF = jnp.bfloat16
F32 = jnp.float32


def kind_of(pair):
    return 0 if pair < 2 else 1 if pair < 4 else 2


def branch_of(pair, member):
    return 0 if pair < 2 else 1 if pair < 4 else member


def first_of(pair, member):
    if pair < 2:
        return pair * GRID_L * GRID_L + member * STRIPE * GRID_L
    if pair < 4:
        return (pair - 2) * GRID_L * GRID_L + member * STRIPE
    return BIG + (pair - 4) * COPIES[0] * GRID_S * GRID_S


def tokens_of(pair):
    return STRIPE * GRID_L if pair < 4 else COPIES[pair - 4] * GRID_S * GRID_S


def shape_of(kind):
    return ((STRIPE, GRID_L), (GRID_L, STRIPE), (GRID_S, GRID_S))[kind]


def edge_masks():
    out = np.zeros((3, 9, QROWS, HALF), np.float32)
    for kind in range(3):
        high, broad = shape_of(kind)
        size = high * broad
        for copy in range(1 if kind < 2 else COPIES[0]):
            for at in range(size):
                r, c = divmod(at, broad)
                for tap, (dy, dx) in enumerate(TAPS):
                    if 0 <= r + dy < high and 0 <= c + dx < broad:
                        out[kind, tap, copy * size + at] = 1
    return out


def tap_matrix(kind):
    shape = shape_of(kind)
    copies = 1 if kind < 2 else COPIES[0]
    size = shape[0] * shape[1]
    out = np.zeros((9, QROWS, WIN), np.float32)
    for copy in range(copies):
        for r in range(shape[0]):
            for c in range(shape[1]):
                for tap in range(9):
                    rr, cc = r + tap // 3 - 1, c + tap % 3 - 1
                    if 0 <= rr < shape[0] and 0 <= cc < shape[1]:
                        out[tap, copy * size + r * shape[1] + c, copy * size + rr * shape[1] + cc] = 1
    return out


def mask_operands():
    size = GRID_S * GRID_S
    rows = np.zeros((3, QROWS, HALF), np.float32)
    keys = np.zeros((3, WIN, HALF), np.float32)
    rows[0, :, 0] = 1
    keys[0, STRIPE * GRID_L :, 0] = -1e30
    for kind, crops in ((1, 3), (2, 2)):
        for at in range(QROWS):
            rows[kind, at, at // size if at < crops * size else 0] = 1
        for at in range(WIN):
            for crop in range(crops):
                if at >= crops * size or at // size != crop:
                    keys[kind, at, crop] = -1e30
    return rows, np.tile(keys, (1, HEADS, 1))


def bf(array):
    return jnp.asarray(array, BF)


def dot(left, right):
    return jnp.dot(left, right, preferred_element_type=F32)


def dot_nt(left, right):
    return lax.dot_general(left, right, (((1,), (1,)), ((), ())), preferred_element_type=F32)


def dot_tn(left, right):
    return lax.dot_general(left, right, (((0,), (0,)), ((), ())), preferred_element_type=F32)


def normalise(values):
    center = values - jnp.mean(values, axis=-1, keepdims=True)
    spread = jnp.mean(center * center, axis=-1, keepdims=True)
    scale = lax.rsqrt(spread + EPSILON)
    return center * scale, scale


def norm_back(grad_hat, hat, scale):
    mean_grad = jnp.mean(grad_hat, axis=-1, keepdims=True)
    mean_dot = jnp.mean(grad_hat * hat, axis=-1, keepdims=True)
    return scale * (grad_hat - mean_grad - hat * mean_dot)


def rows_of(ref, low, high):
    if high <= TOK_IMG:
        return ref[low:high, :]
    tail = jnp.zeros((high - TOK_IMG, ref.shape[1]), F32)
    return jnp.concatenate([ref[low:TOK_IMG, :], tail], axis=0)


def store_rows(ref, low, high, values):
    last = min(high, TOK_IMG)
    ref[low:last, :] = values[: last - low]


def fold(values):
    return jnp.sum(values.reshape(values.shape[0] // 8, 8, values.shape[1]), axis=0)


def head_lanes(head):
    lanes = lax.broadcasted_iota(jnp.int32, (1, HALF), 1)
    return jnp.where(lanes // HEAD == head, 1.0, 0.0).astype(BF)


def by_head(values):
    return jnp.concatenate([values * head_lanes(h) for h in range(HEADS)], axis=0)


def head_block(rows):
    return jnp.concatenate(
        [jnp.broadcast_to(head_lanes(h), (rows, HALF)) for h in range(HEADS)], axis=0
    )


def first_rows(values, count):
    low = count // 16 * 16
    if low >= values.shape[0]:
        return values
    row = lax.broadcasted_iota(jnp.int32, (values.shape[0] - low, 1), 0)
    tail = jnp.where(row < count - low, values[low:], 0.0)
    return jnp.concatenate([values[:low], tail], axis=0)


def pieces_of(pair, member):
    low = first_of(pair, member)
    return [(low + r * GRID_L, r * STRIPE) for r in range(GRID_L)]


def pipelined(stages, order, extra=()):
    extra = dict(extra)
    state = {}
    for turn in range(len(order) + len(stages) - 1):
        if turn in extra:
            extra[turn]()
        for at, stage in enumerate(stages):
            item = turn - at
            if 0 <= item < len(order):
                state[order[item]] = stage(order[item], state.get(order[item]))


def attend_kernel(
    x_ref,
    w_ref,
    s_ref,
    k_ref,
    tap_ref,
    mrow_ref,
    mkey_ref,
    hat_ref,
    att_ref,
    win_ref,
    e_ref,
    il_ref,
    o_ref,
    qkv_scr,
    turn_scr,
    back_scr,
    att_scr,
):
    @pl.when(pl.program_id(0) == 0)
    def _():
        for branch in range(2):
            qkv_scr[branch, ROWS:, :] = jnp.zeros((LONG - ROWS, 3 * HALF), F32)
        turn_scr[...] = jnp.zeros_like(turn_scr)
        att_scr[TOK_IMG:, :] = jnp.zeros((ROWS - TOK_IMG, D), F32)

    gain, shift = s_ref[0:1, :], s_ref[1:2, :]
    ones = head_block(WIN)

    def project(chunk):
        low, high = CHUNKS[chunk]
        hat, _ = normalise(rows_of(x_ref, low, high))
        hat_ref[0, low:high, :] = hat.astype(BF)
        a = (hat * gain + shift).astype(BF)
        for part in range(3):
            lanes = slice(part * D, (part + 1) * D)
            piece = dot(a, w_ref[:, lanes]) + s_ref[2 + part : 3 + part, :]
            if part == 0:
                piece = piece * (SCALE * LOG2E)
            for branch in range(2):
                qkv_scr[branch, low:high, part * HALF : (part + 1) * HALF] = piece[
                    :, branch * HALF : (branch + 1) * HALF
                ]

    def score(pair, _):
        state = []
        mask = max(pair - 4, 0) if pair < 4 else (1 if pair < 6 else 2)
        for member in range(2):
            at = 2 * pair + member
            if kind_of(pair) == 1:
                for source, target in pieces_of(pair, member):
                    turn_scr[at - 4, target : target + STRIPE, :] = qkv_scr[
                        1, source : source + STRIPE, :
                    ]
                window = turn_scr[at - 4, :QROWS, :]
            else:
                low = first_of(pair, member)
                window = qkv_scr[branch_of(pair, member), low : low + QROWS, :]
            window = window.astype(BF)
            win_ref[0, at] = window
            q, k, v = (window[:, part * HALF : (part + 1) * HALF] for part in range(3))
            none = jnp.zeros((WIN - QROWS, HALF), BF)
            k = jnp.concatenate([k, none], axis=0)
            left = jnp.concatenate([q, mrow_ref[mask]], axis=1)
            right = jnp.concatenate([by_head(k), mkey_ref[mask]], axis=1)
            state.append((v, dot_nt(left, right)))
        return state

    def soften(pair, state):
        new = []
        for member, (v, scores) in enumerate(state):
            exps = []
            for h in range(HEADS):
                part = scores[:, h * WIN : (h + 1) * WIN]
                peak = jnp.max(part, axis=-1, keepdims=True)
                exps.append(jnp.exp2(part - peak).astype(BF))
            e = jnp.concatenate(exps, axis=1)
            e_ref[0, 2 * pair + member] = e
            new.append((v, e))
        return new

    def mix(pair, state):
        taps, mixed = [], []
        none = jnp.zeros((WIN - QROWS, HALF), BF)
        for member, (v, e) in enumerate(state):
            at = 2 * pair + member
            kernel = k_ref[branch_of(pair, member)]
            v = jnp.concatenate([v, none], axis=0)
            both = dot(e, jnp.concatenate([by_head(v), ones], axis=1))
            inv = 1.0 / both[:, HALF:]
            o = both[:, :HALF] * inv
            il_ref[0, at] = inv
            o_ref[0, at] = o.astype(BF)
            mixed.append(o + kernel[9:10])
            low = kernel.astype(BF)
            taps.append(jnp.concatenate([v * low[tap : tap + 1] for tap in range(9)], axis=0))
        conv = dot(tap_ref[kind_of(pair)], jnp.concatenate(taps, axis=1))
        for member in range(2):
            piece = mixed[member] + conv[:, member * HALF : (member + 1) * HALF]
            branch = branch_of(pair, member)
            lanes = slice(branch * HALF, (branch + 1) * HALF)
            if kind_of(pair) == 1:
                at = 2 * pair + member - 4
                back_scr[at] = piece
                for source, target in pieces_of(pair, member):
                    att_scr[source : source + STRIPE, lanes] = back_scr[
                        at, target : target + STRIPE, :
                    ]
            else:
                low, count = first_of(pair, member), tokens_of(pair)
                att_scr[low : low + count, lanes] = piece[:count]

    project(0)
    extra = {1: functools.partial(project, 1), 3: functools.partial(project, 2)}
    pipelined((score, soften, mix), ORDER, extra)
    att_ref[0] = att_scr[...].astype(BF)


def gelu_parts(u):
    phi = 0.5 * lax.erf(u * 2**-0.5) + 0.5
    decay = jnp.exp2((-0.5 * LOG2E) * (u * u))
    return phi, phi + (u * 0.3989422804014327) * decay


def beside(*streams):
    left = [[list(stream), 0] for stream in streams]
    total = max((len(steps) for steps, _ in left), default=0)
    for at in range(total):
        for entry in left:
            steps, done = entry
            goal = -(-len(steps) * (at + 1) // total)
            for step in steps[done:goal]:
                step()
            entry[1] = goal


def feed_kernel(
    shard,
    cnt_ref,
    x_ref,
    c_ref,
    att_ref,
    w_ref,
    down_ref,
    s_ref,
    out_ref,
    dx_ref,
    datt_ref,
    pack_ref,
    sums_ref,
    bup_ref,
    h2_scr,
    u_scr,
    dg_scr,
    g_scr,
    du_scr,
    dy_scr,
    dz_scr,
    x1_scr,
    hat_scr,
    rs_scr,
    gup_scr,
    gdn_scr,
    gout_scr,
    turn_scr,
    pack_scr,
):
    image = pl.program_id(0)

    @pl.when(image == 0)
    def _():
        for ref in (gup_scr, gdn_scr, gout_scr, sums_ref, bup_ref):
            ref[...] = jnp.zeros_like(ref)

    bound = BIG + GRID_S * GRID_S * cnt_ref[image]
    bias_out, gain, shift = s_ref[15:16, :], s_ref[16:17, :], s_ref[17:18, :]

    def masked(low, high):
        row = low + lax.broadcasted_iota(jnp.int32, (high - low, 1), 0)
        return jnp.where(row < bound, rows_of(c_ref, low, high), 0.0)

    def enter(chunk):
        low, high = CHUNKS[chunk]

        def cot():
            dyr = masked(low, high).astype(BF)
            dy_scr[low:high, :] = dyr
            sums_ref[0] += fold(dyr.astype(F32))

        def norm():
            att = att_ref[0, low:high, :]
            x1 = rows_of(x_ref, low, high) + dot(att, w_ref[:, :D]) + bias_out
            x1_scr[low:high, :] = x1
            hat, scale = normalise(x1)
            hat_scr[low:high, :] = hat
            rs_scr[low:high, :] = scale
            h2_scr[low:high, :] = (hat * gain + shift).astype(BF)

        return [cot, norm]

    def expand(chunk):
        low, high = CHUNKS[chunk]

        def up(lanes):
            dy = dy_scr[low:high, :]
            dg_scr[low:high, lanes] = dot_nt(dy, down_ref[lanes, :])

        def hidden(lanes):
            cols = slice(D + lanes.start, D + lanes.stop)
            u_scr[low:high, lanes] = dot(h2_scr[low:high, :], w_ref[:, cols])

        steps = []
        for part in range(4):
            lanes = slice(part * D, (part + 1) * D)
            steps += [functools.partial(up, lanes), functools.partial(hidden, lanes)]
        return steps

    def gelu(chunk):
        low, high = CHUNKS[chunk]
        totals = {}

        def step(part, at):
            lanes = slice(part * D, (part + 1) * D)
            u = u_scr[at : at + 16, lanes] + s_ref[18 + part : 19 + part, :]
            phi, slope = gelu_parts(u)
            g_scr[at : at + 16, lanes] = (u * phi).astype(BF)
            du = dg_scr[at : at + 16, lanes] * slope
            totals[part] = fold(du) + totals[part] if part in totals else fold(du)
            du_scr[at : at + 16, lanes] = du.astype(BF)
            if at + 16 >= high:
                bup_ref[:, lanes] += totals[part]

        return [
            functools.partial(step, part, at) for part in range(4) for at in range(low, high, 16)
        ]

    def contract(chunk):
        low, high = CHUNKS[chunk]

        def back():
            dh2 = dot_nt(du_scr[low:high, :], w_ref[:, D : D + FF])
            hat = hat_scr[low:high, :]
            sums_ref[1] += fold(dh2 * hat)
            sums_ref[2] += fold(dh2)
            dx = masked(low, high) + norm_back(dh2 * gain, hat, rs_scr[low:high, :])
            store_rows(dx_ref, low, high, dx)
            dz = dx.astype(BF)
            dz_scr[low:high, :] = dz
            sums_ref[3] += fold(dz.astype(F32))

        def out():
            block = x1_scr[low:high, :] + dot(g_scr[low:high, :], down_ref[...])
            store_rows(out_ref, low, high, block + s_ref[22:23, :])

        def attention():
            datt = dot_nt(dz_scr[low:high, :], w_ref[:, :D])
            sums_ref[4] += fold(datt)
            datt_ref[0, low:high, :] = datt.astype(BF)

        return [back, out, attention]

    def weights(chunk):
        low, high = CHUNKS[chunk]

        def up(lanes):
            gup_scr[:, lanes] += dot_tn(h2_scr[low:high, :], du_scr[low:high, lanes])

        def down(lanes):
            gdn_scr[:, lanes] += dot_tn(dy_scr[low:high, :], g_scr[low:high, lanes])

        def out():
            gout_scr[...] += dot_tn(att_ref[0, low:high, :], dz_scr[low:high, :])

        steps = []
        for part in range(4):
            lanes = slice(part * D, (part + 1) * D)
            steps += [functools.partial(up, lanes), functools.partial(down, lanes)]
        return steps + [out]

    last = len(CHUNKS) - 1
    beside(enter(0) + expand(0))
    for chunk in range(last + 1):
        matrix = []
        if chunk < last:
            matrix += enter(chunk + 1) + expand(chunk + 1)
        if chunk > 0:
            matrix += contract(chunk - 1) + weights(chunk - 1)
        beside(gelu(chunk), matrix)
    beside(contract(last) + weights(last))

    @pl.when(image == pl.num_programs(0) - 1)
    def _():
        turn_scr[...] = gdn_scr[...].T
        for owner in range(D // shard):
            for part in range(FF // D):
                low = (owner * (FF // D) + part) * shard
                pack_scr[owner * shard : (owner + 1) * shard, part * D : (part + 1) * D] = turn_scr[
                    low : low + shard, :
                ]
        pack_ref[:, :D] = gout_scr[...].astype(BF)
        pack_ref[:, D : D + FF] = gup_scr[...].astype(BF)
        pack_ref[:, D + FF :] = pack_scr[...].astype(BF)


def small_spans(shard, narrow):
    count = D // shard
    own = shard * narrow
    rows = max((own * (i + 1) - 1) // HALF - own * i // HALF + 1 for i in range(count))
    return [(own * i // HALF, rows) for i in range(count)]


def back_kernel(
    spans,
    datt_ref,
    win_ref,
    e_ref,
    il_ref,
    o_ref,
    hat_ref,
    w_ref,
    s_ref,
    k_ref,
    feed_ref,
    bup_ref,
    tap_ref,
    edge_ref,
    dqkv_ref,
    pack_ref,
    g_scr,
    kern_scr,
    bias_scr,
    datt_scr,
    turn_scr,
    pad_scr,
    back_scr,
    dqkv_scr,
    small_scr,
    pack_scr,
):
    image = pl.program_id(0)

    @pl.when(image == 0)
    def _():
        for ref in (g_scr, kern_scr, bias_scr, turn_scr, pad_scr, small_scr, pack_scr):
            ref[...] = jnp.zeros_like(ref)
        datt_scr[ROWS:, :] = jnp.zeros((LONG - ROWS, D), F32)
        dqkv_scr[TOK_IMG:, :] = jnp.zeros((ROWS - TOK_IMG, 3 * D), F32)

    for low, high in CHUNKS:
        datt_scr[low:high, :] = datt_ref[0, low:high, :].astype(F32)
    minus = -head_block(WIN)
    none = jnp.zeros((WIN - QROWS, HALF), BF)

    def weigh(pair, _):
        state = []
        for member in range(2):
            at = 2 * pair + member
            branch = branch_of(pair, member)
            lanes = slice(branch * HALF, (branch + 1) * HALF)
            if kind_of(pair) == 1:
                for source, target in pieces_of(pair, member):
                    turn_scr[at - 4, target : target + STRIPE, :] = datt_scr[
                        source : source + STRIPE, lanes
                    ]
                grad = turn_scr[at - 4]
            else:
                low = first_of(pair, member)
                grad = first_rows(datt_scr[low : low + QROWS, lanes], tokens_of(pair))
            v = win_ref[0, at, :, 2 * HALF :]
            pad_scr[at, EDGE : EDGE + QROWS, :] = first_rows(v.astype(F32), tokens_of(pair))
            dn = grad * il_ref[0, at]
            z = (dn * o_ref[0, at].astype(F32)).astype(BF)
            dn = dn.astype(BF)
            left = jnp.concatenate([dn, z], axis=1)
            v = jnp.concatenate([v, none], axis=0)
            right = jnp.concatenate([by_head(v), minus], axis=1)
            state.append((grad, dn, dot_nt(left, right)))
        return state

    def score(pair, state):
        new = []
        for member, (grad, dn, weighed) in enumerate(state):
            e = e_ref[0, 2 * pair + member]
            ds = (weighed * e.astype(F32)).astype(BF)
            new.append((grad, dn, ds, e))
        return new

    def spread(pair, state):
        kind = kind_of(pair)
        taps, dvs = [], []
        for member, (grad, dn, ds, e) in enumerate(state):
            at = 2 * pair + member
            branch = branch_of(pair, member)
            kernel = k_ref[branch].astype(BF)
            q = win_ref[0, at, :, 0:HALF]
            k = jnp.concatenate([win_ref[0, at, :, HALF : 2 * HALF], none], axis=0)
            dq = dot(ds, by_head(k)) * SCALE
            q_t, dn_t = q.T, dn.T
            dk, dv = [], []
            for h in range(HEADS):
                lanes = slice(h * WIN, (h + 1) * WIN)
                own = slice(h * HEAD, (h + 1) * HEAD)
                dk.append(dot(q_t[own], ds[:, lanes]))
                dv.append(dot(dn_t[own], e[:, lanes]))
            dk = jnp.concatenate(dk, axis=0).T[:QROWS] * LN2
            dvs.append((dq, dk, jnp.concatenate(dv, axis=0).T[:QROWS]))
            low = jnp.concatenate([grad.astype(BF), none], axis=0)
            taps.append(
                jnp.concatenate([low * kernel[8 - tap : 9 - tap] for tap in range(9)], axis=0)
            )
            broad = shape_of(kind)[1]
            sides = {0: grad}
            if kind < 2:
                for dx in (-1, 1):
                    sides[dx] = grad * edge_ref[kind, 4 + dx]
            for tap, (dy, dx) in enumerate(TAPS):
                if kind < 2 or tap == 4:
                    side = sides[dx]
                else:
                    side = grad * edge_ref[kind, tap]
                start = EDGE + dy * broad + dx
                kern_scr[branch, tap] += fold(side * pad_scr[at, start : start + QROWS, :])
        conv = dot(tap_ref[kind], jnp.concatenate(taps, axis=1))
        for member in range(2):
            at = 2 * pair + member
            branch = branch_of(pair, member)
            dq, dk, dv = dvs[member]
            dv = dv + conv[:, member * HALF : (member + 1) * HALF]
            for part, piece in enumerate((dq, dk, dv)):
                lanes = slice(part * D + branch * HALF, part * D + (branch + 1) * HALF)
                if kind == 1:
                    back_scr[at - 4, part] = piece
                    for source, target in pieces_of(pair, member):
                        dqkv_scr[source : source + STRIPE, lanes] = back_scr[
                            at - 4, part, target : target + STRIPE, :
                        ]
                else:
                    low, count = first_of(pair, member), tokens_of(pair)
                    dqkv_scr[low : low + count, lanes] = piece[:count]

    pipelined((weigh, score, spread), ORDER)
    for low, high in CHUNKS:
        value = dqkv_scr[low:high, :]
        bias_scr[...] += fold(value)
        dqkv_ref[0, low:high, :] = value.astype(BF)
    g_scr[...] += dot_tn(hat_ref[0], dqkv_ref[0])

    @pl.when(image == pl.num_programs(0) - 1)
    def _():
        wide = w_ref[...].astype(F32)
        exact = functools.partial(
            lax.dot_general,
            dimension_numbers=(((1,), (1,)), ((), ())),
            precision=lax.Precision.HIGHEST,
            preferred_element_type=F32,
        )

        def put(row, terms):
            for at in range(0, terms.shape[1], HALF):
                small_scr[row : row + 1, :] = terms[:, at : at + HALF]
                row += 1

        total = lambda terms: jnp.sum(terms, axis=0, keepdims=True)
        bias = total(bias_scr[...])
        put(0, total(exact(jnp.ones((8, 3 * D), F32), wide * g_scr[...])) * 0.125)
        put(2, total(exact(bias_scr[...], wide)))
        put(4, bias)
        for tap in range(9):
            for branch in range(2):
                put(10 + 2 * tap + branch, total(kern_scr[branch, tap]))
        for row, entry in ((28, 4), (30, 3), (32, 1), (34, 2), (44, 0)):
            put(row, total(feed_ref[entry]))
        put(36, total(bup_ref[...]))
        for owner, (row, rows) in enumerate(spans):
            shard = D // len(spans)
            pack_scr[owner * shard : owner * shard + rows, :] = small_scr[row : row + rows, :]
        columns = s_ref[0:8, :].T
        grad = columns[:, 0:1] * g_scr[...] + columns[:, 1:2] * bias
        pack_ref[:, : 3 * D] = grad.astype(BF)
        pack_ref[:, 3 * D :] = pack_scr[...].astype(BF)


def input_kernel(x_ref, dqkv_ref, dx_ref, w_ref, s_ref, out_ref):
    for low, high in CHUNKS:
        dh = dot_nt(dqkv_ref[0, low:high, :], w_ref[...])
        hat, scale = normalise(rows_of(x_ref, low, high))
        grad = rows_of(dx_ref, low, high) + norm_back(dh * s_ref[0:1, :], hat, scale)
        store_rows(out_ref, low, high, grad)


def whole(shape):
    return pl.BlockSpec(shape, lambda i, *_: (0,) * len(shape))


def image_of(shape):
    return pl.BlockSpec((1,) + shape, lambda i, *_: (i,) + (0,) * len(shape))


def tokens():
    return pl.BlockSpec((TOK_IMG, D), lambda i, *_: (i, 0))


def params():
    return pltpu.CompilerParams(
        vmem_limit_bytes=VMEM, dimension_semantics=("arbitrary",)
    )


def sds(shape, dtype):
    return jax.ShapeDtypeStruct(shape, dtype)


def small_tables(small):
    rows = small.reshape(-1, D)
    taps = rows[5:15].reshape(10, 2, HALF).transpose(1, 0, 2)
    return jnp.pad(rows, ((0, 1), (0, 0))), jnp.pad(taps, ((0, 0), (0, 6), (0, 0)))


def run_attend(tokens_in, w_qkv, table, kernels, side):
    images = tokens_in.shape[0] // TOK_IMG
    mrow, mkey = mask_operands()
    consts = [table, kernels, side, bf(mrow), bf(mkey)]
    outs = [
        ((ROWS, D), BF),
        ((ROWS, D), BF),
        ((2 * PAIRS, QROWS, 3 * HALF), BF),
        ((2 * PAIRS, QROWS, HEADS * WIN), BF),
        ((2 * PAIRS, QROWS, HALF), F32),
        ((2 * PAIRS, QROWS, HALF), BF),
    ]
    return pl.pallas_call(
        attend_kernel,
        grid=(images,),
        in_specs=[tokens(), whole(w_qkv.shape)] + [whole(c.shape) for c in consts],
        out_specs=[image_of(shape) for shape, _ in outs],
        out_shape=[sds((images,) + shape, dtype) for shape, dtype in outs],
        scratch_shapes=[
            pltpu.VMEM((2, LONG, 3 * HALF), F32),
            pltpu.VMEM((4, QROWS, 3 * HALF), F32),
            pltpu.VMEM((4, QROWS, HALF), F32),
            pltpu.VMEM((ROWS, D), F32),
        ],
        compiler_params=params(),
        name="attend",
    )(tokens_in, w_qkv, *consts)


def run_feed(shard, counts, tokens_in, cotangent, att, wide, down, table):
    images = tokens_in.shape[0] // TOK_IMG
    return pl.pallas_call(
        functools.partial(feed_kernel, shard),
        grid_spec=pltpu.PrefetchScalarGridSpec(
            num_scalar_prefetch=1,
            grid=(images,),
            in_specs=[
                tokens(),
                tokens(),
                image_of((ROWS, D)),
                whole(wide.shape),
                whole(down.shape),
                whole(table.shape),
            ],
            out_specs=[
                tokens(),
                tokens(),
                image_of((ROWS, D)),
                whole((D, D + 2 * FF)),
                whole((5, 8, D)),
                whole((8, FF)),
            ],
            scratch_shapes=[
                pltpu.VMEM((ROWS, D), BF),
                pltpu.VMEM((ROWS, FF), F32),
                pltpu.VMEM((ROWS, FF), F32),
                pltpu.VMEM((ROWS, FF), BF),
                pltpu.VMEM((ROWS, FF), BF),
                pltpu.VMEM((ROWS, D), BF),
                pltpu.VMEM((ROWS, D), BF),
                pltpu.VMEM((ROWS, D), F32),
                pltpu.VMEM((ROWS, D), F32),
                pltpu.VMEM((ROWS, 1), F32),
                pltpu.VMEM((D, FF), F32),
                pltpu.VMEM((D, FF), F32),
                pltpu.VMEM((D, D), F32),
                pltpu.VMEM((FF, D), F32),
                pltpu.VMEM((D, FF), F32),
            ],
        ),
        out_shape=[
            sds(tokens_in.shape, F32),
            sds(tokens_in.shape, F32),
            sds((images, ROWS, D), BF),
            sds((D, D + 2 * FF), BF),
            sds((5, 8, D), F32),
            sds((8, FF), F32),
        ],
        compiler_params=params(),
        name="feed",
    )(counts, tokens_in, cotangent, att, wide, down, table)


def run_back(spans, blocks, w_qkv, table, kernels, sums, b_up, side):
    images = blocks[0].shape[0]
    consts = [w_qkv, table, kernels, sums, b_up, side, jnp.asarray(edge_masks())]
    return pl.pallas_call(
        functools.partial(back_kernel, spans),
        grid=(images,),
        in_specs=[image_of(b.shape[1:]) for b in blocks] + [whole(c.shape) for c in consts],
        out_specs=[image_of((ROWS, 3 * D)), whole((D, 3 * D + HALF))],
        out_shape=[sds((images, ROWS, 3 * D), BF), sds((D, 3 * D + HALF), BF)],
        scratch_shapes=[
            pltpu.VMEM((D, 3 * D), F32),
            pltpu.VMEM((2, 9, 8, HALF), F32),
            pltpu.VMEM((8, 3 * D), F32),
            pltpu.VMEM((LONG, D), F32),
            pltpu.VMEM((4, QROWS, HALF), F32),
            pltpu.VMEM((2 * PAIRS, QROWS + 2 * EDGE, HALF), F32),
            pltpu.VMEM((4, 3, QROWS, HALF), F32),
            pltpu.VMEM((ROWS, 3 * D), F32),
            pltpu.VMEM((56, HALF), F32),
            pltpu.VMEM((D, HALF), F32),
        ],
        compiler_params=params(),
        name="back",
    )(*blocks, *consts)


def run_input(tokens_in, dqkv, dx, w_qkv, table):
    return pl.pallas_call(
        input_kernel,
        grid=(dqkv.shape[0],),
        in_specs=[
            tokens(),
            image_of((ROWS, 3 * D)),
            tokens(),
            whole(w_qkv.shape),
            whole(table.shape),
        ],
        out_specs=tokens(),
        out_shape=sds(tokens_in.shape, F32),
        compiler_params=params(),
        name="input_grad",
    )(tokens_in, dqkv, dx, w_qkv, table)


def moments(grad, first, second):
    first_new = BETA_ONE * first + (1.0 - BETA_ONE) * grad
    second_new = BETA_TWO * second + (1.0 - BETA_TWO) * grad * grad
    direction = (
        first_new
        / (1.0 - BETA_ONE**STEP)
        / (jnp.sqrt(second_new / (1.0 - BETA_TWO**STEP)) + ADAM_EPS)
    )
    return (first_new, second_new, direction)


MATRICES = (slice(0, 3 * D), slice(3 * D, 4 * D), slice(4 * D, 4 * D + FF))


def lane_sums(values):
    column = jnp.sum(values * values, axis=0, keepdims=True)
    parts = [column[:, at : at + HALF] for at in range(0, column.shape[1], HALF)]
    return functools.reduce(jnp.add, parts)


def moment_kernel(
    gq_ref,
    gq_other_ref,
    gl_ref,
    gl_other_ref,
    ww_ref,
    wm_ref,
    wv_ref,
    dw_ref,
    dm_ref,
    dv_ref,
    wf_ref,
    ws_ref,
    wu_ref,
    df_ref,
    ds_ref,
    du_ref,
    sq_ref,
):
    for lanes, own, other in (
        (slice(0, 3 * D), gq_ref[:, : 3 * D], gq_other_ref[:, : 3 * D]),
        (slice(3 * D, 4 * D + FF), gl_ref[:, : D + FF], gl_other_ref[:, : D + FF]),
    ):
        first, second, way = moments(own + other, wm_ref[:, lanes], wv_ref[:, lanes])
        wf_ref[:, lanes] = first
        ws_ref[:, lanes] = second
        wu_ref[:, lanes] = way + DECAY * ww_ref[:, lanes]
    count = ww_ref.shape[0]
    for part in range(FF // D):
        lanes = slice(D + FF + part * D, D + FF + (part + 1) * D)
        own = slice(part * count, (part + 1) * count)
        grad = gl_ref[:, lanes] + gl_other_ref[:, lanes]
        first, second, way = moments(grad, dm_ref[own, :], dv_ref[own, :])
        df_ref[own, :] = first
        ds_ref[own, :] = second
        du_ref[own, :] = way + DECAY * dw_ref[own, :]
    for base, wide, down in ((0, ww_ref, dw_ref), (4, wu_ref, du_ref)):
        for at, lanes in enumerate(MATRICES):
            sq_ref[base + at : base + at + 1, :] = lane_sums(wide[:, lanes])
        sq_ref[base + 3 : base + 4, :] = lane_sums(down[...])


def update_kernel(
    sq_ref,
    ww_ref,
    wu_ref,
    we_ref,
    dw_ref,
    du_ref,
    de_ref,
    wn_ref,
    wa_ref,
    dn_ref,
    da_ref,
    norm_ref,
):
    total = jnp.sum(sq_ref[...], axis=1, keepdims=True)
    norm = jnp.sqrt(total)
    norm_ref[...] = jnp.broadcast_to(norm, norm_ref.shape)
    ratio = norm[0:4] / norm[4:8]
    keep = min(EMA_CEILING, (1.0 + STEP) / (10.0 + STEP))
    for at, lanes in enumerate(MATRICES):
        new = ww_ref[:, lanes] - (RATE * ratio[at : at + 1]) * wu_ref[:, lanes]
        wn_ref[:, lanes] = new
        wa_ref[:, lanes] = keep * we_ref[:, lanes] + (1.0 - keep) * new
    new = dw_ref[...] - (RATE * ratio[3:4]) * du_ref[...]
    dn_ref[...] = new
    da_ref[...] = keep * de_ref[...] + (1.0 - keep) * new


def plain(kernel, name, out_shape, *operands):
    return pl.pallas_call(kernel, out_shape=out_shape, compiler_params=pltpu.CompilerParams(
        vmem_limit_bytes=VMEM), name=name)(*operands)


def to_other(values):
    return lax.ppermute(values, "dp", [(0, 1), (1, 0)])


def side_by_side(wide, down):
    rows = wide.shape[0]
    blocks = [down[at : at + rows] for at in range(0, down.shape[0], rows)]
    return jnp.concatenate([wide] + blocks, axis=1)


def gather(values, count):
    copies = jnp.broadcast_to(values[None], (count,) + values.shape)
    return lax.all_to_all(copies, "fsdp", 0, 0).reshape(-1, values.shape[1])


def send_terms(values, count):
    return lax.all_to_all(values.reshape(count, -1, values.shape[1]), "fsdp", 0, 0)


def add_terms(terms):
    return jnp.sum(terms.astype(F32), axis=0)


def add_all(values, count):
    step = 1
    while step < count:
        values = values + lax.ppermute(values, "fsdp", [(i, i ^ step) for i in range(count)])
        step *= 2
    return values


def on_device(
    count,
    tokens_in,
    cotangent,
    crop_count,
    wide_w,
    wide_m,
    wide_v,
    wide_ema,
    down_w,
    down_m,
    down_v,
    down_ema,
    small_p,
    small_m,
    small_v,
    small_ema,
):
    rows = wide_w.shape[0]
    narrow = small_p.shape[0] // rows
    wide_low = wide_w.astype(BF)
    small_low = jnp.pad(small_p.astype(BF).reshape(rows, narrow), ((0, 0), (0, HALF - narrow)))
    first = jnp.concatenate([wide_low[:, : 3 * D], small_low], axis=1)
    first = gather(first, count)
    late_all = gather(side_by_side(wide_low[:, 3 * D :], down_w.astype(BF)), count)
    down_all = late_all[:, D + FF :].reshape(count, rows, FF // D, D)
    down_all = down_all.transpose(0, 2, 1, 3).reshape(FF, D)
    w_qkv = first[:, : 3 * D]
    table, kernels = small_tables(first[:, 3 * D : 3 * D + narrow].astype(F32).reshape(-1))
    side = np.stack([tap_matrix(kind) for kind in range(3)])
    side = bf(side.transpose(0, 2, 1, 3).reshape(3, QROWS, 9 * WIN))
    hat, att, win, e, il, o = run_attend(tokens_in, w_qkv, table, kernels, side)
    block_out, dx, datt, g_late, sums, b_up = run_feed(
        rows, crop_count, tokens_in, cotangent, att, late_all, down_all, table
    )
    late = send_terms(g_late, count)
    spans = small_spans(rows, narrow)
    dqkv, g_last = run_back(
        spans, [datt, win, e, il, o, hat], w_qkv, table, kernels, sums, b_up, side
    )
    late, g_last = lax.optimization_barrier((late, g_last))
    late = add_terms(late)
    last = send_terms(g_last, count)
    grad_in = run_input(tokens_in, dqkv, dx, w_qkv, table)
    last, grad_in = lax.optimization_barrier((last, grad_in))
    last = add_terms(last)
    last_other = to_other(last)
    late_other = to_other(late)
    wide_like, down_like = sds(wide_w.shape, F32), sds(down_w.shape, F32)
    wide_first, wide_second, wide_upd, down_first, down_second, down_upd, squares = plain(
        moment_kernel,
        "moment",
        [wide_like] * 3 + [down_like] * 3 + [sds((8, HALF), F32)],
        *(last, last_other, late, late_other),
        *(wide_w, wide_m, wide_v, down_w, down_m, down_v),
    )
    squares = add_all(squares, count)
    wide_new, wide_avg, down_new, down_avg, norms = plain(
        update_kernel,
        "update",
        [wide_like] * 2 + [down_like] * 2 + [sds((8, HALF), F32)],
        *(squares, wide_w, wide_upd, wide_ema, down_w, down_upd, down_ema),
    )
    shard_small = (last + last_other)[: spans[0][1], 3 * D :].reshape(-1)
    offset = lax.axis_index("fsdp") * (rows * narrow) % HALF
    shard_small = lax.dynamic_slice(shard_small, (offset,), (rows * narrow,))
    small_first, small_second, small_dir = moments(shard_small, small_m, small_v)
    small_new = small_p - RATE * small_dir
    ema_keep = min(EMA_CEILING, (1.0 + STEP) / (10.0 + STEP))
    small_avg = ema_keep * small_ema + (1.0 - ema_keep) * small_new
    return (
        block_out,
        grad_in,
        wide_new,
        wide_first,
        wide_second,
        wide_avg,
        down_new,
        down_first,
        down_second,
        down_avg,
        small_new,
        small_first,
        small_second,
        small_avg,
        norms[:, 0].reshape(2, 4),
    )


def solution(mesh):
    tok, row, vec = P(("dp", "fsdp"), None), P("fsdp", None), P("fsdp")
    in_specs = (tok, tok, P(("dp", "fsdp"))) + (row,) * 8 + (vec,) * 4
    out_specs = (tok, tok) + (row,) * 8 + (vec,) * 4 + (P(),)
    return jax.shard_map(
        functools.partial(on_device, mesh.shape["fsdp"]),
        mesh=mesh,
        in_specs=in_specs,
        out_specs=out_specs,
        check_vma=False,
    )
```

time: 296 us -> 192 us (0.65)
  Pallas kernels: 203 us -> 122 us
  waiting for transfers between devices: 36.9 us -> 19.4 us
  other arithmetic: 12 us -> 5.37 us
  starting transfers between devices: 29.3 us -> 35.2 us
  local copies, waits for them, and re-layouts: 12.5 us -> 8.13 us
    pallas_call x2 -> x3, Pallas kernels: 137 us -> 89.7 us  [the longest x1 39.2 us: run_back(): pl.pallas_call(functools.partial(back_kernel, spans), grid=(images,), in_...]
    pallas_call x1, Pallas kernels: 61.5 us -> 28.4 us  [run_attend(): pl.pallas_call(attend_kernel, grid=(images,), in_specs=[tokens(), whole(w...]
    all_to_all x2, waiting for transfers between devices: 11.8 us -> 0.01 us  [send_terms(): lax.all_to_all(values.reshape(count, -1, values.shape[1]), 'fsdp', 0, 0)]
    ppermute x4, starting transfers between devices: 3.32 us -> 8.63 us  [add_all(): lax.ppermute(values, 'fsdp', [(i, i ^ step) for i in range(count)])]
    ppermute x4, waiting for transfers between devices: 10.8 us -> 5.54 us  [add_all(): lax.ppermute(values, 'fsdp', [(i, i ^ step) for i in range(count)])]
    concatenate x3 -> x0, other arithmetic: 3 us -> none  [the longest x1 2.19 us: on_device(): late = scatter_sum(jnp.concatenate([g_late, g_down], axis=1), count)]
  transfers between devices with their start and end apart: 10 -> 10, of which waited for: 7 -> 7; matrix products, arithmetic and copies ran while one was open for 4% -> 2% of each run, Pallas kernels for 47% -> 42%
where the time goes in v3:
time: 192 us; the launch traced here: 191 us
  Pallas kernels  122 us (64%)
  starting transfers between devices  35.2 us (18%)
  waiting for transfers between devices  19.4 us (10%)
  local copies, waits for them, and re-layouts  8.13 us (4%)
  other arithmetic  5.37 us (3%)
    pallas_call x1, Pallas kernels, run_back(): pl.pallas_call(functools.partial(back_kernel, spans), grid=(images,), in_...  39.2 us
    pallas_call x1, Pallas kernels, run_feed(): pl.pallas_call(functools.partial(feed_kernel, shard), grid_spec=pltpu.Pre...  37.6 us
    pallas_call x1, Pallas kernels, run_attend(): pl.pallas_call(attend_kernel, grid=(images,), in_specs=[tokens(), whole(w...  28.4 us
    all_to_all x2, starting transfers between devices, send_terms(): lax.all_to_all(values.reshape(count, -1, values.shape[1]), 'fsdp', 0, 0)  13.8 us
    all_to_all x2, waiting for transfers between devices, gather(): return lax.all_to_all(copies, 'fsdp', 0, 0).reshape(-1, values.shape[1])  13 us
    pallas_call x1, Pallas kernels, run_input(): pl.pallas_call(input_kernel, grid=(dqkv.shape[0],), in_specs=[tokens(), i...  12.9 us
    all_to_all x2, starting transfers between devices, gather(): return lax.all_to_all(copies, 'fsdp', 0, 0).reshape(-1, values.shape[1])  12.1 us
    ppermute x4, starting transfers between devices, add_all(): lax.ppermute(values, 'fsdp', [(i, i ^ step) for i in range(count)])  8.63 us
  transfers between devices with their start and end apart: 10, of which 7 were waited for; matrix products, arithmetic and copies ran while one was open for 2% of the time, Pallas kernels for 42%

profile of v3, /device:TPU:0, one launch (start us, length us, event | category | flops | bytes accessed | tf_op | source)
XLA Modules:
  0.0 191.1 jit_solution(13197420673615081156)
XLA Ops:
  0.6 0.9 convert_element_type.22
  1.6 0.7 convert_element_type.23
  2.3 0.1 reshape.59
  2.4 0.8 broadcast_in_dim.4
  3.2 8.3 %all-to-all-start = ((bf16[16,16,896]{2,1,0:T(8,128)(2,1)}), bf16[16,16,896]{2,1,0:T(8,128)(2,1)S(1)}, u32[]{:S(2)}, u32[]{:S(2)}) async-start(bf16[16,16,896]{2,1,0:T(8,128)(2,1)} %broadcast_in_dim.4), calls=%async_computation | async-start | bytes 917504 | tf_op jit(solution)/shard_map/all_to_all | solution.py:958
  11.5 0.8 convert_element_type.24
  12.4 13.0 %all-to-all-done = bf16[16,16,896]{2,1,0:T(8,128)(2,1)S(1)} async-done(((bf16[16,16,896]{2,1,0:T(8,128)(2,1)}), bf16[16,16,896]{2,1,0:T(8,128)(2,1)S(1)}, u32[]{:S(2)}, u32[]{:S(2)}) %all-to-all-start) | async-done | bytes 458784 | tf_op jit(solution)/shard_map/all_to_all | solution.py:958
  25.4 1.1 broadcast_in_dim.5
  26.4 3.8 %all-to-all-start.1 = ((bf16[16,16,2304]{2,1,0:T(8,128)(2,1)}), bf16[16,16,2304]{2,1,0:T(8,128)(2,1)S(1)}, u32[]{:S(2)}, u32[]{:S(2)}) async-start(bf16[16,16,2304]{2,1,0:T(8,128)(2,1)} %broadcast_in_dim.5), calls=%async_computation.1 | async-start | bytes 2359296 | tf_op jit(solution)/shard_map/all_to_all | solution.py:958
  30.2 0.8 slice.49.w_ref
  31.0 0.2 reshape.68
  31.2 0.6 pad.13.s_ref
  31.9 0.6 pad.14.k_ref
  32.5 28.4 %attend.1 = (bf16[8,688,256]{2,1,0:T(8,128)(2,1)}, bf16[8,688,256]{2,1,0:T(8,128)(2,1)}, bf16[8,14,112,384]{3,2,1,0:T(8,128)(2,1)}, bf16[8,14,112,512]{3,2,1,0:T...) custom-call(f32[5440,256]{1,0:T(8,128)} %x_ref.5, bf16[256,768]{1,0:T(8,128)(2,1)} %slice.49.w_ref, ...), custom_call_target="tpu_custom_call" | custom-call | tf_op jit(solution)/shard_map/attend/pallas_call | solution.py:736
  60.9 0.0 all-to-all-done.1
  60.9 0.0 copy-start
  61.0 0.1 slice.57
  61.0 0.4 reshape.63
  61.4 0.9 copy.38
  62.3 0.0 copy-done
  62.3 37.6 %feed.1 = (f32[5440,256]{1,0:T(8,128)}, f32[5440,256]{1,0:T(8,128)}, bf16[8,688,256]{2,1,0:T(8,128)(2,1)}, bf16[256,2304]{1,0:T(8,128)(2,1)}, f32[5,8,256]{2,1,0:T(8,128)}, /*index=5*/f32[8,1024]{1,0:T(8,128)}) custom-call(s32[8]{0:T(128)} %cnt_ref.1, f32[5440,256]{1,0:T(8,128)} %x_ref.5, f32[5440,256]{1,0:T(8,128)} %c_ref.1, ...), custom_call_target="tpu_custom_call" | custom-call | tf_op jit(solution)/shard_map/feed/pallas_call | solution.py:755
  99.9 6.9 %all-to-all-start.2 = ((bf16[16,16,2304]{2,1,0:T(8,128)(2,1)}), bf16[16,16,2304]{2,1,0:T(8,128)(2,1)S(1)}, u32[]{:S(2)}, u32[]{:S(2)}) async-start(bf16[16,16,2304]{2,1,0:T(8,128)(2,1)} %bitcast.17), calls=%async_computation.2 | async-start | bytes 2359296 | tf_op jit(solution)/shard_map/all_to_all | solution.py:962
  106.8 39.2 %back.1 = (bf16[8,688,768]{2,1,0:T(8,128)(2,1)}, bf16[256,896]{1,0:T(8,128)(2,1)}) custom-call(bf16[8,688,256]{2,1,0:T(8,128)(2,1)} %get-tuple-element.48.datt_ref, bf16[8,14,112,384]{3,2,1,0:T(8,128)(2,1)} %get-tuple-element.49.win_ref, bf16[8,14,112,512]{3,2,1,0:T(8,128)(2,1)} %get-tuple-element.50.e_ref, f32[8,14,112,128]{3,2,1,0:T(8,128)} %get-tuple-element.51.il_ref, ...), custom_call_target="tpu_custom_call" | custom-call | tf_op jit(solution)/shard_map/back/pallas_call | solution.py:810
  146.0 0.0 all-to-all-done.2
  146.0 6.9 %all-to-all-start.3 = ((bf16[16,16,896]{2,1,0:T(8,128)(2,1)}), bf16[16,16,896]{2,1,0:T(8,128)(2,1)S(1)}, u32[]{:S(2)}, u32[]{:S(2)}) async-start(bf16[16,16,896]{2,1,0:T(8,128)(2,1)} %bitcast.18), calls=%async_computation.3 | async-start | bytes 917504 | tf_op jit(solution)/shard_map/all_to_all | solution.py:962
  152.9 0.0 copy-start.5
  152.9 0.0 copy-start.6
  153.0 0.0 copy-start.7
  153.0 0.0 copy-start.8
  153.0 12.9 %input_grad.1 = f32[5440,256]{1,0:T(8,128)} custom-call(f32[5440,256]{1,0:T(8,128)} %x_ref.5, bf16[8,688,768]{2,1,0:T(8,128)(2,1)} %get-tuple-element.58.dqkv_ref, f32[5440,256]{1,0:T(8,128)} %get-tuple-element.59.dx_ref, bf16[256,768]{1,0:T(8,128)(2,1)} %slice.49.w_ref, f32[24,256]{1,0:T(8,128)} %pad.13.s_ref), custom_call_target="tpu_custom_call" | custom-call | tf_op jit(solution)/shard_map/input_grad/pallas_call | solution.py:834
  165.9 0.2 convert_reduce_fusion.gl_ref
  166.1 0.0 copy-start.1
  166.1 0.1 collective-permute-start.1
  166.1 0.0 all-to-all-done.3
  166.2 0.1 convert_reduce_fusion.1.gq_ref
  166.2 0.0 copy-start.2
  166.2 0.6 collective-permute-start
  166.8 0.7 collective-permute-done.1.gl_other_ref
  167.5 0.0 copy-start.3
  167.5 0.2 collective-permute-done.gq_other_ref
  167.7 0.0 copy-done.1
  167.7 0.0 copy-done.2
  167.7 0.5 copy-done.3
  168.2 0.6 copy-done.4
  168.8 2.1 %moment.1 = (f32[16,2048]{1,0:T(8,128)}, f32[16,2048]{1,0:T(8,128)}, f32[16,2048]{1,0:T(8,128)}, f32[64,256]{1,0:T(8,128)}, f32[64,256]{1,0:T(8,128)}, /*index=5*/f32[64,256]{1,0:T(8,128)}, f32[8,128]{1,0:T(8,128)}) custom-call(f32[16,896]{1,0:T(8,128)} %copy-done.2, f32[16,896]{1,0:T(8,128)} %copy-done.4, f32[16,2304]{1,0:T(8,128)} %copy-done.1, ...), custom_call_target="tpu_custom_call" | custom-call | tf_op jit(solution)/shard_map/moment/pallas_call | solution.py:942
  170.9 2.0 %collective-permute-start.2 = (f32[8,128]{1,0:T(8,128)}, f32[8,128]{1,0:T(8,128)S(1)}, u32[]{:S(2)}, u32[]{:S(2)}) collective-permute-start(f32[8,128]{1,0:T(8,128)} %get-tuple-element.63), channel_id=1, source_target_pairs={{0,1},{1,0},{2,3},{3,2},{4,5},{5,4},{6,7},{7,6},{8,9},{9,8},{10,11... | collective-permute-start | bytes 12296 | tf_op jit(solution)/shard_map/ppermute | solution.py:972
  172.8 1.9 collective-permute-done.2
  174.7 0.7 add.43
  175.4 1.9 %collective-permute-start.3 = (f32[8,128]{1,0:T(8,128)S(1)}, f32[8,128]{1,0:T(8,128)S(1)}, u32[]{:S(2)}, u32[]{:S(2)}) collective-permute-start(f32[8,128]{1,0:T(8,128)S(1)} %add.43), channel_id=1, source_target_pairs={{0,2},{1,3},{2,0},{3,1},{4,6},{5,7},{6,4},{7,5},{8,10},{9,11},{10,... | collective-permute-start | bytes 12296 | tf_op jit(solution)/shard_map/ppermute | solution.py:972
  177.3 1.7 collective-permute-done.3
  179.0 1.9 %collective-permute-start.4 = (f32[8,128]{1,0:T(8,128)S(1)}, f32[8,128]{1,0:T(8,128)S(1)}, u32[]{:S(2)}, u32[]{:S(2)}) collective-permute-start(f32[8,128]{1,0:T(8,128)S(1)} %add.44), channel_id=1, source_target_pairs={{0,4},{1,5},{2,6},{3,7},{4,0},{5,1},{6,2},{7,3},{8,12},{9,13},{10,... | collective-permute-start | bytes 12296 | tf_op jit(solution)/shard_map/ppermute | solution.py:972
  180.9 0.7 fusion.3
  181.7 1.0 collective-permute-done.4
  182.6 2.8 %collective-permute-start.5 = (f32[8,128]{1,0:T(8,128)S(1)}, f32[8,128]{1,0:T(8,128)S(1)}, u32[]{:S(2)}, u32[]{:S(2)}) collective-permute-start(f32[8,128]{1,0:T(8,128)S(1)} %add.45), channel_id=1, source_target_pairs={{0,8},{1,9},{2,10},{3,11},{4,12},{5,13},{6,14},{7,15},{8,0},{9,1},... | collective-permute-start | bytes 12296 | tf_op jit(solution)/shard_map/ppermute | solution.py:972
  185.5 0.0 copy-done.5
  185.5 0.0 copy-done.6
  185.5 0.0 copy-done.7
  185.5 0.0 copy-done.8
  185.5 0.7 multiply_add_fusion
  186.2 1.0 collective-permute-done.5
  187.1 0.6 add.46.sq_ref
  187.7 2.0 %update.1 = (f32[16,2048]{1,0:T(8,128)}, f32[16,2048]{1,0:T(8,128)}, f32[64,256]{1,0:T(8,128)}, f32[64,256]{1,0:T(8,128)}, f32[8,128]{1,0:T(8,128)}) custom-call(f32[8,128]{1,0:T(8,128)} %add.46.sq_ref, f32[16,2048]{1,0:T(8,128)} %ww_ref.3, f32[16,2048]{1,0:T(8,128)} %get-tuple-element.64.wu_ref, f32[16,2048]{1,0:T(8,128)} %we_ref.1, f32[64,256]{1,0:T(8,128)} %dw_ref.3, ...), custom_call_target="tpu_custom_call" | custom-call | tf_op jit(solution)/shard_map/update/pallas_call | solution.py:942
  189.7 0.8 slice_reduce_fusion
  190.5 0.6 reshape_squeeze.3
  (14 shorter events, 0.1 us)
Async XLA Ops:
  3.2 22.2 %all-to-all-start = ((bf16[16,16,896]{2,1,0:T(8,128)(2,1)}), bf16[16,16,896]{2,1,0:T(8,128)(2,1)S(1)}, u32[]{:S(2)}, u32[]{:S(2)}) async-start(bf16[16,16,896]{2,1,0:T(8,128)(2,1)} %broadcast_in_dim.4), calls=%async_computation | async-start | bytes 917504 | tf_op jit(solution)/shard_map/all_to_all | solution.py:958
  26.4 34.5 %all-to-all-start.1 = ((bf16[16,16,2304]{2,1,0:T(8,128)(2,1)}), bf16[16,16,2304]{2,1,0:T(8,128)(2,1)S(1)}, u32[]{:S(2)}, u32[]{:S(2)}) async-start(bf16[16,16,2304]{2,1,0:T(8,128)(2,1)} %broadcast_in_dim.5), calls=%async_computation.1 | async-start | bytes 2359296 | tf_op jit(solution)/shard_map/all_to_all | solution.py:958
  60.9 1.3 copy-start
  99.9 46.1 %all-to-all-start.2 = ((bf16[16,16,2304]{2,1,0:T(8,128)(2,1)}), bf16[16,16,2304]{2,1,0:T(8,128)(2,1)S(1)}, u32[]{:S(2)}, u32[]{:S(2)}) async-start(bf16[16,16,2304]{2,1,0:T(8,128)(2,1)} %bitcast.17), calls=%async_computation.2 | async-start | bytes 2359296 | tf_op jit(solution)/shard_map/all_to_all | solution.py:962
  146.0 20.1 %all-to-all-start.3 = ((bf16[16,16,896]{2,1,0:T(8,128)(2,1)}), bf16[16,16,896]{2,1,0:T(8,128)(2,1)S(1)}, u32[]{:S(2)}, u32[]{:S(2)}) async-start(bf16[16,16,896]{2,1,0:T(8,128)(2,1)} %bitcast.18), calls=%async_computation.3 | async-start | bytes 917504 | tf_op jit(solution)/shard_map/all_to_all | solution.py:962
  152.9 32.5 %copy-start.5 = (f32[368]{0:T(512)S(1)}, f32[368]{0:T(512)}, u32[]{:S(2)}) copy-start(f32[368]{0:T(512)} %param.30) | copy-start | bytes 4420
  152.9 32.5 %copy-start.6 = (f32[368]{0:T(512)S(1)}, f32[368]{0:T(512)}, u32[]{:S(2)}) copy-start(f32[368]{0:T(512)} %param.33) | copy-start | bytes 4420
  153.0 32.5 %copy-start.7 = (f32[368]{0:T(512)S(1)}, f32[368]{0:T(512)}, u32[]{:S(2)}) copy-start(f32[368]{0:T(512)} %param.31) | copy-start | bytes 4420
  153.0 32.5 %copy-start.8 = (f32[368]{0:T(512)S(1)}, f32[368]{0:T(512)}, u32[]{:S(2)}) copy-start(f32[368]{0:T(512)} %param.32) | copy-start | bytes 4420
  166.1 1.6 copy-start.1
  166.1 1.4 collective-permute-start.1
  166.2 1.5 copy-start.2
  166.2 1.4 collective-permute-start
  167.5 0.7 copy-start.3
  168.2 0.6 copy-start.4
  170.9 3.9 %collective-permute-start.2 = (f32[8,128]{1,0:T(8,128)}, f32[8,128]{1,0:T(8,128)S(1)}, u32[]{:S(2)}, u32[]{:S(2)}) collective-permute-start(f32[8,128]{1,0:T(8,128)} %get-tuple-element.63), channel_id=1, source_target_pairs={{0,1},{1,0},{2,3},{3,2},{4,5},{5,4},{6,7},{7,6},{8,9},{9,8},{10,11... | collective-permute-start | bytes 12296 | tf_op jit(solution)/shard_map/ppermute | solution.py:972
  175.4 3.6 %collective-permute-start.3 = (f32[8,128]{1,0:T(8,128)S(1)}, f32[8,128]{1,0:T(8,128)S(1)}, u32[]{:S(2)}, u32[]{:S(2)}) collective-permute-start(f32[8,128]{1,0:T(8,128)S(1)} %add.43), channel_id=1, source_target_pairs={{0,2},{1,3},{2,0},{3,1},{4,6},{5,7},{6,4},{7,5},{8,10},{9,11},{10,... | collective-permute-start | bytes 12296 | tf_op jit(solution)/shard_map/ppermute | solution.py:972
  179.0 3.6 %collective-permute-start.4 = (f32[8,128]{1,0:T(8,128)S(1)}, f32[8,128]{1,0:T(8,128)S(1)}, u32[]{:S(2)}, u32[]{:S(2)}) collective-permute-start(f32[8,128]{1,0:T(8,128)S(1)} %add.44), channel_id=1, source_target_pairs={{0,4},{1,5},{2,6},{3,7},{4,0},{5,1},{6,2},{7,3},{8,12},{9,13},{10,... | collective-permute-start | bytes 12296 | tf_op jit(solution)/shard_map/ppermute | solution.py:972
  182.6 4.5 %collective-permute-start.5 = (f32[8,128]{1,0:T(8,128)S(1)}, f32[8,128]{1,0:T(8,128)S(1)}, u32[]{:S(2)}, u32[]{:S(2)}) collective-permute-start(f32[8,128]{1,0:T(8,128)S(1)} %add.45), channel_id=1, source_target_pairs={{0,8},{1,9},{2,10},{3,11},{4,12},{5,13},{6,14},{7,15},{8,0},{9,1},... | collective-permute-start | bytes 12296 | tf_op jit(solution)/shard_map/ppermute | solution.py:972

commit v4 on v3

--- a/solution.py
+++ b/solution.py
@@ -36,6 +36,7 @@
 SCALE = HEAD**-0.5
 LOG2E = 1.4426950408889634
 LN2 = 0.6931471805599453
+ROOT = 2**-0.5
 CHUNKS = ((0, 240), (240, 464), (464, 688))
 LONG = 744
 EDGE = 16
@@ -73,24 +74,27 @@
 
 
 def edge_masks():
-    out = np.zeros((3, 9, QROWS, HALF), np.float32)
+    masks, places = [], {}
     for kind in range(3):
         high, broad = shape_of(kind)
         size = high * broad
-        for copy in range(1 if kind < 2 else COPIES[0]):
-            for at in range(size):
-                r, c = divmod(at, broad)
-                for tap, (dy, dx) in enumerate(TAPS):
-                    if 0 <= r + dy < high and 0 <= c + dx < broad:
-                        out[kind, tap, copy * size + at] = 1
-    return out
+        for dy, dx in TAPS:
+            if (dy, dx) == (0, 0) or (kind < 2 and (dy != 0 or dx == 0)):
+                continue
+            mask = np.zeros((QROWS, HALF), np.float32)
+            for at in range(size * (1 if kind < 2 else COPIES[0])):
+                r, c = divmod(at % size, broad)
+                mask[at] = 0 <= r + dy < high and 0 <= c + dx < broad
+            places[kind, dy, dx] = len(masks)
+            masks.append(mask)
+    return np.stack(masks), places
 
 
 def tap_matrix(kind):
     shape = shape_of(kind)
     copies = 1 if kind < 2 else COPIES[0]
     size = shape[0] * shape[1]
-    out = np.zeros((9, QROWS, WIN), np.float32)
+    out = np.zeros((9, QROWS, QROWS), np.float32)
     for copy in range(copies):
         for r in range(shape[0]):
             for c in range(shape[1]):
@@ -103,18 +107,19 @@
 
 def mask_operands():
     size = GRID_S * GRID_S
-    rows = np.zeros((3, QROWS, HALF), np.float32)
-    keys = np.zeros((3, WIN, HALF), np.float32)
-    rows[0, :, 0] = 1
-    keys[0, STRIPE * GRID_L :, 0] = -1e30
-    for kind, crops in ((1, 3), (2, 2)):
+    rows = np.zeros((3, 2, QROWS, HALF), np.float32)
+    keys = np.zeros((3, HALF // 2, WIN), np.float32)
+    for kind, crops in ((0, 1), (1, 3), (2, 2)):
+        count = STRIPE * GRID_L if kind == 0 else crops * size
+        each = count // crops
         for at in range(QROWS):
-            rows[kind, at, at // size if at < crops * size else 0] = 1
+            rows[kind, 0, at, HALF // 2 + (at // each if at < count else 0)] = 1
         for at in range(WIN):
             for crop in range(crops):
-                if at >= crops * size or at // size != crop:
-                    keys[kind, at, crop] = -1e30
-    return rows, np.tile(keys, (1, HEADS, 1))
+                if at >= count or at // each != crop:
+                    keys[kind, crop, at] = -1e30
+    rows[:, 1, :, : HALF // 2] = rows[:, 0, :, HALF // 2 :]
+    return rows, np.tile(keys, (1, 1, 2))
 
 
 def bf(array):
@@ -158,6 +163,10 @@
     ref[low:last, :] = values[: last - low]
 
 
+def with_ones(turned):
+    return jnp.concatenate([turned, jnp.ones((16, turned.shape[1]), turned.dtype)], axis=0)
+
+
 def fold(values):
     return jnp.sum(values.reshape(values.shape[0] // 8, 8, values.shape[1]), axis=0)
 
@@ -169,6 +178,30 @@
 
 def by_head(values):
     return jnp.concatenate([values * head_lanes(h) for h in range(HEADS)], axis=0)
+
+
+def lane_half(upper):
+    lanes = lax.broadcasted_iota(jnp.int32, (1, HALF), 1)
+    return jnp.where((lanes >= HALF // 2) == upper, 1.0, 0.0).astype(BF)
+
+
+def two_heads(turned, pair):
+    low = pair * 2 * HEAD
+    none = jnp.zeros((HEAD, WIN), turned.dtype)
+    first = jnp.concatenate([turned[low : low + HEAD], none], axis=1)
+    second = jnp.concatenate([none, turned[low + HEAD : low + 2 * HEAD]], axis=1)
+    return jnp.concatenate([first, second], axis=0)
+
+
+def by_two_heads(left, other, turned, added):
+    low, high = lane_half(False), lane_half(True)
+    first = dot(
+        left * low + other[0], jnp.concatenate([two_heads(turned, 0), added], axis=0)
+    )
+    second = dot(
+        left * high + other[1], jnp.concatenate([added, two_heads(turned, 1)], axis=0)
+    )
+    return [first[:, :WIN], first[:, WIN:], second[:, :WIN], second[:, WIN:]]
 
 
 def head_block(rows):
@@ -193,14 +226,22 @@
 
 def pipelined(stages, order, extra=()):
     extra = dict(extra)
-    state = {}
+    state = {item: {} for item in order}
     for turn in range(len(order) + len(stages) - 1):
         if turn in extra:
             extra[turn]()
+        running = []
         for at, stage in enumerate(stages):
-            item = turn - at
-            if 0 <= item < len(order):
-                state[order[item]] = stage(order[item], state.get(order[item]))
+            if 0 <= turn - at < len(order):
+                item = order[turn - at]
+                running.append(stage(item, state[item]))
+        while running:
+            running = [stage for stage in running if next(stage, True) is None]
+
+
+def norm_kernel(x_ref, hat_ref):
+    for low in range(0, x_ref.shape[0], TOK_IMG // 5):
+        hat_ref[low : low + TOK_IMG // 5, :] = normalise(x_ref[low : low + TOK_IMG // 5, :])[0]
 
 
 def attend_kernel(
@@ -234,7 +275,7 @@
 
     def project(chunk):
         low, high = CHUNKS[chunk]
-        hat, _ = normalise(rows_of(x_ref, low, high))
+        hat = rows_of(x_ref, low, high)
         hat_ref[0, low:high, :] = hat.astype(BF)
         a = (hat * gain + shift).astype(BF)
         for part in range(3):
@@ -247,9 +288,9 @@
                     :, branch * HALF : (branch + 1) * HALF
                 ]
 
-    def score(pair, _):
-        state = []
-        mask = max(pair - 4, 0) if pair < 4 else (1 if pair < 6 else 2)
+    none = jnp.zeros((WIN - QROWS, HALF), BF)
+
+    def cut(pair, state):
         for member in range(2):
             at = 2 * pair + member
             if kind_of(pair) == 1:
@@ -263,68 +304,75 @@
                 window = qkv_scr[branch_of(pair, member), low : low + QROWS, :]
             window = window.astype(BF)
             win_ref[0, at] = window
-            q, k, v = (window[:, part * HALF : (part + 1) * HALF] for part in range(3))
-            none = jnp.zeros((WIN - QROWS, HALF), BF)
-            k = jnp.concatenate([k, none], axis=0)
-            left = jnp.concatenate([q, mrow_ref[mask]], axis=1)
-            right = jnp.concatenate([by_head(k), mkey_ref[mask]], axis=1)
-            state.append((v, dot_nt(left, right)))
-        return state
+            state[member] = [window[:, part * HALF : (part + 1) * HALF] for part in range(3)]
+            yield
+
+    def score(pair, state):
+        mask = 0 if pair < 4 else 1 if pair < 6 else 2
+        for member in range(2):
+            q, k, v = state[member]
+            k = jnp.concatenate([k, none], axis=0).T
+            rows = mrow_ref[mask, 0], mrow_ref[mask, 1]
+            state[member] = v, by_two_heads(q, rows, k, mkey_ref[mask])
+            yield
 
     def soften(pair, state):
-        new = []
-        for member, (v, scores) in enumerate(state):
+        for member in range(2):
+            v, scores = state[member]
             exps = []
-            for h in range(HEADS):
-                part = scores[:, h * WIN : (h + 1) * WIN]
+            for part in scores:
                 peak = jnp.max(part, axis=-1, keepdims=True)
                 exps.append(jnp.exp2(part - peak).astype(BF))
             e = jnp.concatenate(exps, axis=1)
             e_ref[0, 2 * pair + member] = e
-            new.append((v, e))
-        return new
+            state[member] = v, e
+            yield
 
     def mix(pair, state):
-        taps, mixed = [], []
-        none = jnp.zeros((WIN - QROWS, HALF), BF)
-        for member, (v, e) in enumerate(state):
+        taps = []
+        for member in range(2):
+            v, e = state[member]
+            low = k_ref[branch_of(pair, member)].astype(BF)
+            keys = jnp.concatenate([v, none], axis=0)
+            state[member] = dot(e, jnp.concatenate([by_head(keys), ones], axis=1))
+            taps.append(jnp.concatenate([v * low[tap : tap + 1] for tap in range(9)], axis=0))
+            yield
+        state[2] = dot(tap_ref[kind_of(pair)], jnp.concatenate(taps, axis=1))
+        yield
+
+    def put(pair, state):
+        for member in range(2):
             at = 2 * pair + member
-            kernel = k_ref[branch_of(pair, member)]
-            v = jnp.concatenate([v, none], axis=0)
-            both = dot(e, jnp.concatenate([by_head(v), ones], axis=1))
+            branch = branch_of(pair, member)
+            lanes = slice(branch * HALF, (branch + 1) * HALF)
+            both = state[member]
             inv = 1.0 / both[:, HALF:]
             o = both[:, :HALF] * inv
             il_ref[0, at] = inv
             o_ref[0, at] = o.astype(BF)
-            mixed.append(o + kernel[9:10])
-            low = kernel.astype(BF)
-            taps.append(jnp.concatenate([v * low[tap : tap + 1] for tap in range(9)], axis=0))
-        conv = dot(tap_ref[kind_of(pair)], jnp.concatenate(taps, axis=1))
-        for member in range(2):
-            piece = mixed[member] + conv[:, member * HALF : (member + 1) * HALF]
-            branch = branch_of(pair, member)
-            lanes = slice(branch * HALF, (branch + 1) * HALF)
+            conv = state[2][:, member * HALF : (member + 1) * HALF]
+            piece = o + k_ref[branch, 9:10, :] + conv
             if kind_of(pair) == 1:
-                at = 2 * pair + member - 4
-                back_scr[at] = piece
+                back_scr[at - 4] = piece
                 for source, target in pieces_of(pair, member):
                     att_scr[source : source + STRIPE, lanes] = back_scr[
-                        at, target : target + STRIPE, :
+                        at - 4, target : target + STRIPE, :
                     ]
             else:
                 low, count = first_of(pair, member), tokens_of(pair)
                 att_scr[low : low + count, lanes] = piece[:count]
+            yield
 
     project(0)
     extra = {1: functools.partial(project, 1), 3: functools.partial(project, 2)}
-    pipelined((score, soften, mix), ORDER, extra)
+    pipelined((cut, score, soften, mix, put), ORDER, extra)
     att_ref[0] = att_scr[...].astype(BF)
 
 
-def gelu_parts(u):
-    phi = 0.5 * lax.erf(u * 2**-0.5) + 0.5
-    decay = jnp.exp2((-0.5 * LOG2E) * (u * u))
-    return phi, phi + (u * 0.3989422804014327) * decay
+def gelu_parts(v):
+    above = lax.erf(v) + 1.0
+    decay = jnp.exp2((v * v) * -LOG2E)
+    return v * above, above + (v * decay) * (2 / np.sqrt(np.pi))
 
 
 def beside(*streams):
@@ -337,6 +385,14 @@
             for step in steps[done:goal]:
                 step()
             entry[1] = goal
+
+
+def weight_terms(grad, weight, bias):
+    terms = []
+    for value in (weight * bias,) if grad is None else (weight * grad, weight * bias):
+        column = jnp.sum(value, axis=1, keepdims=True)
+        terms.append(jnp.broadcast_to(column, (D, HALF)).T[0:1, :])
+    return terms
 
 
 def feed_kernel(
@@ -354,16 +410,8 @@
     pack_ref,
     sums_ref,
     bup_ref,
-    h2_scr,
-    u_scr,
-    dg_scr,
-    g_scr,
-    du_scr,
-    dy_scr,
-    dz_scr,
+    rs_scr,
     x1_scr,
-    hat_scr,
-    rs_scr,
     gup_scr,
     gdn_scr,
     gout_scr,
@@ -379,131 +427,148 @@
 
     bound = BIG + GRID_S * GRID_S * cnt_ref[image]
     bias_out, gain, shift = s_ref[15:16, :], s_ref[16:17, :], s_ref[17:18, :]
-
-    def masked(low, high):
-        row = low + lax.broadcasted_iota(jnp.int32, (high - low, 1), 0)
-        return jnp.where(row < bound, rows_of(c_ref, low, high), 0.0)
-
-    def enter(chunk):
-        low, high = CHUNKS[chunk]
-
-        def cot():
-            dyr = masked(low, high).astype(BF)
-            dy_scr[low:high, :] = dyr
-            sums_ref[0] += fold(dyr.astype(F32))
-
-        def norm():
-            att = att_ref[0, low:high, :]
-            x1 = rows_of(x_ref, low, high) + dot(att, w_ref[:, :D]) + bias_out
-            x1_scr[low:high, :] = x1
-            hat, scale = normalise(x1)
-            hat_scr[low:high, :] = hat
-            rs_scr[low:high, :] = scale
-            h2_scr[low:high, :] = (hat * gain + shift).astype(BF)
-
-        return [cot, norm]
-
-    def expand(chunk):
-        low, high = CHUNKS[chunk]
-
-        def up(lanes):
-            dy = dy_scr[low:high, :]
-            dg_scr[low:high, lanes] = dot_nt(dy, down_ref[lanes, :])
-
-        def hidden(lanes):
-            cols = slice(D + lanes.start, D + lanes.stop)
-            u_scr[low:high, lanes] = dot(h2_scr[low:high, :], w_ref[:, cols])
-
-        steps = []
-        for part in range(4):
-            lanes = slice(part * D, (part + 1) * D)
-            steps += [functools.partial(up, lanes), functools.partial(hidden, lanes)]
-        return steps
-
-    def gelu(chunk):
-        low, high = CHUNKS[chunk]
-        totals = {}
-
-        def step(part, at):
-            lanes = slice(part * D, (part + 1) * D)
-            u = u_scr[at : at + 16, lanes] + s_ref[18 + part : 19 + part, :]
-            phi, slope = gelu_parts(u)
-            g_scr[at : at + 16, lanes] = (u * phi).astype(BF)
-            du = dg_scr[at : at + 16, lanes] * slope
-            totals[part] = fold(du) + totals[part] if part in totals else fold(du)
-            du_scr[at : at + 16, lanes] = du.astype(BF)
-            if at + 16 >= high:
-                bup_ref[:, lanes] += totals[part]
-
-        return [
-            functools.partial(step, part, at) for part in range(4) for at in range(low, high, 16)
-        ]
-
-    def contract(chunk):
-        low, high = CHUNKS[chunk]
-
-        def back():
-            dh2 = dot_nt(du_scr[low:high, :], w_ref[:, D : D + FF])
-            hat = hat_scr[low:high, :]
-            sums_ref[1] += fold(dh2 * hat)
-            sums_ref[2] += fold(dh2)
-            dx = masked(low, high) + norm_back(dh2 * gain, hat, rs_scr[low:high, :])
-            store_rows(dx_ref, low, high, dx)
-            dz = dx.astype(BF)
-            dz_scr[low:high, :] = dz
-            sums_ref[3] += fold(dz.astype(F32))
-
-        def out():
-            block = x1_scr[low:high, :] + dot(g_scr[low:high, :], down_ref[...])
-            store_rows(out_ref, low, high, block + s_ref[22:23, :])
-
-        def attention():
-            datt = dot_nt(dz_scr[low:high, :], w_ref[:, :D])
-            sums_ref[4] += fold(datt)
-            datt_ref[0, low:high, :] = datt.astype(BF)
-
-        return [back, out, attention]
-
-    def weights(chunk):
-        low, high = CHUNKS[chunk]
-
-        def up(lanes):
-            gup_scr[:, lanes] += dot_tn(h2_scr[low:high, :], du_scr[low:high, lanes])
-
-        def down(lanes):
-            gdn_scr[:, lanes] += dot_tn(dy_scr[low:high, :], g_scr[low:high, lanes])
-
-        def out():
-            gout_scr[...] += dot_tn(att_ref[0, low:high, :], dz_scr[low:high, :])
-
-        steps = []
-        for part in range(4):
-            lanes = slice(part * D, (part + 1) * D)
-            steps += [functools.partial(up, lanes), functools.partial(down, lanes)]
-        return steps + [out]
-
-    last = len(CHUNKS) - 1
-    beside(enter(0) + expand(0))
-    for chunk in range(last + 1):
-        matrix = []
-        if chunk < last:
-            matrix += enter(chunk + 1) + expand(chunk + 1)
-        if chunk > 0:
-            matrix += contract(chunk - 1) + weights(chunk - 1)
-        beside(gelu(chunk), matrix)
-    beside(contract(last) + weights(last))
+    lanes_of = [slice(part * D, (part + 1) * D) for part in range(FF // D)]
+    count = 16
+    rows = range(0, ROWS, count)
+    biases = [s_ref[18 + part : 19 + part, :] * ROOT for part in range(FF // D)]
+    sums = {}
+    held = {}
+
+    def add_sum(key, values, at, ref, *index):
+        sums[key] = sums[key] + fold(values) if key in sums else fold(values)
+        if at + count >= ROWS:
+            ref[index] += sums[key]
+
+    def keep(key, at, values):
+        held.setdefault(key, []).append(values)
+        if at + count >= ROWS:
+            held[key] = jnp.concatenate(held[key], axis=0)
+
+    def masked(at):
+        row = at + lax.broadcasted_iota(jnp.int32, (count, 1), 0)
+        return jnp.where(row < bound, rows_of(c_ref, at, at + count), 0.0)
+
+    def cot(at):
+        dy = masked(at)
+        keep("dy", at, dy.astype(BF))
+        add_sum("dy", dy, at, sums_ref, 0)
+
+    def project():
+        held["x1"] = dot(att_ref[0], w_ref[:, :D])
+
+    def norm(at):
+        own = slice(at, at + count)
+        x1 = rows_of(x_ref, at, at + count) + held["x1"][own] + bias_out
+        x1_scr[own, :] = x1
+        hat, scale = normalise(x1)
+        rs_scr[own, :] = scale
+        keep("hat", at, hat.astype(BF))
+        keep("h2", at, (hat * (gain * ROOT) + shift * ROOT).astype(BF))
+
+    def hidden(part):
+        cols = slice(D + part * D, D + (part + 1) * D)
+        held["v", part] = dot(held["h2"], w_ref[:, cols])
+
+    def hidden_back(part):
+        held["dg", part] = dot_nt(held["dy"], down_ref[lanes_of[part], :])
+
+    def gelu(part, at):
+        own = slice(at, at + count)
+        v = held["v", part][own] + biases[part]
+        g, slope = gelu_parts(v)
+        keep(("g", part), at, g.astype(BF))
+        du = held["dg", part][own] * slope
+        keep(("du", part), at, du.astype(BF))
+
+    def gelus(part):
+        return [functools.partial(gelu, part, at) for at in rows]
+
+    def grad_up(part):
+        both = dot(held["hat_t"], held["du", part])
+        gup_scr[:, lanes_of[part]] += both[:D]
+        bup_ref[:, lanes_of[part]] += both[D : D + 8]
+
+    def grad_down(part):
+        gdn_scr[:, lanes_of[part]] += dot(held["dy_t"], held["g", part])
+
+    def joined(key, *parts):
+        return jnp.concatenate([held[key, part] for part in parts], axis=1)
+
+    half = FF // 2
+
+    def out_first():
+        held["out"] = dot(joined("g", 0, 1), down_ref[:half, :])
+
+    def out_last():
+        held["out"] += dot(joined("g", 2, 3), down_ref[half:, :])
+
+    def out_store(at):
+        own = slice(at, at + count)
+        out = x1_scr[own, :] + held["out"][own] * ROOT + s_ref[22:23, :]
+        store_rows(out_ref, at, at + count, out)
+
+    def back_first():
+        held["dh"] = dot_nt(joined("du", 0, 1), w_ref[:, D : D + half])
+
+    def back_last():
+        held["dh"] += dot_nt(joined("du", 2, 3), w_ref[:, D + half : D + FF])
+
+    def norm_grad(at):
+        own = slice(at, at + count)
+        hat = held["hat"][own].astype(F32)
+        dx = masked(at) + norm_back(held["dh"][own] * (gain * 0.5), hat, rs_scr[own, :])
+        store_rows(dx_ref, at, at + count, dx)
+        keep("dz", at, dx.astype(BF))
+        add_sum("dz", dx, at, sums_ref, 1)
+
+    def attention():
+        datt = dot_nt(held["dz"], w_ref[:, :D])
+        datt_ref[0] = datt.astype(BF)
+
+    def grad_out():
+        gout_scr[...] += dot_tn(att_ref[0], held["dz"])
+
+    def each(step, *parts):
+        return [functools.partial(step, part) for part in parts]
+
+    def turn(key):
+        held[key + "_t"] = held[key].T
+
+    beside(each(cot, *rows), [project])
+    turn("dy")
+    beside(each(norm, *rows), each(hidden_back, 0, 1, 2, 3))
+    turn("hat")
+    held["hat_t"] = with_ones(held["hat_t"])
+    hidden(0)
+    beside(each(hidden, 1, 2, 3), gelus(0))
+    beside(each(grad_up, 0) + each(grad_down, 0), gelus(1))
+    beside([back_first] + each(grad_up, 1) + each(grad_down, 1), gelus(2))
+    beside([out_first] + each(grad_up, 2) + each(grad_down, 2), gelus(3))
+    back_last()
+    beside([out_last] + each(grad_up, 3) + each(grad_down, 3), each(norm_grad, *rows))
+    beside([attention, grad_out], each(out_store, *rows))
 
     @pl.when(image == pl.num_programs(0) - 1)
     def _():
-        turn_scr[...] = gdn_scr[...].T
+        turn_scr[...] = gdn_scr[...].T * ROOT
         for owner in range(D // shard):
             for part in range(FF // D):
                 low = (owner * (FF // D) + part) * shard
                 pack_scr[owner * shard : (owner + 1) * shard, part * D : (part + 1) * D] = turn_scr[
                     low : low + shard, :
                 ]
+        bup_ref[...] *= 0.5
+        bias = bup_ref[0:1, :]
+        grad = gup_scr[...] * 0.5
+        terms = weight_terms(grad, w_ref[:, D : D + FF].astype(F32), bias)
+        out_bias = jnp.sum(sums_ref[1], axis=0, keepdims=True)
+        terms += weight_terms(None, w_ref[:, :D].astype(F32), out_bias)
+        for at, term in enumerate(terms):
+            sums_ref[2 + at, 0:1, :] = term
+        columns = s_ref[15:23, :].T
+        grad = columns[:, 1:2] * grad + columns[:, 2:3] * bias
         pack_ref[:, :D] = gout_scr[...].astype(BF)
-        pack_ref[:, D : D + FF] = gup_scr[...].astype(BF)
+        pack_ref[:, D : D + FF] = grad.astype(BF)
         pack_ref[:, D + FF :] = pack_scr[...].astype(BF)
 
 
@@ -516,6 +581,7 @@
 
 def back_kernel(
     spans,
+    places,
     datt_ref,
     win_ref,
     e_ref,
@@ -553,11 +619,10 @@
 
     for low, high in CHUNKS:
         datt_scr[low:high, :] = datt_ref[0, low:high, :].astype(F32)
-    minus = -head_block(WIN)
+    minus = two_heads(jnp.full((HALF, WIN), -1.0, BF), 0)
     none = jnp.zeros((WIN - QROWS, HALF), BF)
 
-    def weigh(pair, _):
-        state = []
+    def weigh(pair, state):
         for member in range(2):
             at = 2 * pair + member
             branch = branch_of(pair, member)
@@ -574,66 +639,80 @@
             v = win_ref[0, at, :, 2 * HALF :]
             pad_scr[at, EDGE : EDGE + QROWS, :] = first_rows(v.astype(F32), tokens_of(pair))
             dn = grad * il_ref[0, at]
-            z = (dn * o_ref[0, at].astype(F32)).astype(BF)
+            z = pltpu.roll(dn * o_ref[0, at].astype(F32), HALF // 2, 1).astype(BF)
             dn = dn.astype(BF)
-            left = jnp.concatenate([dn, z], axis=1)
-            v = jnp.concatenate([v, none], axis=0)
-            right = jnp.concatenate([by_head(v), minus], axis=1)
-            state.append((grad, dn, dot_nt(left, right)))
-        return state
+            rows = z * lane_half(True), z * lane_half(False)
+            v = jnp.concatenate([v, none], axis=0).T
+            state[member] = grad, dn, by_two_heads(dn, rows, v, minus)
+            yield
 
     def score(pair, state):
-        new = []
-        for member, (grad, dn, weighed) in enumerate(state):
+        for member in range(2):
+            grad, dn, weighed = state[member]
             e = e_ref[0, 2 * pair + member]
-            ds = (weighed * e.astype(F32)).astype(BF)
-            new.append((grad, dn, ds, e))
-        return new
+            ds = jnp.concatenate(weighed, axis=1).astype(BF) * e
+            state[member] = grad, dn, ds, e
+            yield
 
     def spread(pair, state):
         kind = kind_of(pair)
-        taps, dvs = [], []
-        for member, (grad, dn, ds, e) in enumerate(state):
+        taps = []
+        for member in range(2):
+            grad, dn, ds, e = state[member]
             at = 2 * pair + member
-            branch = branch_of(pair, member)
-            kernel = k_ref[branch].astype(BF)
+            kernel = k_ref[branch_of(pair, member)].astype(BF)
             q = win_ref[0, at, :, 0:HALF]
             k = jnp.concatenate([win_ref[0, at, :, HALF : 2 * HALF], none], axis=0)
-            dq = dot(ds, by_head(k)) * SCALE
+            dq = dot(ds, by_head(k))
             q_t, dn_t = q.T, dn.T
             dk, dv = [], []
-            for h in range(HEADS):
-                lanes = slice(h * WIN, (h + 1) * WIN)
-                own = slice(h * HEAD, (h + 1) * HEAD)
-                dk.append(dot(q_t[own], ds[:, lanes]))
-                dv.append(dot(dn_t[own], e[:, lanes]))
-            dk = jnp.concatenate(dk, axis=0).T[:QROWS] * LN2
-            dvs.append((dq, dk, jnp.concatenate(dv, axis=0).T[:QROWS]))
-            low = jnp.concatenate([grad.astype(BF), none], axis=0)
+            for half in range(2):
+                lanes = slice(2 * half * WIN, 2 * (half + 1) * WIN)
+                own = slice(2 * half * HEAD, 2 * (half + 1) * HEAD)
+                for parts, left, right in ((dk, q_t, ds), (dv, dn_t, e)):
+                    both = dot(left[own], right[:, lanes])
+                    parts += [both[:HEAD, :WIN], both[HEAD:, WIN:]]
+            state[member] = dq, dk, dv, grad
+            low = grad.astype(BF)
             taps.append(
                 jnp.concatenate([low * kernel[8 - tap : 9 - tap] for tap in range(9)], axis=0)
             )
-            broad = shape_of(kind)[1]
+            yield
+        state[2] = dot(tap_ref[kind], jnp.concatenate(taps, axis=1))
+        yield
+
+    def kernels(pair, state):
+        kind = kind_of(pair)
+        broad = shape_of(kind)[1]
+        for member in range(2):
+            at = 2 * pair + member
+            grad = state[member][3]
             sides = {0: grad}
             if kind < 2:
                 for dx in (-1, 1):
-                    sides[dx] = grad * edge_ref[kind, 4 + dx]
+                    sides[dx] = grad * edge_ref[places[kind, 0, dx]]
             for tap, (dy, dx) in enumerate(TAPS):
                 if kind < 2 or tap == 4:
                     side = sides[dx]
                 else:
-                    side = grad * edge_ref[kind, tap]
+                    side = grad * edge_ref[places[kind, dy, dx]]
                 start = EDGE + dy * broad + dx
-                kern_scr[branch, tap] += fold(side * pad_scr[at, start : start + QROWS, :])
-        conv = dot(tap_ref[kind], jnp.concatenate(taps, axis=1))
+                kern_scr[branch_of(pair, member), tap] += fold(
+                    side * pad_scr[at, start : start + QROWS, :]
+                )
+            yield
+
+    def put(pair, state):
         for member in range(2):
             at = 2 * pair + member
             branch = branch_of(pair, member)
-            dq, dk, dv = dvs[member]
-            dv = dv + conv[:, member * HALF : (member + 1) * HALF]
-            for part, piece in enumerate((dq, dk, dv)):
+            dq, dk, dv, _ = state[member]
+            dk = jnp.concatenate(dk, axis=0).T[:QROWS] * LN2
+            dv = jnp.concatenate(dv, axis=0).T[:QROWS]
+            dv = dv + state[2][:, member * HALF : (member + 1) * HALF]
+            for part, piece in enumerate((dq * SCALE, dk, dv)):
                 lanes = slice(part * D + branch * HALF, part * D + (branch + 1) * HALF)
-                if kind == 1:
+                if kind_of(pair) == 1:
                     back_scr[at - 4, part] = piece
                     for source, target in pieces_of(pair, member):
                         dqkv_scr[source : source + STRIPE, lanes] = back_scr[
@@ -642,40 +721,36 @@
                 else:
                     low, count = first_of(pair, member), tokens_of(pair)
                     dqkv_scr[low : low + count, lanes] = piece[:count]
-
-    pipelined((weigh, score, spread), ORDER)
-    for low, high in CHUNKS:
-        value = dqkv_scr[low:high, :]
-        bias_scr[...] += fold(value)
-        dqkv_ref[0, low:high, :] = value.astype(BF)
-    g_scr[...] += dot_tn(hat_ref[0], dqkv_ref[0])
+            yield
+
+    pipelined((weigh, score, spread, put, kernels), ORDER)
+    dqkv = dqkv_scr[...].astype(BF)
+    dqkv_ref[0] = dqkv
+    both = dot(with_ones(hat_ref[0].T), dqkv)
+    g_scr[...] += both[:D]
+    bias_scr[...] += both[D : D + 8]
 
     @pl.when(image == pl.num_programs(0) - 1)
     def _():
-        wide = w_ref[...].astype(F32)
-        exact = functools.partial(
-            lax.dot_general,
-            dimension_numbers=(((1,), (1,)), ((), ())),
-            precision=lax.Precision.HIGHEST,
-            preferred_element_type=F32,
-        )
-
         def put(row, terms):
             for at in range(0, terms.shape[1], HALF):
                 small_scr[row : row + 1, :] = terms[:, at : at + HALF]
                 row += 1
 
         total = lambda terms: jnp.sum(terms, axis=0, keepdims=True)
-        bias = total(bias_scr[...])
-        put(0, total(exact(jnp.ones((8, 3 * D), F32), wide * g_scr[...])) * 0.125)
-        put(2, total(exact(bias_scr[...], wide)))
+        bias = bias_scr[0:1, :]
+        gain, shift = weight_terms(g_scr[...], w_ref[:, : 3 * D].astype(F32), bias)
+        put(0, gain)
+        put(2, shift)
         put(4, bias)
         for tap in range(9):
             for branch in range(2):
                 put(10 + 2 * tap + branch, total(kern_scr[branch, tap]))
-        for row, entry in ((28, 4), (30, 3), (32, 1), (34, 2), (44, 0)):
+        for row, entry in ((30, 1), (44, 0)):
             put(row, total(feed_ref[entry]))
-        put(36, total(bup_ref[...]))
+        for row, entry in ((32, 2), (34, 3), (28, 4)):
+            put(row, feed_ref[entry, 0:1, :])
+        put(36, bup_ref[0:1, :])
         for owner, (row, rows) in enumerate(spans):
             shard = D // len(spans)
             pack_scr[owner * shard : owner * shard + rows, :] = small_scr[row : row + rows, :]
@@ -685,9 +760,10 @@
         pack_ref[:, 3 * D :] = pack_scr[...].astype(BF)
 
 
-def input_kernel(x_ref, dqkv_ref, dx_ref, w_ref, s_ref, out_ref):
+def input_kernel(x_ref, dqkv_ref, dx_ref, w_ref, s_ref, *out_refs):
+    out_ref = out_refs[-1]
     for low, high in CHUNKS:
-        dh = dot_nt(dqkv_ref[0, low:high, :], w_ref[...])
+        dh = dot_nt(dqkv_ref[0, low:high, :], w_ref[:, : 3 * D])
         hat, scale = normalise(rows_of(x_ref, low, high))
         grad = rows_of(dx_ref, low, high) + norm_back(dh * s_ref[0:1, :], hat, scale)
         store_rows(out_ref, low, high, grad)
@@ -718,7 +794,21 @@
 def small_tables(small):
     rows = small.reshape(-1, D)
     taps = rows[5:15].reshape(10, 2, HALF).transpose(1, 0, 2)
-    return jnp.pad(rows, ((0, 1), (0, 0))), jnp.pad(taps, ((0, 0), (0, 6), (0, 0)))
+    return rows, taps
+
+
+def run_norm(tokens_in):
+    rows = TOK_IMG * 2
+    block = pl.BlockSpec((rows, D), lambda i: (i, 0))
+    return pl.pallas_call(
+        norm_kernel,
+        grid=(tokens_in.shape[0] // rows,),
+        in_specs=[block],
+        out_specs=block,
+        out_shape=sds(tokens_in.shape, F32),
+        compiler_params=params(),
+        name="norm",
+    )(tokens_in)
 
 
 def run_attend(tokens_in, w_qkv, table, kernels, side):
@@ -774,16 +864,8 @@
                 whole((8, FF)),
             ],
             scratch_shapes=[
-                pltpu.VMEM((ROWS, D), BF),
-                pltpu.VMEM((ROWS, FF), F32),
-                pltpu.VMEM((ROWS, FF), F32),
-                pltpu.VMEM((ROWS, FF), BF),
-                pltpu.VMEM((ROWS, FF), BF),
-                pltpu.VMEM((ROWS, D), BF),
-                pltpu.VMEM((ROWS, D), BF),
+                pltpu.VMEM((ROWS, 1), F32),
                 pltpu.VMEM((ROWS, D), F32),
-                pltpu.VMEM((ROWS, D), F32),
-                pltpu.VMEM((ROWS, 1), F32),
                 pltpu.VMEM((D, FF), F32),
                 pltpu.VMEM((D, FF), F32),
                 pltpu.VMEM((D, D), F32),
@@ -806,9 +888,10 @@
 
 def run_back(spans, blocks, w_qkv, table, kernels, sums, b_up, side):
     images = blocks[0].shape[0]
-    consts = [w_qkv, table, kernels, sums, b_up, side, jnp.asarray(edge_masks())]
+    masks, places = edge_masks()
+    consts = [w_qkv, table, kernels, sums, b_up, side, jnp.asarray(masks)]
     return pl.pallas_call(
-        functools.partial(back_kernel, spans),
+        functools.partial(back_kernel, spans, places),
         grid=(images,),
         in_specs=[image_of(b.shape[1:]) for b in blocks] + [whole(c.shape) for c in consts],
         out_specs=[image_of((ROWS, 3 * D)), whole((D, 3 * D + HALF))],
@@ -830,22 +913,26 @@
     )(*blocks, *consts)
 
 
-def run_input(tokens_in, dqkv, dx, w_qkv, table):
+def run_input(tokens_in, dqkv, dx, w_qkv, table, low, high, out=None):
+    own = pl.BlockSpec((TOK_IMG, D), lambda i: (low + i, 0))
+    rows = pl.BlockSpec((1, ROWS, 3 * D), lambda i: (low + i, 0, 0))
+    ends = [] if out is None else [out]
     return pl.pallas_call(
         input_kernel,
-        grid=(dqkv.shape[0],),
-        in_specs=[
-            tokens(),
-            image_of((ROWS, 3 * D)),
-            tokens(),
-            whole(w_qkv.shape),
-            whole(table.shape),
-        ],
-        out_specs=tokens(),
+        grid=(high - low,),
+        in_specs=[own, rows, own, whole(w_qkv.shape), whole(table.shape)]
+        + [pl.BlockSpec(memory_space=pl.ANY) for _ in ends],
+        out_specs=own,
         out_shape=sds(tokens_in.shape, F32),
+        input_output_aliases={5: 0} if ends else {},
         compiler_params=params(),
+        cost_estimate=pl.CostEstimate(
+            flops=(high - low) * 2 * ROWS * 3 * D * D,
+            bytes_accessed=(high - low) * ROWS * D * 18,
+            transcendentals=0,
+        ),
         name="input_grad",
-    )(tokens_in, dqkv, dx, w_qkv, table)
+    )(tokens_in, dqkv, dx, w_qkv, table, *ends)
 
 
 def moments(grad, first, second):
@@ -924,9 +1011,13 @@
     da_ref,
     norm_ref,
 ):
-    total = jnp.sum(sq_ref[...], axis=1, keepdims=True)
+    total = jnp.sum(jnp.sum(sq_ref[...], axis=0), axis=1, keepdims=True)
     norm = jnp.sqrt(total)
-    norm_ref[...] = jnp.broadcast_to(norm, norm_ref.shape)
+    row = lax.broadcasted_iota(jnp.int32, (8, HALF), 0)
+    lane = lax.broadcasted_iota(jnp.int32, (8, HALF), 1)
+    for half in range(2):
+        own = jnp.where(row == lane + 4 * half, norm, 0.0)
+        norm_ref[half : half + 1, :] = jnp.sum(own, axis=0, keepdims=True)[:, 0:4]
     ratio = norm[0:4] / norm[4:8]
     keep = min(EMA_CEILING, (1.0 + STEP) / (10.0 + STEP))
     for at, lanes in enumerate(MATRICES):
@@ -953,25 +1044,16 @@
     return jnp.concatenate([wide] + blocks, axis=1)
 
 
-def gather(values, count):
-    copies = jnp.broadcast_to(values[None], (count,) + values.shape)
-    return lax.all_to_all(copies, "fsdp", 0, 0).reshape(-1, values.shape[1])
+def copies(values, count):
+    return jnp.broadcast_to(values[None], (count,) + values.shape)
 
 
 def send_terms(values, count):
-    return lax.all_to_all(values.reshape(count, -1, values.shape[1]), "fsdp", 0, 0)
+    return lax.all_to_all(values.reshape(count, -1, values.shape[-1]), "fsdp", 0, 0)
 
 
 def add_terms(terms):
     return jnp.sum(terms.astype(F32), axis=0)
-
-
-def add_all(values, count):
-    step = 1
-    while step < count:
-        values = values + lax.ppermute(values, "fsdp", [(i, i ^ step) for i in range(count)])
-        step *= 2
-    return values
 
 
 def on_device(
@@ -997,27 +1079,32 @@
     wide_low = wide_w.astype(BF)
     small_low = jnp.pad(small_p.astype(BF).reshape(rows, narrow), ((0, 0), (0, HALF - narrow)))
     first = jnp.concatenate([wide_low[:, : 3 * D], small_low], axis=1)
-    first = gather(first, count)
-    late_all = gather(side_by_side(wide_low[:, 3 * D :], down_w.astype(BF)), count)
+    first = send_terms(copies(first, count), count)
+    late_all = copies(side_by_side(wide_low[:, 3 * D :], down_w.astype(BF)), count)
+    hat = run_norm(tokens_in)
+    first, late_all, hat = lax.optimization_barrier((first, late_all, hat))
+    first = first.reshape(D, -1)
+    late_all = send_terms(late_all, count).reshape(D, -1)
     down_all = late_all[:, D + FF :].reshape(count, rows, FF // D, D)
     down_all = down_all.transpose(0, 2, 1, 3).reshape(FF, D)
-    w_qkv = first[:, : 3 * D]
     table, kernels = small_tables(first[:, 3 * D : 3 * D + narrow].astype(F32).reshape(-1))
     side = np.stack([tap_matrix(kind) for kind in range(3)])
-    side = bf(side.transpose(0, 2, 1, 3).reshape(3, QROWS, 9 * WIN))
-    hat, att, win, e, il, o = run_attend(tokens_in, w_qkv, table, kernels, side)
+    side = bf(side.transpose(0, 2, 1, 3).reshape(3, QROWS, 9 * QROWS))
+    hat, att, win, e, il, o = run_attend(hat, first, table, kernels, side)
     block_out, dx, datt, g_late, sums, b_up = run_feed(
         rows, crop_count, tokens_in, cotangent, att, late_all, down_all, table
     )
     late = send_terms(g_late, count)
     spans = small_spans(rows, narrow)
     dqkv, g_last = run_back(
-        spans, [datt, win, e, il, o, hat], w_qkv, table, kernels, sums, b_up, side
+        spans, [datt, win, e, il, o, hat], first, table, kernels, sums, b_up, side
     )
     late, g_last = lax.optimization_barrier((late, g_last))
     late = add_terms(late)
     last = send_terms(g_last, count)
-    grad_in = run_input(tokens_in, dqkv, dx, w_qkv, table)
+    images = dqkv.shape[0]
+    begin = images * 3 // 4
+    grad_in = run_input(tokens_in, dqkv, dx, first, table, 0, begin)
     last, grad_in = lax.optimization_barrier((last, grad_in))
     last = add_terms(last)
     last_other = to_other(last)
@@ -1030,11 +1117,14 @@
         *(last, last_other, late, late_other),
         *(wide_w, wide_m, wide_v, down_w, down_m, down_v),
     )
-    squares = add_all(squares, count)
+    squares, grad_in = lax.optimization_barrier((copies(squares, count), grad_in))
+    squares = send_terms(squares, count)
+    grad_in = run_input(tokens_in, dqkv, dx, first, table, begin, images, grad_in)
+    squares, grad_in = lax.optimization_barrier((squares, grad_in))
     wide_new, wide_avg, down_new, down_avg, norms = plain(
         update_kernel,
         "update",
-        [wide_like] * 2 + [down_like] * 2 + [sds((8, HALF), F32)],
+        [wide_like] * 2 + [down_like] * 2 + [sds((2, 4), F32)],
         *(squares, wide_w, wide_upd, wide_ema, down_w, down_upd, down_ema),
     )
     shard_small = (last + last_other)[: spans[0][1], 3 * D :].reshape(-1)
@@ -1059,7 +1149,7 @@
         small_first,
         small_second,
         small_avg,
-        norms[:, 0].reshape(2, 4),
+        norms,
     )
 
 

time: 192 us -> 172 us (0.90)
  Pallas kernels: 122 us -> 114 us
  waiting for transfers between devices: 19.4 us -> 14 us
  starting transfers between devices: 35.2 us -> 31.2 us
    ppermute x4 -> x0, starting transfers between devices: 8.63 us -> none  [add_all(): lax.ppermute(values, 'fsdp', [(i, i ^ step) for i in range(count)])]
    pallas_call x1, Pallas kernels: 28.4 us -> 22.1 us  [run_attend(): pl.pallas_call(attend_kernel, grid=(images,), in_specs=[tokens(), whole(w...]
    ppermute x4 -> x0, waiting for transfers between devices: 5.54 us -> none  [add_all(): lax.ppermute(values, 'fsdp', [(i, i ^ step) for i in range(count)])]
    all_to_all x4 -> x5, starting transfers between devices: 25.9 us -> 31 us  [send_terms(): lax.all_to_all(values.reshape(count, -1, values.shape[-1]), 'fsdp', 0, 0)]
    pallas_call x1, Pallas kernels: 37.6 us -> 34.3 us  [run_feed(): pl.pallas_call(functools.partial(feed_kernel, shard), grid_spec=pltpu.Pre...]
    pallas_call x2 -> x4, Pallas kernels: 52.1 us -> 53.2 us  [the longest x1 31.8 us: run_back(): pl.pallas_call(functools.partial(back_kernel, spans, places), grid=(image...]
    all_to_all x4 -> x5, waiting for transfers between devices: 13 us -> 12.8 us  [send_terms(): lax.all_to_all(values.reshape(count, -1, values.shape[-1]), 'fsdp', 0, 0)]
  transfers between devices with their start and end apart: 10 -> 7, of which waited for: 7 -> 5; matrix products, arithmetic and copies ran while one was open for 2% -> 2% of each run, Pallas kernels for 42% -> 44%
where the time goes in v4:
time: 172 us; the launch traced here: 171 us
  Pallas kernels  114 us (66%)
  starting transfers between devices  31.2 us (18%)
  waiting for transfers between devices  14 us (8%)
  local copies, waits for them, and re-layouts  6.82 us (4%)
  other arithmetic  4.09 us (2%)
    pallas_call x1, Pallas kernels, run_feed(): pl.pallas_call(functools.partial(feed_kernel, shard), grid_spec=pltpu.Pre...  34.3 us
    pallas_call x1, Pallas kernels, run_back(): pl.pallas_call(functools.partial(back_kernel, spans, places), grid=(image...  31.8 us
    all_to_all x5, starting transfers between devices, send_terms(): lax.all_to_all(values.reshape(count, -1, values.shape[-1]), 'fsdp', 0, 0)  31 us
    pallas_call x1, Pallas kernels, run_attend(): pl.pallas_call(attend_kernel, grid=(images,), in_specs=[tokens(), whole(w...  22.1 us
    pallas_call x2, Pallas kernels, run_input(): pl.pallas_call(input_kernel, grid=(high - low,), in_specs=[own, rows, own...  14.4 us
    all_to_all x5, waiting for transfers between devices, send_terms(): lax.all_to_all(values.reshape(count, -1, values.shape[-1]), 'fsdp', 0, 0)  12.8 us
    pallas_call x1, Pallas kernels, run_norm(): pl.pallas_call(norm_kernel, grid=(tokens_in.shape[0] // rows,), in_specs=...  6.95 us
    pallas_call x2, Pallas kernels, plain(): pl.pallas_call(kernel, out_shape=out_shape, compiler_params=pltpu.Compile...  4.11 us
  transfers between devices with their start and end apart: 7, of which 5 were waited for; matrix products, arithmetic and copies ran while one was open for 2% of the time, Pallas kernels for 44%

profile of v4, /device:TPU:0, one launch (start us, length us, event | category | flops | bytes accessed | tf_op | source)
XLA Modules:
  0.0 170.6 jit_solution(1575470860711528846)
XLA Ops:
  0.6 0.9 convert_element_type.18
  1.6 0.7 convert_element_type.19
  2.3 0.1 reshape.60
  2.4 0.8 broadcast_in_dim.6
  3.2 8.3 %all-to-all-start = ((bf16[16,16,896]{2,1,0:T(8,128)(2,1)}), bf16[16,16,896]{2,1,0:T(8,128)(2,1)S(1)}, u32[]{:S(2)}, u32[]{:S(2)}) async-start(bf16[16,16,896]{2,1,0:T(8,128)(2,1)} %broadcast_in_dim.6), calls=%async_computation | async-start | bytes 917504 | tf_op jit(solution)/shard_map/all_to_all | solution.py:1052
  11.5 0.8 convert_element_type.20
  12.3 6.9 %norm.1.x_ref = f32[5440,256]{1,0:T(8,128)} custom-call(f32[5440,256]{1,0:T(8,128)} %x_ref.7), custom_call_target="tpu_custom_call" | custom-call | tf_op jit(solution)/shard_map/norm/pallas_call | solution.py:803
  19.3 6.0 %all-to-all-done = bf16[16,16,896]{2,1,0:T(8,128)(2,1)S(1)} async-done(((bf16[16,16,896]{2,1,0:T(8,128)(2,1)}), bf16[16,16,896]{2,1,0:T(8,128)(2,1)S(1)}, u32[]{:S(2)}, u32[]{:S(2)}) %all-to-all-start) | async-done | bytes 458784 | tf_op jit(solution)/shard_map/all_to_all | solution.py:1052
  25.4 0.0 copy-start
  25.4 1.2 broadcast_in_dim.7
  26.5 3.8 %all-to-all-start.1 = ((bf16[16,16,2304]{2,1,0:T(8,128)(2,1)}), bf16[16,16,2304]{2,1,0:T(8,128)(2,1)S(1)}, u32[]{:S(2)}, u32[]{:S(2)}) async-start(bf16[16,16,2304]{2,1,0:T(8,128)(2,1)} %broadcast_in_dim.7), calls=%async_computation.1 | async-start | bytes 2359296 | tf_op jit(solution)/shard_map/all_to_all | solution.py:1052
  30.3 0.2 reshape.69.s_ref
  30.5 0.0 copy-start.2
  30.5 0.6 copy.41
  31.2 0.0 copy-done
  31.2 0.0 copy-done.2
  31.2 22.1 %attend.1 = (bf16[8,688,256]{2,1,0:T(8,128)(2,1)}, bf16[8,688,256]{2,1,0:T(8,128)(2,1)}, bf16[8,14,112,384]{3,2,1,0:T(8,128)(2,1)}, bf16[8,14,112,512]{3,2,1,0:T...) custom-call(f32[5440,256]{1,0:T(8,128)} %norm.1.x_ref, bf16[256,896]{1,0:T(8,128)(2,1)} %bitcast.13, ...), custom_call_target="tpu_custom_call" | custom-call | tf_op jit(solution)/shard_map/attend/pallas_call | solution.py:826
  53.2 3.3 %all-to-all-done.1 = bf16[16,16,2304]{2,1,0:T(8,128)(2,1)S(1)} async-done(((bf16[16,16,2304]{2,1,0:T(8,128)(2,1)}), bf16[16,16,2304]{2,1,0:T(8,128)(2,1)S(1)}, u32[]{:S(2)}, u32[]{:S(2)}) %all-to-all-start.1) | async-done | bytes 1179680 | tf_op jit(solution)/shard_map/all_to_all | solution.py:1052
  56.6 0.0 copy-start.1
  56.6 0.1 slice.48
  56.6 0.4 reshape.64
  57.0 0.9 copy.39
  57.9 0.0 copy-done.1
  57.9 34.3 %feed.1 = (f32[5440,256]{1,0:T(8,128)}, f32[5440,256]{1,0:T(8,128)}, bf16[8,688,256]{2,1,0:T(8,128)(2,1)}, bf16[256,2304]{1,0:T(8,128)(2,1)}, f32[5,8,256]{2,1,0:T(8,128)}, /*index=5*/f32[8,1024]{1,0:T(8,128)}) custom-call(s32[8]{0:T(128)} %cnt_ref.1, f32[5440,256]{1,0:T(8,128)} %x_ref.7, f32[5440,256]{1,0:T(8,128)} %c_ref.1, ...), custom_call_target="tpu_custom_call" | custom-call | tf_op jit(solution)/shard_map/feed/pallas_call | solution.py:845
  92.2 6.1 %all-to-all-start.2 = ((bf16[16,16,2304]{2,1,0:T(8,128)(2,1)}), bf16[16,16,2304]{2,1,0:T(8,128)(2,1)S(1)}, u32[]{:S(2)}, u32[]{:S(2)}) async-start(bf16[16,16,2304]{2,1,0:T(8,128)(2,1)} %bitcast.20), calls=%async_computation.2 | async-start | bytes 2359296 | tf_op jit(solution)/shard_map/all_to_all | solution.py:1052
  98.3 31.8 %back.1 = (bf16[8,688,768]{2,1,0:T(8,128)(2,1)}, bf16[256,896]{1,0:T(8,128)(2,1)}) custom-call(bf16[8,688,256]{2,1,0:T(8,128)(2,1)} %get-tuple-element.58.datt_ref, bf16[8,14,112,384]{3,2,1,0:T(8,128)(2,1)} %get-tuple-element.59.win_ref, bf16[8,14,112,512]{3,2,1,0:T(8,128)(2,1)} %get-tuple-element.60.e_ref, f32[8,14,112,128]{3,2,1,0:T(8,128)} %get-tuple-element.61.il_ref, ...), custom_call_target="tpu_custom_call" | custom-call | tf_op jit(solution)/shard_map/back/pallas_call | solution.py:893
  130.1 0.0 all-to-all-done.2
  130.2 6.9 %all-to-all-start.3 = ((bf16[16,16,896]{2,1,0:T(8,128)(2,1)}), bf16[16,16,896]{2,1,0:T(8,128)(2,1)S(1)}, u32[]{:S(2)}, u32[]{:S(2)}) async-start(bf16[16,16,896]{2,1,0:T(8,128)(2,1)} %bitcast.21), calls=%async_computation.3 | async-start | bytes 917504 | tf_op jit(solution)/shard_map/all_to_all | solution.py:1052
  137.1 0.0 copy-start.8
  137.1 0.0 copy-start.9
  137.1 0.0 copy-start.10
  137.1 0.0 copy-start.11
  137.1 10.1 %input_grad.2.out_refs_0_ = f32[5440,256]{1,0:T(8,128)} custom-call(f32[5440,256]{1,0:T(8,128)} %x_ref.7, bf16[8,688,768]{2,1,0:T(8,128)(2,1)} %get-tuple-element.68.dqkv_ref, f32[5440,256]{1,0:T(8,128)} %get-tuple-element.69.dx_ref, bf16[256,896]{1,0:T(8,128)(2,1)} %bitcast.15, f32[23,256]{1,0:T(8,128)} %copy-done.2), custom_call_target="tpu_custom_call" | custom-call | flops 1623195648 | bytes 19021824 | tf_op jit(solution)/shard_map/input_grad/pallas_call | solution.py:920
  147.2 0.2 convert_reduce_fusion.gl_ref
  147.4 0.0 copy-start.3
  147.4 0.1 collective-permute-start.1
  147.5 1.6 all-to-all-done.3
  149.1 0.1 convert_reduce_fusion.1.gq_ref
  149.2 0.0 copy-start.5
  149.2 0.1 collective-permute-start
  149.3 0.0 collective-permute-done.1.gl_other_ref
  149.3 0.0 copy-start.6
  149.3 1.2 collective-permute-done.gq_other_ref
  150.5 0.0 copy-done.3
  150.5 0.0 copy-done.5
  150.5 0.0 copy-done.6
  150.5 0.0 copy-start.7
  150.5 0.6 copy-done.7
  151.1 2.1 %moment.1 = (f32[16,2048]{1,0:T(8,128)}, f32[16,2048]{1,0:T(8,128)}, f32[16,2048]{1,0:T(8,128)}, f32[64,256]{1,0:T(8,128)}, f32[64,256]{1,0:T(8,128)}, /*index=5*/f32[64,256]{1,0:T(8,128)}, f32[8,128]{1,0:T(8,128)}) custom-call(f32[16,896]{1,0:T(8,128)} %copy-done.5, f32[16,896]{1,0:T(8,128)} %copy-done.7, f32[16,2304]{1,0:T(8,128)} %copy-done.3, ...), custom_call_target="tpu_custom_call" | custom-call | tf_op jit(solution)/shard_map/moment/pallas_call | solution.py:1033
  153.2 1.3 broadcast_in_dim.8
  154.5 5.9 %all-to-all-start.4 = ((f32[16,8,128]{2,1,0:T(8,128)}), f32[16,8,128]{2,1,0:T(8,128)S(1)}, u32[]{:S(2)}, u32[]{:S(2)}) async-start(f32[16,8,128]{2,1,0:T(8,128)} %broadcast_in_dim.8), calls=%async_computation.4 | async-start | bytes 131072 | tf_op jit(solution)/shard_map/all_to_all | solution.py:1052
  160.5 0.7 fusion.3
  161.2 0.0 copy-done.8
  161.2 0.0 copy-done.9
  161.2 0.0 copy-done.10
  161.2 0.0 copy-done.11
  161.2 0.7 multiply_add_fusion
  161.9 4.3 %input_grad.3 = f32[5440,256]{1,0:T(8,128)} custom-call(f32[5440,256]{1,0:T(8,128)} %x_ref.7, bf16[8,688,768]{2,1,0:T(8,128)(2,1)} %get-tuple-element.68.dqkv_ref, f32[5440,256]{1,0:T(8,128)} %get-tuple-element.69.dx_ref, bf16[256,896]{1,0:T(8,128)(2,1)} %bitcast.16, f32[23,256]{1,0:T(8,128)} %copy-done.2, ...), custom_call_target="tpu_custom_call", output_to_operand_aliasing={{}: (5, {})} | custom-call | flops 541065216 | bytes 6340608 | tf_op jit(solution)/shard_map/input_grad/pallas_call | solution.py:920
  166.2 1.8 %all-to-all-done.4.sq_ref = f32[16,8,128]{2,1,0:T(8,128)S(1)} async-done(((f32[16,8,128]{2,1,0:T(8,128)}), f32[16,8,128]{2,1,0:T(8,128)S(1)}, u32[]{:S(2)}, u32[]{:S(2)}) %all-to-all-start.4) | async-done | bytes 65568 | tf_op jit(solution)/shard_map/all_to_all | solution.py:1052
  168.0 0.0 copy-start.4
  168.0 0.6 copy-done.4
  168.6 2.0 %update.1 = (f32[16,2048]{1,0:T(8,128)}, f32[16,2048]{1,0:T(8,128)}, f32[64,256]{1,0:T(8,128)}, f32[64,256]{1,0:T(8,128)}, f32[2,4]{1,0:T(2,128)}) custom-call(f32[16,8,128]{2,1,0:T(8,128)} %copy-done.4, f32[16,2048]{1,0:T(8,128)} %ww_ref.3, f32[16,2048]{1,0:T(8,128)} %get-tuple-element.78.wu_ref, f32[16,2048]{1,0:T(8,128)} %we_ref.1, f32[64,256]{1,0:T(8,128)} %dw_ref.3, ...), custom_call_target="tpu_custom_call" | custom-call | tf_op jit(solution)/shard_map/update/pallas_call | solution.py:1033
  (10 shorter events, 0.0 us)
Async XLA Ops:
  3.2 22.2 %all-to-all-start = ((bf16[16,16,896]{2,1,0:T(8,128)(2,1)}), bf16[16,16,896]{2,1,0:T(8,128)(2,1)S(1)}, u32[]{:S(2)}, u32[]{:S(2)}) async-start(bf16[16,16,896]{2,1,0:T(8,128)(2,1)} %broadcast_in_dim.6), calls=%async_computation | async-start | bytes 917504 | tf_op jit(solution)/shard_map/all_to_all | solution.py:1052
  25.4 5.8 %copy-start = (bf16[16,16,896]{2,1,0:T(8,128)(2,1)}, bf16[16,16,896]{2,1,0:T(8,128)(2,1)S(1)}, u32[]{:S(2)}) copy-start(bf16[16,16,896]{2,1,0:T(8,128)(2,1)S(1)} %all-to-all-done) | copy-start | bytes 1376260
  26.5 30.1 %all-to-all-start.1 = ((bf16[16,16,2304]{2,1,0:T(8,128)(2,1)}), bf16[16,16,2304]{2,1,0:T(8,128)(2,1)S(1)}, u32[]{:S(2)}, u32[]{:S(2)}) async-start(bf16[16,16,2304]{2,1,0:T(8,128)(2,1)} %broadcast_in_dim.7), calls=%async_computation.1 | async-start | bytes 2359296 | tf_op jit(solution)/shard_map/all_to_all | solution.py:1052
  30.5 0.7 copy-start.2
  56.6 1.3 copy-start.1
  92.2 38.0 %all-to-all-start.2 = ((bf16[16,16,2304]{2,1,0:T(8,128)(2,1)}), bf16[16,16,2304]{2,1,0:T(8,128)(2,1)S(1)}, u32[]{:S(2)}, u32[]{:S(2)}) async-start(bf16[16,16,2304]{2,1,0:T(8,128)(2,1)} %bitcast.20), calls=%async_computation.2 | async-start | bytes 2359296 | tf_op jit(solution)/shard_map/all_to_all | solution.py:1052
  130.2 18.9 %all-to-all-start.3 = ((bf16[16,16,896]{2,1,0:T(8,128)(2,1)}), bf16[16,16,896]{2,1,0:T(8,128)(2,1)S(1)}, u32[]{:S(2)}, u32[]{:S(2)}) async-start(bf16[16,16,896]{2,1,0:T(8,128)(2,1)} %bitcast.21), calls=%async_computation.3 | async-start | bytes 917504 | tf_op jit(solution)/shard_map/all_to_all | solution.py:1052
  137.1 24.1 %copy-start.8 = (f32[368]{0:T(512)S(1)}, f32[368]{0:T(512)}, u32[]{:S(2)}) copy-start(f32[368]{0:T(512)} %param.30) | copy-start | bytes 4420
  137.1 24.1 %copy-start.9 = (f32[368]{0:T(512)S(1)}, f32[368]{0:T(512)}, u32[]{:S(2)}) copy-start(f32[368]{0:T(512)} %param.33) | copy-start | bytes 4420
  137.1 24.1 %copy-start.10 = (f32[368]{0:T(512)S(1)}, f32[368]{0:T(512)}, u32[]{:S(2)}) copy-start(f32[368]{0:T(512)} %param.31) | copy-start | bytes 4420
  137.1 24.1 %copy-start.11 = (f32[368]{0:T(512)S(1)}, f32[368]{0:T(512)}, u32[]{:S(2)}) copy-start(f32[368]{0:T(512)} %param.32) | copy-start | bytes 4420
  147.4 3.1 %copy-start.3 = (f32[16,2304]{1,0:T(8,128)}, f32[16,2304]{1,0:T(8,128)S(1)}, u32[]{:S(2)}) copy-start(f32[16,2304]{1,0:T(8,128)S(1)} %convert_reduce_fusion.gl_ref) | copy-start | bytes 442372
  147.4 1.9 %collective-permute-start.1 = (f32[16,2304]{1,0:T(8,128)S(1)}, f32[16,2304]{1,0:T(8,128)S(1)}, u32[]{:S(2)}, u32[]{:S(2)}) collective-permute-start(f32[16,2304]{1,0:T(8,128)S(1)} %convert_reduce_fusion.gl_ref), channel_id=1, source_target_pairs={{0,16},{16,0},{1,17},{17,1},{2,18},{18,2},{3,19},{19,3},{4,20},{20... | collective-permute-start | bytes 442376 | tf_op jit(solution)/shard_map/ppermute | solution.py:1038
  149.2 1.3 copy-start.5
  149.2 1.3 collective-permute-start
  149.3 1.2 copy-start.6
  150.5 0.6 copy-start.7
  154.5 13.5 %all-to-all-start.4 = ((f32[16,8,128]{2,1,0:T(8,128)}), f32[16,8,128]{2,1,0:T(8,128)S(1)}, u32[]{:S(2)}, u32[]{:S(2)}) async-start(f32[16,8,128]{2,1,0:T(8,128)} %broadcast_in_dim.8), calls=%async_computation.4 | async-start | bytes 131072 | tf_op jit(solution)/shard_map/all_to_all | solution.py:1052
  168.0 0.6 copy-start.4

commit v5 on v4

--- a/solution.py
+++ b/solution.py
@@ -43,7 +43,7 @@
 COPIES = (3, 3, 2)
 TAPS = tuple((dy, dx) for dy in (-1, 0, 1) for dx in (-1, 0, 1))
 ORDER = (0, 2, 1, 3, 4, 5, 6)
-VMEM = 62 * 1024 * 1024
+VMEM = 60 * 1024 * 1024
 
 BF = jnp.bfloat16
 F32 = jnp.float32
@@ -227,21 +227,30 @@
 def pipelined(stages, order, extra=()):
     extra = dict(extra)
     state = {item: {} for item in order}
-    for turn in range(len(order) + len(stages) - 1):
+    for turn in range(len(order) + max(lag for lag, _ in stages)):
         if turn in extra:
             extra[turn]()
         running = []
-        for at, stage in enumerate(stages):
-            if 0 <= turn - at < len(order):
-                item = order[turn - at]
+        for lag, stage in stages:
+            if 0 <= turn - lag < len(order):
+                item = order[turn - lag]
                 running.append(stage(item, state[item]))
         while running:
             running = [stage for stage in running if next(stage, True) is None]
 
 
-def norm_kernel(x_ref, hat_ref):
+def norm_kernel(x_ref, wide_ref, down_ref, hat_ref, late_ref):
     for low in range(0, x_ref.shape[0], TOK_IMG // 5):
         hat_ref[low : low + TOK_IMG // 5, :] = normalise(x_ref[low : low + TOK_IMG // 5, :])[0]
+
+    @pl.when(pl.program_id(0) == 0)
+    def _():
+        rows = wide_ref.shape[0]
+        pieces = [wide_ref[:, 3 * D :]]
+        pieces += [down_ref[at : at + rows, :] for at in range(0, down_ref.shape[0], rows)]
+        late = jnp.concatenate(pieces, axis=1).astype(BF)
+        for owner in range(late_ref.shape[0]):
+            late_ref[owner] = late
 
 
 def attend_kernel(
@@ -365,7 +374,8 @@
 
     project(0)
     extra = {1: functools.partial(project, 1), 3: functools.partial(project, 2)}
-    pipelined((cut, score, soften, mix, put), ORDER, extra)
+    stages = enumerate((cut, score, soften, mix, put))
+    pipelined(tuple(stages), ORDER, extra)
     att_ref[0] = att_scr[...].astype(BF)
 
 
@@ -395,6 +405,11 @@
     return terms
 
 
+def down_blocks(shard):
+    parts = FF // D
+    return [(i, part, (i * parts + part) * shard) for i in range(D // shard) for part in range(parts)]
+
+
 def feed_kernel(
     shard,
     cnt_ref,
@@ -402,7 +417,6 @@
     c_ref,
     att_ref,
     w_ref,
-    down_ref,
     s_ref,
     out_ref,
     dx_ref,
@@ -417,6 +431,7 @@
     gout_scr,
     turn_scr,
     pack_scr,
+    down_scr,
 ):
     image = pl.program_id(0)
 
@@ -424,6 +439,12 @@
     def _():
         for ref in (gup_scr, gdn_scr, gout_scr, sums_ref, bup_ref):
             ref[...] = jnp.zeros_like(ref)
+        pack_scr[...] = w_ref[:, D + FF :].astype(F32)
+        for owner, part, low in down_blocks(shard):
+            turn_scr[low : low + shard, :] = pack_scr[
+                owner * shard : (owner + 1) * shard, part * D : (part + 1) * D
+            ]
+        down_scr[...] = turn_scr[...].astype(BF)
 
     bound = BIG + GRID_S * GRID_S * cnt_ref[image]
     bias_out, gain, shift = s_ref[15:16, :], s_ref[16:17, :], s_ref[17:18, :]
@@ -470,7 +491,7 @@
         held["v", part] = dot(held["h2"], w_ref[:, cols])
 
     def hidden_back(part):
-        held["dg", part] = dot_nt(held["dy"], down_ref[lanes_of[part], :])
+        held["dg", part] = dot_nt(held["dy"], down_scr[lanes_of[part], :])
 
     def gelu(part, at):
         own = slice(at, at + count)
@@ -497,10 +518,10 @@
     half = FF // 2
 
     def out_first():
-        held["out"] = dot(joined("g", 0, 1), down_ref[:half, :])
+        held["out"] = dot(joined("g", 0, 1), down_scr[:half, :])
 
     def out_last():
-        held["out"] += dot(joined("g", 2, 3), down_ref[half:, :])
+        held["out"] += dot(joined("g", 2, 3), down_scr[half:, :])
 
     def out_store(at):
         own = slice(at, at + count)
@@ -551,12 +572,10 @@
     @pl.when(image == pl.num_programs(0) - 1)
     def _():
         turn_scr[...] = gdn_scr[...].T * ROOT
-        for owner in range(D // shard):
-            for part in range(FF // D):
-                low = (owner * (FF // D) + part) * shard
-                pack_scr[owner * shard : (owner + 1) * shard, part * D : (part + 1) * D] = turn_scr[
-                    low : low + shard, :
-                ]
+        for owner, part, low in down_blocks(shard):
+            pack_scr[owner * shard : (owner + 1) * shard, part * D : (part + 1) * D] = turn_scr[
+                low : low + shard, :
+            ]
         bup_ref[...] *= 0.5
         bias = bup_ref[0:1, :]
         grad = gup_scr[...] * 0.5
@@ -601,6 +620,7 @@
     kern_scr,
     bias_scr,
     datt_scr,
+    grad_scr,
     turn_scr,
     pad_scr,
     back_scr,
@@ -636,6 +656,7 @@
             else:
                 low = first_of(pair, member)
                 grad = first_rows(datt_scr[low : low + QROWS, lanes], tokens_of(pair))
+            grad_scr[at * QROWS : (at + 1) * QROWS, :] = grad
             v = win_ref[0, at, :, 2 * HALF :]
             pad_scr[at, EDGE : EDGE + QROWS, :] = first_rows(v.astype(F32), tokens_of(pair))
             dn = grad * il_ref[0, at]
@@ -664,6 +685,8 @@
             q = win_ref[0, at, :, 0:HALF]
             k = jnp.concatenate([win_ref[0, at, :, HALF : 2 * HALF], none], axis=0)
             dq = dot(ds, by_head(k))
+            row = 2 * PAIRS * QROWS + 8 * at
+            grad_scr[row : row + 8, :] = dq[:8]
             q_t, dn_t = q.T, dn.T
             dk, dv = [], []
             for half in range(2):
@@ -672,7 +695,7 @@
                 for parts, left, right in ((dk, q_t, ds), (dv, dn_t, e)):
                     both = dot(left[own], right[:, lanes])
                     parts += [both[:HEAD, :WIN], both[HEAD:, WIN:]]
-            state[member] = dq, dk, dv, grad
+            state[member] = dq, dk, dv
             low = grad.astype(BF)
             taps.append(
                 jnp.concatenate([low * kernel[8 - tap : 9 - tap] for tap in range(9)], axis=0)
@@ -686,27 +709,28 @@
         broad = shape_of(kind)[1]
         for member in range(2):
             at = 2 * pair + member
-            grad = state[member][3]
-            sides = {0: grad}
-            if kind < 2:
-                for dx in (-1, 1):
-                    sides[dx] = grad * edge_ref[places[kind, 0, dx]]
-            for tap, (dy, dx) in enumerate(TAPS):
-                if kind < 2 or tap == 4:
-                    side = sides[dx]
-                else:
-                    side = grad * edge_ref[places[kind, dy, dx]]
-                start = EDGE + dy * broad + dx
-                kern_scr[branch_of(pair, member), tap] += fold(
-                    side * pad_scr[at, start : start + QROWS, :]
-                )
+            base = pl.multiple_of(at * QROWS + image // 4096 * 8, 8)
+            totals = [jnp.zeros((8, HALF), F32)] * 9
+            for low in range(0, tokens_of(pair), 8):
+                own = slice(low, low + 8)
+                grad = grad_scr[pl.ds(pl.multiple_of(base + low, 8), 8), :]
+                sides = {}
+                for tap, (dy, dx) in enumerate(TAPS):
+                    place = places.get((kind, 0 if kind < 2 else dy, dx))
+                    if place not in sides:
+                        mask = 1.0 if place is None else edge_ref[place, own, :]
+                        sides[place] = grad * mask
+                    start = EDGE + low + dy * broad + dx
+                    totals[tap] = totals[tap] + sides[place] * pad_scr[at, start : start + 8, :]
+            for tap in range(9):
+                kern_scr[branch_of(pair, member), tap] += totals[tap]
             yield
 
     def put(pair, state):
         for member in range(2):
             at = 2 * pair + member
             branch = branch_of(pair, member)
-            dq, dk, dv, _ = state[member]
+            dq, dk, dv = state[member]
             dk = jnp.concatenate(dk, axis=0).T[:QROWS] * LN2
             dv = jnp.concatenate(dv, axis=0).T[:QROWS]
             dv = dv + state[2][:, member * HALF : (member + 1) * HALF]
@@ -723,7 +747,7 @@
                     dqkv_scr[low : low + count, lanes] = piece[:count]
             yield
 
-    pipelined((weigh, score, spread, put, kernels), ORDER)
+    pipelined(((3, kernels), (0, weigh), (1, score), (2, spread), (3, put)), ORDER)
     dqkv = dqkv_scr[...].astype(BF)
     dqkv_ref[0] = dqkv
     both = dot(with_ones(hat_ref[0].T), dqkv)
@@ -781,9 +805,9 @@
     return pl.BlockSpec((TOK_IMG, D), lambda i, *_: (i, 0))
 
 
-def params():
+def params(room=0):
     return pltpu.CompilerParams(
-        vmem_limit_bytes=VMEM, dimension_semantics=("arbitrary",)
+        vmem_limit_bytes=VMEM - room * 1024 * 1024, dimension_semantics=("arbitrary",)
     )
 
 
@@ -797,18 +821,19 @@
     return rows, taps
 
 
-def run_norm(tokens_in):
+def run_norm(tokens_in, wide, down, count):
     rows = TOK_IMG * 2
     block = pl.BlockSpec((rows, D), lambda i: (i, 0))
+    late = (count, wide.shape[0], D + 2 * FF)
     return pl.pallas_call(
         norm_kernel,
         grid=(tokens_in.shape[0] // rows,),
-        in_specs=[block],
-        out_specs=block,
-        out_shape=sds(tokens_in.shape, F32),
+        in_specs=[block, whole(wide.shape), whole(down.shape)],
+        out_specs=[block, whole(late)],
+        out_shape=[sds(tokens_in.shape, F32), sds(late, BF)],
         compiler_params=params(),
         name="norm",
-    )(tokens_in)
+    )(tokens_in, wide, down)
 
 
 def run_attend(tokens_in, w_qkv, table, kernels, side):
@@ -840,7 +865,7 @@
     )(tokens_in, w_qkv, *consts)
 
 
-def run_feed(shard, counts, tokens_in, cotangent, att, wide, down, table):
+def run_feed(shard, counts, tokens_in, cotangent, att, wide, table):
     images = tokens_in.shape[0] // TOK_IMG
     return pl.pallas_call(
         functools.partial(feed_kernel, shard),
@@ -852,7 +877,6 @@
                 tokens(),
                 image_of((ROWS, D)),
                 whole(wide.shape),
-                whole(down.shape),
                 whole(table.shape),
             ],
             out_specs=[
@@ -871,6 +895,7 @@
                 pltpu.VMEM((D, D), F32),
                 pltpu.VMEM((FF, D), F32),
                 pltpu.VMEM((D, FF), F32),
+                pltpu.VMEM((FF, D), BF),
             ],
         ),
         out_shape=[
@@ -883,7 +908,7 @@
         ],
         compiler_params=params(),
         name="feed",
-    )(counts, tokens_in, cotangent, att, wide, down, table)
+    )(counts, tokens_in, cotangent, att, wide, table)
 
 
 def run_back(spans, blocks, w_qkv, table, kernels, sums, b_up, side):
@@ -901,6 +926,7 @@
             pltpu.VMEM((2, 9, 8, HALF), F32),
             pltpu.VMEM((8, 3 * D), F32),
             pltpu.VMEM((LONG, D), F32),
+            pltpu.VMEM((2 * PAIRS * (QROWS + 8), HALF), F32),
             pltpu.VMEM((4, QROWS, HALF), F32),
             pltpu.VMEM((2 * PAIRS, QROWS + 2 * EDGE, HALF), F32),
             pltpu.VMEM((4, 3, QROWS, HALF), F32),
@@ -1030,18 +1056,12 @@
 
 
 def plain(kernel, name, out_shape, *operands):
-    return pl.pallas_call(kernel, out_shape=out_shape, compiler_params=pltpu.CompilerParams(
-        vmem_limit_bytes=VMEM), name=name)(*operands)
+    small = pltpu.CompilerParams(vmem_limit_bytes=8 * 1024 * 1024)
+    return pl.pallas_call(kernel, out_shape=out_shape, compiler_params=small, name=name)(*operands)
 
 
 def to_other(values):
     return lax.ppermute(values, "dp", [(0, 1), (1, 0)])
-
-
-def side_by_side(wide, down):
-    rows = wide.shape[0]
-    blocks = [down[at : at + rows] for at in range(0, down.shape[0], rows)]
-    return jnp.concatenate([wide] + blocks, axis=1)
 
 
 def copies(values, count):
@@ -1076,23 +1096,19 @@
 ):
     rows = wide_w.shape[0]
     narrow = small_p.shape[0] // rows
-    wide_low = wide_w.astype(BF)
     small_low = jnp.pad(small_p.astype(BF).reshape(rows, narrow), ((0, 0), (0, HALF - narrow)))
-    first = jnp.concatenate([wide_low[:, : 3 * D], small_low], axis=1)
+    first = jnp.concatenate([wide_w[:, : 3 * D].astype(BF), small_low], axis=1)
     first = send_terms(copies(first, count), count)
-    late_all = copies(side_by_side(wide_low[:, 3 * D :], down_w.astype(BF)), count)
-    hat = run_norm(tokens_in)
+    hat, late_all = run_norm(tokens_in, wide_w, down_w, count)
     first, late_all, hat = lax.optimization_barrier((first, late_all, hat))
     first = first.reshape(D, -1)
     late_all = send_terms(late_all, count).reshape(D, -1)
-    down_all = late_all[:, D + FF :].reshape(count, rows, FF // D, D)
-    down_all = down_all.transpose(0, 2, 1, 3).reshape(FF, D)
     table, kernels = small_tables(first[:, 3 * D : 3 * D + narrow].astype(F32).reshape(-1))
     side = np.stack([tap_matrix(kind) for kind in range(3)])
     side = bf(side.transpose(0, 2, 1, 3).reshape(3, QROWS, 9 * QROWS))
     hat, att, win, e, il, o = run_attend(hat, first, table, kernels, side)
     block_out, dx, datt, g_late, sums, b_up = run_feed(
-        rows, crop_count, tokens_in, cotangent, att, late_all, down_all, table
+        rows, crop_count, tokens_in, cotangent, att, late_all, table
     )
     late = send_terms(g_late, count)
     spans = small_spans(rows, narrow)

time: 172 us -> 164 us (0.953)
  Pallas kernels: 114 us -> 111 us
  local copies, waits for them, and re-layouts: 6.82 us -> 4.29 us
  other arithmetic: 4.09 us -> 1.62 us
    pallas_call x2, Pallas kernels: 4.11 us -> 1.77 us  [plain(): pl.pallas_call(kernel, out_shape=out_shape, compiler_params=small, name=n...]
    broadcast_in_dim x3 -> x2, local copies, waits for them, and re-layouts: 3.28 us -> 1.46 us  [copies(): return jnp.broadcast_to(values[None], (count,) + values.shape)]
    convert_element_type x2 -> x0, other arithmetic: 1.76 us -> none  [the longest x1 0.91 us: on_device(): wide_low = wide_w.astype(BF)]
  transfers between devices with their start and end apart: 7 -> 7, of which waited for: 5 -> 5; matrix products, arithmetic and copies ran while one was open for 2% -> 1% of each run, Pallas kernels for 44% -> 46%
where the time goes in v5:
time: 164 us; the launch traced here: 163 us
  Pallas kernels  111 us (68%)
  starting transfers between devices  30.9 us (19%)
  waiting for transfers between devices  14.7 us (9%)
  local copies, waits for them, and re-layouts  4.29 us (3%)
    pallas_call x1, Pallas kernels, run_feed(): pl.pallas_call(functools.partial(feed_kernel, shard), grid_spec=pltpu.Pre...  34.2 us
    all_to_all x5, starting transfers between devices, send_terms(): lax.all_to_all(values.reshape(count, -1, values.shape[-1]), 'fsdp', 0, 0)  30.8 us
    pallas_call x1, Pallas kernels, run_back(): pl.pallas_call(functools.partial(back_kernel, spans, places), grid=(image...  30.4 us
    pallas_call x1, Pallas kernels, run_attend(): pl.pallas_call(attend_kernel, grid=(images,), in_specs=[tokens(), whole(w...  22.1 us
    pallas_call x2, Pallas kernels, run_input(): pl.pallas_call(input_kernel, grid=(high - low,), in_specs=[own, rows, own...  14.7 us
    all_to_all x5, waiting for transfers between devices, send_terms(): lax.all_to_all(values.reshape(count, -1, values.shape[-1]), 'fsdp', 0, 0)  13.4 us
    pallas_call x1, Pallas kernels, run_norm(): pl.pallas_call(norm_kernel, grid=(tokens_in.shape[0] // rows,), in_specs=...  7.53 us
  transfers between devices with their start and end apart: 7, of which 5 were waited for; matrix products, arithmetic and copies ran while one was open for 1% of the time, Pallas kernels for 46%

profile of v5, /device:TPU:0, one launch (start us, length us, event | category | flops | bytes accessed | tf_op | source)
XLA Modules:
  0.0 163.1 jit_solution(723496604476997479)
XLA Ops:
  0.6 0.8 slice.28
  1.4 0.7 convert_element_type.13
  2.1 0.1 reshape.53
  2.2 0.8 broadcast_in_dim.4
  3.1 8.3 %all-to-all-start = ((bf16[16,16,896]{2,1,0:T(8,128)(2,1)}), bf16[16,16,896]{2,1,0:T(8,128)(2,1)S(1)}, u32[]{:S(2)}, u32[]{:S(2)}) async-start(bf16[16,16,896]{2,1,0:T(8,128)(2,1)} %broadcast_in_dim.4), calls=%async_computation | async-start | bytes 917504 | tf_op jit(solution)/shard_map/all_to_all | solution.py:1072
  11.4 7.5 %norm.1 = (f32[5440,256]{1,0:T(8,128)}, bf16[16,16,2304]{2,1,0:T(8,128)(2,1)}) custom-call(f32[5440,256]{1,0:T(8,128)} %x_ref.7, f32[16,2048]{1,0:T(8,128)} %ww_ref.3, f32[64,256]{1,0:T(8,128)} %dw_ref.3), custom_call_target="tpu_custom_call" | custom-call | tf_op jit(solution)/shard_map/norm/pallas_call | solution.py:828
  18.9 6.3 %all-to-all-done = bf16[16,16,896]{2,1,0:T(8,128)(2,1)S(1)} async-done(((bf16[16,16,896]{2,1,0:T(8,128)(2,1)}), bf16[16,16,896]{2,1,0:T(8,128)(2,1)S(1)}, u32[]{:S(2)}, u32[]{:S(2)}) %all-to-all-start) | async-done | bytes 458784 | tf_op jit(solution)/shard_map/all_to_all | solution.py:1072
  25.3 0.0 copy-start.8
  25.3 3.8 %all-to-all-start.1 = ((bf16[16,16,2304]{2,1,0:T(8,128)(2,1)}), bf16[16,16,2304]{2,1,0:T(8,128)(2,1)S(1)}, u32[]{:S(2)}, u32[]{:S(2)}) async-start(bf16[16,16,2304]{2,1,0:T(8,128)(2,1)} %get-tuple-element.59), calls=%async_computation.1 | async-start | bytes 2359296 | tf_op jit(solution)/shard_map/all_to_all | solution.py:1072
  29.0 0.2 reshape.60.s_ref
  29.3 0.0 copy-start.10
  29.3 0.6 copy.38
  29.9 0.0 copy-done.8
  29.9 0.0 copy-done.10
  29.9 22.1 %attend.1 = (bf16[8,688,256]{2,1,0:T(8,128)(2,1)}, bf16[8,688,256]{2,1,0:T(8,128)(2,1)}, bf16[8,14,112,384]{3,2,1,0:T(8,128)(2,1)}, bf16[8,14,112,512]{3,2,1,0:T...) custom-call(f32[5440,256]{1,0:T(8,128)} %get-tuple-element.56.x_ref, ...), custom_call_target="tpu_custom_call" | custom-call | tf_op jit(solution)/shard_map/attend/pallas_call | solution.py:851
  52.0 3.3 %all-to-all-done.1 = bf16[16,16,2304]{2,1,0:T(8,128)(2,1)S(1)} async-done(((bf16[16,16,2304]{2,1,0:T(8,128)(2,1)}), bf16[16,16,2304]{2,1,0:T(8,128)(2,1)S(1)}, u32[]{:S(2)}, u32[]{:S(2)}) %all-to-all-start.1) | async-done | bytes 1179680 | tf_op jit(solution)/shard_map/all_to_all | solution.py:1072
  55.3 0.0 copy-start.9
  55.3 1.0 copy-done.9
  56.3 34.2 %feed.1 = (f32[5440,256]{1,0:T(8,128)}, f32[5440,256]{1,0:T(8,128)}, bf16[8,688,256]{2,1,0:T(8,128)(2,1)}, bf16[256,2304]{1,0:T(8,128)(2,1)}, f32[5,8,256]{2,1,0:T(8,128)}, /*index=5*/f32[8,1024]{1,0:T(8,128)}) custom-call(s32[8]{0:T(128)} %cnt_ref.1, f32[5440,256]{1,0:T(8,128)} %x_ref.7, f32[5440,256]{1,0:T(8,128)} %c_ref.1, ...), custom_call_target="tpu_custom_call" | custom-call | tf_op jit(solution)/shard_map/feed/pallas_call | solution.py:870
  90.5 6.1 %all-to-all-start.2 = ((bf16[16,16,2304]{2,1,0:T(8,128)(2,1)}), bf16[16,16,2304]{2,1,0:T(8,128)(2,1)S(1)}, u32[]{:S(2)}, u32[]{:S(2)}) async-start(bf16[16,16,2304]{2,1,0:T(8,128)(2,1)} %bitcast.15), calls=%async_computation.2 | async-start | bytes 2359296 | tf_op jit(solution)/shard_map/all_to_all | solution.py:1072
  96.6 30.4 %back.1 = (bf16[8,688,768]{2,1,0:T(8,128)(2,1)}, bf16[256,896]{1,0:T(8,128)(2,1)}) custom-call(bf16[8,688,256]{2,1,0:T(8,128)(2,1)} %get-tuple-element.62.datt_ref, bf16[8,14,112,384]{3,2,1,0:T(8,128)(2,1)} %get-tuple-element.63.win_ref, bf16[8,14,112,512]{3,2,1,0:T(8,128)(2,1)} %get-tuple-element.64.e_ref, f32[8,14,112,128]{3,2,1,0:T(8,128)} %get-tuple-element.65.il_ref, ...), custom_call_target="tpu_custom_call" | custom-call | tf_op jit(solution)/shard_map/back/pallas_call | solution.py:918
  127.1 0.0 all-to-all-done.2
  127.1 6.9 %all-to-all-start.3 = ((bf16[16,16,896]{2,1,0:T(8,128)(2,1)}), bf16[16,16,896]{2,1,0:T(8,128)(2,1)S(1)}, u32[]{:S(2)}, u32[]{:S(2)}) async-start(bf16[16,16,896]{2,1,0:T(8,128)(2,1)} %bitcast.16), calls=%async_computation.3 | async-start | bytes 917504 | tf_op jit(solution)/shard_map/all_to_all | solution.py:1072
  134.0 0.0 copy-start
  134.0 0.0 copy-start.1
  134.0 0.0 copy-start.2
  134.0 0.0 copy-start.3
  134.1 0.0 copy-start.6
  134.1 0.0 copy-start.7
  134.1 0.0 copy-start.11
  134.1 0.0 copy-start.12
  134.1 0.0 copy-start.13
  134.1 0.0 copy-start.14
  134.1 10.3 %input_grad.2.out_refs_0_ = f32[5440,256]{1,0:T(8,128)} custom-call(f32[5440,256]{1,0:T(8,128)} %x_ref.7, bf16[8,688,768]{2,1,0:T(8,128)(2,1)} %get-tuple-element.72.dqkv_ref, f32[5440,256]{1,0:T(8,128)} %get-tuple-element.73.dx_ref, bf16[256,896]{1,0:T(8,128)(2,1)} %bitcast.12, f32[23,256]{1,0:T(8,128)} %copy-done.10), custom_call_target="tpu_custom_call" | custom-call | flops 1623195648 | bytes 19021824 | tf_op jit(solution)/shard_map/input_grad/pallas_call | solution.py:946
  144.4 0.2 convert_reduce_fusion.gl_ref
  144.6 0.1 collective-permute-start.1
  144.7 1.4 all-to-all-done.3
  146.0 0.1 convert_reduce_fusion.1.gq_ref
  146.1 0.1 collective-permute-start
  146.2 0.0 collective-permute-done.1.gl_other_ref
  146.2 1.2 collective-permute-done.gq_other_ref
  147.4 0.0 copy-done
  147.4 0.0 copy-done.1
  147.4 0.0 copy-done.2
  147.4 0.0 copy-done.3
  147.4 0.0 copy-done.6
  147.4 0.0 copy-done.7
  147.4 0.9 moment.1
  148.3 0.6 broadcast_in_dim.5
  148.9 5.7 %all-to-all-start.4 = ((f32[16,8,128]{2,1,0:T(8,128)}), f32[16,8,128]{2,1,0:T(8,128)S(1)}, u32[]{:S(2)}, u32[]{:S(2)}) async-start(f32[16,8,128]{2,1,0:T(8,128)} %broadcast_in_dim.5), calls=%async_computation.4 | async-start | bytes 131072 | tf_op jit(solution)/shard_map/all_to_all | solution.py:1072
  154.7 0.0 copy-done.11
  154.7 0.0 copy-done.12
  154.7 0.0 copy-done.13
  154.7 0.0 copy-done.14
  154.7 0.7 multiply_add_fusion
  155.4 0.0 copy-start.4
  155.4 0.0 copy-start.5
  155.4 4.4 %input_grad.3 = f32[5440,256]{1,0:T(8,128)} custom-call(f32[5440,256]{1,0:T(8,128)} %x_ref.7, bf16[8,688,768]{2,1,0:T(8,128)(2,1)} %get-tuple-element.72.dqkv_ref, f32[5440,256]{1,0:T(8,128)} %get-tuple-element.73.dx_ref, bf16[256,896]{1,0:T(8,128)(2,1)} %bitcast.13, f32[23,256]{1,0:T(8,128)} %copy-done.10, ...), custom_call_target="tpu_custom_call", output_to_operand_aliasing={{}: (5, {})} | custom-call | flops 541065216 | bytes 6340608 | tf_op jit(solution)/shard_map/input_grad/pallas_call | solution.py:946
  159.7 2.4 %all-to-all-done.4.sq_ref = f32[16,8,128]{2,1,0:T(8,128)S(1)} async-done(((f32[16,8,128]{2,1,0:T(8,128)}), f32[16,8,128]{2,1,0:T(8,128)S(1)}, u32[]{:S(2)}, u32[]{:S(2)}) %all-to-all-start.4) | async-done | bytes 65568 | tf_op jit(solution)/shard_map/all_to_all | solution.py:1072
  162.2 0.0 copy-done.4
  162.2 0.0 copy-done.5
  162.2 0.9 update.1
  (5 shorter events, 0.0 us)
Async XLA Ops:
  3.1 22.2 %all-to-all-start = ((bf16[16,16,896]{2,1,0:T(8,128)(2,1)}), bf16[16,16,896]{2,1,0:T(8,128)(2,1)S(1)}, u32[]{:S(2)}, u32[]{:S(2)}) async-start(bf16[16,16,896]{2,1,0:T(8,128)(2,1)} %broadcast_in_dim.4), calls=%async_computation | async-start | bytes 917504 | tf_op jit(solution)/shard_map/all_to_all | solution.py:1072
  25.3 4.6 %copy-start.8 = (bf16[16,16,896]{2,1,0:T(8,128)(2,1)}, bf16[16,16,896]{2,1,0:T(8,128)(2,1)S(1)}, u32[]{:S(2)}) copy-start(bf16[16,16,896]{2,1,0:T(8,128)(2,1)S(1)} %all-to-all-done) | copy-start | bytes 1376260
  25.3 30.1 %all-to-all-start.1 = ((bf16[16,16,2304]{2,1,0:T(8,128)(2,1)}), bf16[16,16,2304]{2,1,0:T(8,128)(2,1)S(1)}, u32[]{:S(2)}, u32[]{:S(2)}) async-start(bf16[16,16,2304]{2,1,0:T(8,128)(2,1)} %get-tuple-element.59), calls=%async_computation.1 | async-start | bytes 2359296 | tf_op jit(solution)/shard_map/all_to_all | solution.py:1072
  29.3 0.7 copy-start.10
  55.3 1.0 copy-start.9
  90.5 36.6 %all-to-all-start.2 = ((bf16[16,16,2304]{2,1,0:T(8,128)(2,1)}), bf16[16,16,2304]{2,1,0:T(8,128)(2,1)S(1)}, u32[]{:S(2)}, u32[]{:S(2)}) async-start(bf16[16,16,2304]{2,1,0:T(8,128)(2,1)} %bitcast.15), calls=%async_computation.2 | async-start | bytes 2359296 | tf_op jit(solution)/shard_map/all_to_all | solution.py:1072
  127.1 18.9 %all-to-all-start.3 = ((bf16[16,16,896]{2,1,0:T(8,128)(2,1)}), bf16[16,16,896]{2,1,0:T(8,128)(2,1)S(1)}, u32[]{:S(2)}, u32[]{:S(2)}) async-start(bf16[16,16,896]{2,1,0:T(8,128)(2,1)} %bitcast.16), calls=%async_computation.3 | async-start | bytes 917504 | tf_op jit(solution)/shard_map/all_to_all | solution.py:1072
  134.0 13.4 %copy-start = (f32[16,2048]{1,0:T(8,128)S(1)}, f32[16,2048]{1,0:T(8,128)}, u32[]{:S(2)}) copy-start(f32[16,2048]{1,0:T(8,128)} %ww_ref.3) | copy-start | bytes 393220
  134.0 13.4 %copy-start.1 = (f32[64,256]{1,0:T(8,128)S(1)}, f32[64,256]{1,0:T(8,128)}, u32[]{:S(2)}) copy-start(f32[64,256]{1,0:T(8,128)} %dw_ref.3) | copy-start | bytes 196612
  134.0 13.4 %copy-start.2 = (f32[16,2048]{1,0:T(8,128)S(1)}, f32[16,2048]{1,0:T(8,128)}, u32[]{:S(2)}) copy-start(f32[16,2048]{1,0:T(8,128)} %wm_ref.1) | copy-start | bytes 393220
  134.0 13.4 %copy-start.3 = (f32[16,2048]{1,0:T(8,128)S(1)}, f32[16,2048]{1,0:T(8,128)}, u32[]{:S(2)}) copy-start(f32[16,2048]{1,0:T(8,128)} %wv_ref.1) | copy-start | bytes 393220
  134.1 13.4 %copy-start.6 = (f32[64,256]{1,0:T(8,128)S(1)}, f32[64,256]{1,0:T(8,128)}, u32[]{:S(2)}) copy-start(f32[64,256]{1,0:T(8,128)} %dm_ref.1) | copy-start | bytes 196612
  134.1 13.4 %copy-start.7 = (f32[64,256]{1,0:T(8,128)S(1)}, f32[64,256]{1,0:T(8,128)}, u32[]{:S(2)}) copy-start(f32[64,256]{1,0:T(8,128)} %dv_ref.1) | copy-start | bytes 196612
  134.1 20.6 %copy-start.11 = (f32[368]{0:T(512)S(1)}, f32[368]{0:T(512)}, u32[]{:S(2)}) copy-start(f32[368]{0:T(512)} %param.30) | copy-start | bytes 4420
  134.1 20.6 %copy-start.12 = (f32[368]{0:T(512)S(1)}, f32[368]{0:T(512)}, u32[]{:S(2)}) copy-start(f32[368]{0:T(512)} %param.33) | copy-start | bytes 4420
  134.1 20.6 %copy-start.13 = (f32[368]{0:T(512)S(1)}, f32[368]{0:T(512)}, u32[]{:S(2)}) copy-start(f32[368]{0:T(512)} %param.31) | copy-start | bytes 4420
  134.1 20.6 %copy-start.14 = (f32[368]{0:T(512)S(1)}, f32[368]{0:T(512)}, u32[]{:S(2)}) copy-start(f32[368]{0:T(512)} %param.32) | copy-start | bytes 4420
  144.6 1.6 collective-permute-start.1
  146.1 1.3 collective-permute-start
  148.9 13.2 %all-to-all-start.4 = ((f32[16,8,128]{2,1,0:T(8,128)}), f32[16,8,128]{2,1,0:T(8,128)S(1)}, u32[]{:S(2)}, u32[]{:S(2)}) async-start(f32[16,8,128]{2,1,0:T(8,128)} %broadcast_in_dim.5), calls=%async_computation.4 | async-start | bytes 131072 | tf_op jit(solution)/shard_map/all_to_all | solution.py:1072
  155.4 6.8 %copy-start.4 = (f32[16,2048]{1,0:T(8,128)S(1)}, f32[16,2048]{1,0:T(8,128)}, u32[]{:S(2)}) copy-start(f32[16,2048]{1,0:T(8,128)} %we_ref.1) | copy-start | bytes 393220
  155.4 6.8 %copy-start.5 = (f32[64,256]{1,0:T(8,128)S(1)}, f32[64,256]{1,0:T(8,128)}, u32[]{:S(2)}) copy-start(f32[64,256]{1,0:T(8,128)} %de_ref.1) | copy-start | bytes 196612

commit v6 on v5

--- a/solution.py
+++ b/solution.py
@@ -860,7 +860,7 @@
             pltpu.VMEM((4, QROWS, HALF), F32),
             pltpu.VMEM((ROWS, D), F32),
         ],
-        compiler_params=params(),
+        compiler_params=params(-3),
         name="attend",
     )(tokens_in, w_qkv, *consts)
 
@@ -1098,11 +1098,15 @@
     narrow = small_p.shape[0] // rows
     small_low = jnp.pad(small_p.astype(BF).reshape(rows, narrow), ((0, 0), (0, HALF - narrow)))
     first = jnp.concatenate([wide_w[:, : 3 * D].astype(BF), small_low], axis=1)
-    first = send_terms(copies(first, count), count)
+    core = lax.axis_index("dp")
+    half = lax.dynamic_slice_in_dim(first, core * (rows // 2), rows // 2, axis=0)
+    half = send_terms(copies(half, count), count)
     hat, late_all = run_norm(tokens_in, wide_w, down_w, count)
-    first, late_all, hat = lax.optimization_barrier((first, late_all, hat))
-    first = first.reshape(D, -1)
+    half, late_all, hat = lax.optimization_barrier((half, late_all, hat))
     late_all = send_terms(late_all, count).reshape(D, -1)
+    other = to_other(half)
+    first = [jnp.where(core == at, half, other) for at in range(2)]
+    first = jnp.stack(first, axis=1).reshape(D, -1)
     table, kernels = small_tables(first[:, 3 * D : 3 * D + narrow].astype(F32).reshape(-1))
     side = np.stack([tap_matrix(kind) for kind in range(3)])
     side = bf(side.transpose(0, 2, 1, 3).reshape(3, QROWS, 9 * QROWS))

time: 164 us -> 160 us (0.976)
  waiting for transfers between devices: 14.7 us -> 10.6 us
    all_to_all x5, waiting for transfers between devices: 13.4 us -> 7.9 us  [send_terms(): lax.all_to_all(values.reshape(count, -1, values.shape[-1]), 'fsdp', 0, 0)]
  transfers between devices with their start and end apart: 7 -> 8, of which waited for: 5 -> 6; matrix products, arithmetic and copies ran while one was open for 1% -> 1% of each run, Pallas kernels for 46% -> 47%
where the time goes in v6:
time: 160 us; the launch traced here: 159 us
  Pallas kernels  111 us (69%)
  starting transfers between devices  32 us (20%)
  waiting for transfers between devices  10.6 us (7%)
  local copies, waits for them, and re-layouts  3.14 us (2%)
  other arithmetic  1.72 us (1%)
    pallas_call x1, Pallas kernels, run_feed(): pl.pallas_call(functools.partial(feed_kernel, shard), grid_spec=pltpu.Pre...  34.2 us
    all_to_all x5, starting transfers between devices, send_terms(): lax.all_to_all(values.reshape(count, -1, values.shape[-1]), 'fsdp', 0, 0)  31.8 us
    pallas_call x1, Pallas kernels, run_back(): pl.pallas_call(functools.partial(back_kernel, spans, places), grid=(image...  30.5 us
    pallas_call x1, Pallas kernels, run_attend(): pl.pallas_call(attend_kernel, grid=(images,), in_specs=[tokens(), whole(w...  22 us
    pallas_call x2, Pallas kernels, run_input(): pl.pallas_call(input_kernel, grid=(high - low,), in_specs=[own, rows, own...  14.6 us
    all_to_all x5, waiting for transfers between devices, send_terms(): lax.all_to_all(values.reshape(count, -1, values.shape[-1]), 'fsdp', 0, 0)  7.9 us
    pallas_call x1, Pallas kernels, run_norm(): pl.pallas_call(norm_kernel, grid=(tokens_in.shape[0] // rows,), in_specs=...  7.53 us
  transfers between devices with their start and end apart: 8, of which 6 were waited for; matrix products, arithmetic and copies ran while one was open for 1% of the time, Pallas kernels for 47%

profile of v6, /device:TPU:0, one launch (start us, length us, event | category | flops | bytes accessed | tf_op | source)
XLA Modules:
  0.0 159.0 jit_solution(13185576699688163205)
XLA Ops:
  0.6 0.7 convert_element_type.13
  1.3 0.1 reshape.53
  1.4 0.8 slice.28
  2.2 0.7 broadcast_in_dim.4
  3.0 8.3 %all-to-all-start = ((bf16[16,8,896]{2,1,0:T(8,128)(2,1)}), bf16[16,8,896]{2,1,0:T(8,128)(2,1)S(1)}, u32[]{:S(2)}, u32[]{:S(2)}) async-start(bf16[16,8,896]{2,1,0:T(8,128)(2,1)} %broadcast_in_dim.4), calls=%async_computation | async-start | bytes 458752 | tf_op jit(solution)/shard_map/all_to_all | solution.py:1072
  11.3 7.5 %norm.1 = (f32[5440,256]{1,0:T(8,128)}, bf16[16,16,2304]{2,1,0:T(8,128)(2,1)}) custom-call(f32[5440,256]{1,0:T(8,128)} %x_ref.7, f32[16,2048]{1,0:T(8,128)} %ww_ref.3, f32[64,256]{1,0:T(8,128)} %dw_ref.3), custom_call_target="tpu_custom_call" | custom-call | tf_op jit(solution)/shard_map/norm/pallas_call | solution.py:828
  18.8 1.7 %all-to-all-done = bf16[16,8,896]{2,1,0:T(8,128)(2,1)S(1)} async-done(((bf16[16,8,896]{2,1,0:T(8,128)(2,1)}), bf16[16,8,896]{2,1,0:T(8,128)(2,1)S(1)}, u32[]{:S(2)}, u32[]{:S(2)}) %all-to-all-start) | async-done | bytes 229408 | tf_op jit(solution)/shard_map/all_to_all | solution.py:1072
  20.5 5.2 %all-to-all-start.1 = ((bf16[16,16,2304]{2,1,0:T(8,128)(2,1)}), bf16[16,16,2304]{2,1,0:T(8,128)(2,1)}, u32[]{:S(2)}, u32[]{:S(2)}) async-start(bf16[16,16,2304]{2,1,0:T(8,128)(2,1)} %get-tuple-element.59), calls=%async_computation.1 | async-start | bytes 2359296 | tf_op jit(solution)/shard_map/all_to_all | solution.py:1072
  25.8 0.1 collective-permute-start
  25.9 1.5 collective-permute-done
  27.4 0.1 pad_maximum_fusion
  27.4 0.0 copy-start.8
  27.5 0.2 reshape.60.s_ref
  27.7 0.0 copy-start.9
  27.7 0.6 copy.41
  28.3 0.0 copy-done.8
  28.3 0.0 copy-done.9
  28.3 22.0 %attend.1 = (bf16[8,688,256]{2,1,0:T(8,128)(2,1)}, bf16[8,688,256]{2,1,0:T(8,128)(2,1)}, bf16[8,14,112,384]{3,2,1,0:T(8,128)(2,1)}, bf16[8,14,112,512]{3,2,1,0:T...) custom-call(f32[5440,256]{1,0:T(8,128)} %get-tuple-element.56.x_ref, ...), custom_call_target="tpu_custom_call" | custom-call | tf_op jit(solution)/shard_map/attend/pallas_call | solution.py:851
  50.4 1.9 %all-to-all-done.1 = bf16[16,16,2304]{2,1,0:T(8,128)(2,1)} async-done(((bf16[16,16,2304]{2,1,0:T(8,128)(2,1)}), bf16[16,16,2304]{2,1,0:T(8,128)(2,1)}, u32[]{:S(2)}, u32[]{:S(2)}) %all-to-all-start.1) | async-done | bytes 1179680 | tf_op jit(solution)/shard_map/all_to_all | solution.py:1072
  52.3 34.2 %feed.1 = (f32[5440,256]{1,0:T(8,128)}, f32[5440,256]{1,0:T(8,128)}, bf16[8,688,256]{2,1,0:T(8,128)(2,1)}, bf16[256,2304]{1,0:T(8,128)(2,1)}, f32[5,8,256]{2,1,0:T(8,128)}, /*index=5*/f32[8,1024]{1,0:T(8,128)}) custom-call(s32[8]{0:T(128)} %cnt_ref.1, f32[5440,256]{1,0:T(8,128)} %x_ref.7, f32[5440,256]{1,0:T(8,128)} %c_ref.1, ...), custom_call_target="tpu_custom_call" | custom-call | tf_op jit(solution)/shard_map/feed/pallas_call | solution.py:870
  86.4 6.1 %all-to-all-start.2 = ((bf16[16,16,2304]{2,1,0:T(8,128)(2,1)}), bf16[16,16,2304]{2,1,0:T(8,128)(2,1)S(1)}, u32[]{:S(2)}, u32[]{:S(2)}) async-start(bf16[16,16,2304]{2,1,0:T(8,128)(2,1)} %bitcast.20), calls=%async_computation.2 | async-start | bytes 2359296 | tf_op jit(solution)/shard_map/all_to_all | solution.py:1072
  92.5 30.5 %back.1 = (bf16[8,688,768]{2,1,0:T(8,128)(2,1)}, bf16[256,896]{1,0:T(8,128)(2,1)}) custom-call(bf16[8,688,256]{2,1,0:T(8,128)(2,1)} %get-tuple-element.62.datt_ref, bf16[8,14,112,384]{3,2,1,0:T(8,128)(2,1)} %get-tuple-element.63.win_ref, bf16[8,14,112,512]{3,2,1,0:T(8,128)(2,1)} %get-tuple-element.64.e_ref, f32[8,14,112,128]{3,2,1,0:T(8,128)} %get-tuple-element.65.il_ref, ...), custom_call_target="tpu_custom_call" | custom-call | tf_op jit(solution)/shard_map/back/pallas_call | solution.py:918
  123.0 0.0 all-to-all-done.2
  123.0 6.9 %all-to-all-start.3 = ((bf16[16,16,896]{2,1,0:T(8,128)(2,1)}), bf16[16,16,896]{2,1,0:T(8,128)(2,1)S(1)}, u32[]{:S(2)}, u32[]{:S(2)}) async-start(bf16[16,16,896]{2,1,0:T(8,128)(2,1)} %bitcast.21), calls=%async_computation.3 | async-start | bytes 917504 | tf_op jit(solution)/shard_map/all_to_all | solution.py:1072
  129.9 0.0 copy-start
  129.9 0.0 copy-start.1
  129.9 0.0 copy-start.2
  130.0 0.0 copy-start.3
  130.0 0.0 copy-start.6
  130.0 0.0 copy-start.7
  130.0 0.0 copy-start.10
  130.0 0.0 copy-start.11
  130.0 0.0 copy-start.12
  130.0 0.0 copy-start.13
  130.0 10.3 %input_grad.2.out_refs_0_ = f32[5440,256]{1,0:T(8,128)} custom-call(f32[5440,256]{1,0:T(8,128)} %x_ref.7, bf16[8,688,768]{2,1,0:T(8,128)(2,1)} %get-tuple-element.72.dqkv_ref, f32[5440,256]{1,0:T(8,128)} %get-tuple-element.73.dx_ref, bf16[256,896]{1,0:T(8,128)(2,1)} %bitcast.18, f32[23,256]{1,0:T(8,128)} %copy-done.9), custom_call_target="tpu_custom_call" | custom-call | flops 1623195648 | bytes 19021824 | tf_op jit(solution)/shard_map/input_grad/pallas_call | solution.py:946
  140.3 0.2 convert_reduce_fusion.gl_ref
  140.5 0.1 collective-permute-start.2
  140.6 1.9 %all-to-all-done.3 = bf16[16,16,896]{2,1,0:T(8,128)(2,1)S(1)} async-done(((bf16[16,16,896]{2,1,0:T(8,128)(2,1)}), bf16[16,16,896]{2,1,0:T(8,128)(2,1)S(1)}, u32[]{:S(2)}, u32[]{:S(2)}) %all-to-all-start.3) | async-done | bytes 458784 | tf_op jit(solution)/shard_map/all_to_all | solution.py:1072
  142.4 0.1 convert_reduce_fusion.1.gq_ref
  142.5 0.1 collective-permute-start.1
  142.6 0.0 collective-permute-done.2.gl_other_ref
  142.6 1.2 collective-permute-done.1.gq_other_ref
  143.8 0.0 copy-done
  143.8 0.0 copy-done.1
  143.8 0.0 copy-done.2
  143.8 0.0 copy-done.3
  143.8 0.0 copy-done.6
  143.8 0.0 copy-done.7
  143.8 0.9 moment.1
  144.7 0.6 broadcast_in_dim.5
  145.3 5.2 %all-to-all-start.4 = ((f32[16,8,128]{2,1,0:T(8,128)}), f32[16,8,128]{2,1,0:T(8,128)S(1)}, u32[]{:S(2)}, u32[]{:S(2)}) async-start(f32[16,8,128]{2,1,0:T(8,128)} %broadcast_in_dim.5), calls=%async_computation.4 | async-start | bytes 131072 | tf_op jit(solution)/shard_map/all_to_all | solution.py:1072
  150.6 0.0 copy-done.10
  150.6 0.0 copy-done.11
  150.6 0.0 copy-done.12
  150.6 0.0 copy-done.13
  150.6 0.7 multiply_add_fusion
  151.3 0.0 copy-start.4
  151.3 0.0 copy-start.5
  151.3 4.4 %input_grad.3 = f32[5440,256]{1,0:T(8,128)} custom-call(f32[5440,256]{1,0:T(8,128)} %x_ref.7, bf16[8,688,768]{2,1,0:T(8,128)(2,1)} %get-tuple-element.72.dqkv_ref, f32[5440,256]{1,0:T(8,128)} %get-tuple-element.73.dx_ref, bf16[256,896]{1,0:T(8,128)(2,1)} %bitcast.19, f32[23,256]{1,0:T(8,128)} %copy-done.9, ...), custom_call_target="tpu_custom_call", output_to_operand_aliasing={{}: (5, {})} | custom-call | flops 541065216 | bytes 6340608 | tf_op jit(solution)/shard_map/input_grad/pallas_call | solution.py:946
  155.7 2.4 %all-to-all-done.4.sq_ref = f32[16,8,128]{2,1,0:T(8,128)S(1)} async-done(((f32[16,8,128]{2,1,0:T(8,128)}), f32[16,8,128]{2,1,0:T(8,128)S(1)}, u32[]{:S(2)}, u32[]{:S(2)}) %all-to-all-start.4) | async-done | bytes 65568 | tf_op jit(solution)/shard_map/all_to_all | solution.py:1072
  158.1 0.0 copy-done.4
  158.1 0.0 copy-done.5
  158.1 0.9 update.1
  (6 shorter events, 0.1 us)
Async XLA Ops:
  3.0 17.6 %all-to-all-start = ((bf16[16,8,896]{2,1,0:T(8,128)(2,1)}), bf16[16,8,896]{2,1,0:T(8,128)(2,1)S(1)}, u32[]{:S(2)}, u32[]{:S(2)}) async-start(bf16[16,8,896]{2,1,0:T(8,128)(2,1)} %broadcast_in_dim.4), calls=%async_computation | async-start | bytes 458752 | tf_op jit(solution)/shard_map/all_to_all | solution.py:1072
  20.5 31.7 %all-to-all-start.1 = ((bf16[16,16,2304]{2,1,0:T(8,128)(2,1)}), bf16[16,16,2304]{2,1,0:T(8,128)(2,1)}, u32[]{:S(2)}, u32[]{:S(2)}) async-start(bf16[16,16,2304]{2,1,0:T(8,128)(2,1)} %get-tuple-element.59), calls=%async_computation.1 | async-start | bytes 2359296 | tf_op jit(solution)/shard_map/all_to_all | solution.py:1072
  25.8 1.6 collective-permute-start
  27.4 0.9 copy-start.8
  27.7 0.7 copy-start.9
  86.4 36.6 %all-to-all-start.2 = ((bf16[16,16,2304]{2,1,0:T(8,128)(2,1)}), bf16[16,16,2304]{2,1,0:T(8,128)(2,1)S(1)}, u32[]{:S(2)}, u32[]{:S(2)}) async-start(bf16[16,16,2304]{2,1,0:T(8,128)(2,1)} %bitcast.20), calls=%async_computation.2 | async-start | bytes 2359296 | tf_op jit(solution)/shard_map/all_to_all | solution.py:1072
  123.0 19.4 %all-to-all-start.3 = ((bf16[16,16,896]{2,1,0:T(8,128)(2,1)}), bf16[16,16,896]{2,1,0:T(8,128)(2,1)S(1)}, u32[]{:S(2)}, u32[]{:S(2)}) async-start(bf16[16,16,896]{2,1,0:T(8,128)(2,1)} %bitcast.21), calls=%async_computation.3 | async-start | bytes 917504 | tf_op jit(solution)/shard_map/all_to_all | solution.py:1072
  129.9 13.9 %copy-start = (f32[16,2048]{1,0:T(8,128)S(1)}, f32[16,2048]{1,0:T(8,128)}, u32[]{:S(2)}) copy-start(f32[16,2048]{1,0:T(8,128)} %ww_ref.3) | copy-start | bytes 393220
  129.9 13.9 %copy-start.1 = (f32[64,256]{1,0:T(8,128)S(1)}, f32[64,256]{1,0:T(8,128)}, u32[]{:S(2)}) copy-start(f32[64,256]{1,0:T(8,128)} %dw_ref.3) | copy-start | bytes 196612
  129.9 13.9 %copy-start.2 = (f32[16,2048]{1,0:T(8,128)S(1)}, f32[16,2048]{1,0:T(8,128)}, u32[]{:S(2)}) copy-start(f32[16,2048]{1,0:T(8,128)} %wm_ref.1) | copy-start | bytes 393220
  130.0 13.9 %copy-start.3 = (f32[16,2048]{1,0:T(8,128)S(1)}, f32[16,2048]{1,0:T(8,128)}, u32[]{:S(2)}) copy-start(f32[16,2048]{1,0:T(8,128)} %wv_ref.1) | copy-start | bytes 393220
  130.0 13.9 %copy-start.6 = (f32[64,256]{1,0:T(8,128)S(1)}, f32[64,256]{1,0:T(8,128)}, u32[]{:S(2)}) copy-start(f32[64,256]{1,0:T(8,128)} %dm_ref.1) | copy-start | bytes 196612
  130.0 13.9 %copy-start.7 = (f32[64,256]{1,0:T(8,128)S(1)}, f32[64,256]{1,0:T(8,128)}, u32[]{:S(2)}) copy-start(f32[64,256]{1,0:T(8,128)} %dv_ref.1) | copy-start | bytes 196612
  130.0 20.6 %copy-start.10 = (f32[368]{0:T(512)S(1)}, f32[368]{0:T(512)}, u32[]{:S(2)}) copy-start(f32[368]{0:T(512)} %param.30) | copy-start | bytes 4420
  130.0 20.6 %copy-start.11 = (f32[368]{0:T(512)S(1)}, f32[368]{0:T(512)}, u32[]{:S(2)}) copy-start(f32[368]{0:T(512)} %param.33) | copy-start | bytes 4420
  130.0 20.6 %copy-start.12 = (f32[368]{0:T(512)S(1)}, f32[368]{0:T(512)}, u32[]{:S(2)}) copy-start(f32[368]{0:T(512)} %param.31) | copy-start | bytes 4420
  130.0 20.6 %copy-start.13 = (f32[368]{0:T(512)S(1)}, f32[368]{0:T(512)}, u32[]{:S(2)}) copy-start(f32[368]{0:T(512)} %param.32) | copy-start | bytes 4420
  140.5 2.1 %collective-permute-start.2 = (f32[16,2304]{1,0:T(8,128)S(1)}, f32[16,2304]{1,0:T(8,128)S(1)}, u32[]{:S(2)}, u32[]{:S(2)}) collective-permute-start(f32[16,2304]{1,0:T(8,128)S(1)} %convert_reduce_fusion.gl_ref), channel_id=1, source_target_pairs={{0,16},{16,0},{1,17},{17,1},{2,18},{18,2},{3,19},{19,3},{4,20},{20... | collective-permute-start | bytes 442376 | tf_op jit(solution)/shard_map/ppermute | solution.py:1064
  142.5 1.3 collective-permute-start.1
  145.3 12.8 %all-to-all-start.4 = ((f32[16,8,128]{2,1,0:T(8,128)}), f32[16,8,128]{2,1,0:T(8,128)S(1)}, u32[]{:S(2)}, u32[]{:S(2)}) async-start(f32[16,8,128]{2,1,0:T(8,128)} %broadcast_in_dim.5), calls=%async_computation.4 | async-start | bytes 131072 | tf_op jit(solution)/shard_map/all_to_all | solution.py:1072
  151.3 6.8 %copy-start.4 = (f32[16,2048]{1,0:T(8,128)S(1)}, f32[16,2048]{1,0:T(8,128)}, u32[]{:S(2)}) copy-start(f32[16,2048]{1,0:T(8,128)} %we_ref.1) | copy-start | bytes 393220
  151.3 6.8 %copy-start.5 = (f32[64,256]{1,0:T(8,128)S(1)}, f32[64,256]{1,0:T(8,128)}, u32[]{:S(2)}) copy-start(f32[64,256]{1,0:T(8,128)} %de_ref.1) | copy-start | bytes 196612

commit v7 on v6

--- a/solution.py
+++ b/solution.py
@@ -210,6 +210,10 @@
     )
 
 
+def taps_of(table, branch):
+    return table[5:14, branch * HALF : (branch + 1) * HALF]
+
+
 def first_rows(values, count):
     low = count // 16 * 16
     if low >= values.shape[0]:
@@ -257,7 +261,6 @@
     x_ref,
     w_ref,
     s_ref,
-    k_ref,
     tap_ref,
     mrow_ref,
     mkey_ref,
@@ -341,7 +344,7 @@
         taps = []
         for member in range(2):
             v, e = state[member]
-            low = k_ref[branch_of(pair, member)].astype(BF)
+            low = taps_of(s_ref, branch_of(pair, member)).astype(BF)
             keys = jnp.concatenate([v, none], axis=0)
             state[member] = dot(e, jnp.concatenate([by_head(keys), ones], axis=1))
             taps.append(jnp.concatenate([v * low[tap : tap + 1] for tap in range(9)], axis=0))
@@ -360,7 +363,7 @@
             il_ref[0, at] = inv
             o_ref[0, at] = o.astype(BF)
             conv = state[2][:, member * HALF : (member + 1) * HALF]
-            piece = o + k_ref[branch, 9:10, :] + conv
+            piece = o + s_ref[14:15, lanes] + conv
             if kind_of(pair) == 1:
                 back_scr[at - 4] = piece
                 for source, target in pieces_of(pair, member):
@@ -609,7 +612,6 @@
     hat_ref,
     w_ref,
     s_ref,
-    k_ref,
     feed_ref,
     bup_ref,
     tap_ref,
@@ -681,7 +683,7 @@
         for member in range(2):
             grad, dn, ds, e = state[member]
             at = 2 * pair + member
-            kernel = k_ref[branch_of(pair, member)].astype(BF)
+            kernel = taps_of(s_ref, branch_of(pair, member)).astype(BF)
             q = win_ref[0, at, :, 0:HALF]
             k = jnp.concatenate([win_ref[0, at, :, HALF : 2 * HALF], none], axis=0)
             dq = dot(ds, by_head(k))
@@ -815,12 +817,6 @@
     return jax.ShapeDtypeStruct(shape, dtype)
 
 
-def small_tables(small):
-    rows = small.reshape(-1, D)
-    taps = rows[5:15].reshape(10, 2, HALF).transpose(1, 0, 2)
-    return rows, taps
-
-
 def run_norm(tokens_in, wide, down, count):
     rows = TOK_IMG * 2
     block = pl.BlockSpec((rows, D), lambda i: (i, 0))
@@ -836,10 +832,10 @@
     )(tokens_in, wide, down)
 
 
-def run_attend(tokens_in, w_qkv, table, kernels, side):
+def run_attend(tokens_in, w_qkv, table, side):
     images = tokens_in.shape[0] // TOK_IMG
     mrow, mkey = mask_operands()
-    consts = [table, kernels, side, bf(mrow), bf(mkey)]
+    consts = [table, side, bf(mrow), bf(mkey)]
     outs = [
         ((ROWS, D), BF),
         ((ROWS, D), BF),
@@ -911,10 +907,10 @@
     )(counts, tokens_in, cotangent, att, wide, table)
 
 
-def run_back(spans, blocks, w_qkv, table, kernels, sums, b_up, side):
+def run_back(spans, blocks, w_qkv, table, sums, b_up, side):
     images = blocks[0].shape[0]
     masks, places = edge_masks()
-    consts = [w_qkv, table, kernels, sums, b_up, side, jnp.asarray(masks)]
+    consts = [w_qkv, table, sums, b_up, side, jnp.asarray(masks)]
     return pl.pallas_call(
         functools.partial(back_kernel, spans, places),
         grid=(images,),
@@ -998,6 +994,7 @@
     df_ref,
     ds_ref,
     du_ref,
+    copies_ref,
     sq_ref,
 ):
     for lanes, own, other in (
@@ -1021,6 +1018,7 @@
         for at, lanes in enumerate(MATRICES):
             sq_ref[base + at : base + at + 1, :] = lane_sums(wide[:, lanes])
         sq_ref[base + 3 : base + 4, :] = lane_sums(down[...])
+    copies_ref[...] = jnp.broadcast_to(sq_ref[...][None], copies_ref.shape)
 
 
 def update_kernel(
@@ -1055,9 +1053,15 @@
     da_ref[...] = keep * de_ref[...] + (1.0 - keep) * new
 
 
-def plain(kernel, name, out_shape, *operands):
+def plain(kernel, name, out_shape, *operands, scratch=()):
     small = pltpu.CompilerParams(vmem_limit_bytes=8 * 1024 * 1024)
-    return pl.pallas_call(kernel, out_shape=out_shape, compiler_params=small, name=name)(*operands)
+    return pl.pallas_call(
+        kernel,
+        out_shape=out_shape,
+        scratch_shapes=scratch,
+        compiler_params=small,
+        name=name,
+    )(*operands)
 
 
 def to_other(values):
@@ -1107,37 +1111,39 @@
     other = to_other(half)
     first = [jnp.where(core == at, half, other) for at in range(2)]
     first = jnp.stack(first, axis=1).reshape(D, -1)
-    table, kernels = small_tables(first[:, 3 * D : 3 * D + narrow].astype(F32).reshape(-1))
+    table = first[:, 3 * D : 3 * D + narrow].astype(F32).reshape(-1, D)
     side = np.stack([tap_matrix(kind) for kind in range(3)])
     side = bf(side.transpose(0, 2, 1, 3).reshape(3, QROWS, 9 * QROWS))
-    hat, att, win, e, il, o = run_attend(hat, first, table, kernels, side)
+    hat, att, win, e, il, o = run_attend(hat, first, table, side)
     block_out, dx, datt, g_late, sums, b_up = run_feed(
         rows, crop_count, tokens_in, cotangent, att, late_all, table
     )
     late = send_terms(g_late, count)
     spans = small_spans(rows, narrow)
     dqkv, g_last = run_back(
-        spans, [datt, win, e, il, o, hat], first, table, kernels, sums, b_up, side
+        spans, [datt, win, e, il, o, hat], first, table, sums, b_up, side
     )
     late, g_last = lax.optimization_barrier((late, g_last))
     late = add_terms(late)
     last = send_terms(g_last, count)
+    late_other = to_other(late)
+    late_other, dqkv = lax.optimization_barrier((late_other, dqkv))
     images = dqkv.shape[0]
-    begin = images * 3 // 4
+    begin = images * 5 // 8
     grad_in = run_input(tokens_in, dqkv, dx, first, table, 0, begin)
     last, grad_in = lax.optimization_barrier((last, grad_in))
     last = add_terms(last)
     last_other = to_other(last)
-    late_other = to_other(late)
     wide_like, down_like = sds(wide_w.shape, F32), sds(down_w.shape, F32)
     wide_first, wide_second, wide_upd, down_first, down_second, down_upd, squares = plain(
         moment_kernel,
         "moment",
-        [wide_like] * 3 + [down_like] * 3 + [sds((8, HALF), F32)],
+        [wide_like] * 3 + [down_like] * 3 + [sds((count, 8, HALF), F32)],
         *(last, last_other, late, late_other),
         *(wide_w, wide_m, wide_v, down_w, down_m, down_v),
+        scratch=[pltpu.VMEM((8, HALF), F32)],
     )
-    squares, grad_in = lax.optimization_barrier((copies(squares, count), grad_in))
+    squares, grad_in = lax.optimization_barrier((squares, grad_in))
     squares = send_terms(squares, count)
     grad_in = run_input(tokens_in, dqkv, dx, first, table, begin, images, grad_in)
     squares, grad_in = lax.optimization_barrier((squares, grad_in))

time: 160 us -> 159 us (level)
    all_to_all x5, waiting for transfers between devices: 7.9 us -> 5.28 us  [send_terms(): lax.all_to_all(values.reshape(count, -1, values.shape[-1]), 'fsdp', 0, 0)]
  transfers between devices with their start and end apart: 8 -> 8, of which waited for: 6 -> 7; matrix products, arithmetic and copies ran while one was open for 1% -> 1% of each run, Pallas kernels for 47% -> 48%
where the time goes in v7:
time: 159 us; the launch traced here: 158 us
  Pallas kernels  112 us (70%)
  starting transfers between devices  32.2 us (20%)
  waiting for transfers between devices  9.32 us (6%)
  local copies, waits for them, and re-layouts  2.49 us (2%)
  other arithmetic  1.72 us (1%)
    pallas_call x1, Pallas kernels, run_feed(): pl.pallas_call(functools.partial(feed_kernel, shard), grid_spec=pltpu.Pre...  34.1 us
    all_to_all x5, starting transfers between devices, send_terms(): lax.all_to_all(values.reshape(count, -1, values.shape[-1]), 'fsdp', 0, 0)  32 us
    pallas_call x1, Pallas kernels, run_back(): pl.pallas_call(functools.partial(back_kernel, spans, places), grid=(image...  30.2 us
    pallas_call x1, Pallas kernels, run_attend(): pl.pallas_call(attend_kernel, grid=(images,), in_specs=[tokens(), whole(w...  22.1 us
    pallas_call x2, Pallas kernels, run_input(): pl.pallas_call(input_kernel, grid=(high - low,), in_specs=[own, rows, own...  15.9 us
    pallas_call x1, Pallas kernels, run_norm(): pl.pallas_call(norm_kernel, grid=(tokens_in.shape[0] // rows,), in_specs=...  7.53 us
    all_to_all x5, waiting for transfers between devices, send_terms(): lax.all_to_all(values.reshape(count, -1, values.shape[-1]), 'fsdp', 0, 0)  5.28 us
    ppermute x3, waiting for transfers between devices, to_other(): return lax.ppermute(values, 'dp', [(0, 1), (1, 0)])  4.04 us
  transfers between devices with their start and end apart: 8, of which 7 were waited for; matrix products, arithmetic and copies ran while one was open for 1% of the time, Pallas kernels for 48%

profile of v7, /device:TPU:0, one launch (start us, length us, event | category | flops | bytes accessed | tf_op | source)
XLA Modules:
  0.0 158.5 jit_solution(15344899794110837411)
XLA Ops:
  0.6 0.7 convert_element_type.13
  1.3 0.1 reshape.54
  1.4 0.8 slice.23
  2.2 0.7 broadcast_in_dim.2
  3.0 8.3 %all-to-all-start = ((bf16[16,8,896]{2,1,0:T(8,128)(2,1)}), bf16[16,8,896]{2,1,0:T(8,128)(2,1)S(1)}, u32[]{:S(2)}, u32[]{:S(2)}) async-start(bf16[16,8,896]{2,1,0:T(8,128)(2,1)} %broadcast_in_dim.2), calls=%async_computation | async-start | bytes 458752 | tf_op jit(solution)/shard_map/all_to_all | solution.py:1076
  11.3 7.5 %norm.1 = (f32[5440,256]{1,0:T(8,128)}, bf16[16,16,2304]{2,1,0:T(8,128)(2,1)}) custom-call(f32[5440,256]{1,0:T(8,128)} %x_ref.7, f32[16,2048]{1,0:T(8,128)} %ww_ref.3, f32[64,256]{1,0:T(8,128)} %dw_ref.3), custom_call_target="tpu_custom_call" | custom-call | tf_op jit(solution)/shard_map/norm/pallas_call | solution.py:824
  18.8 1.7 %all-to-all-done = bf16[16,8,896]{2,1,0:T(8,128)(2,1)S(1)} async-done(((bf16[16,8,896]{2,1,0:T(8,128)(2,1)}), bf16[16,8,896]{2,1,0:T(8,128)(2,1)S(1)}, u32[]{:S(2)}, u32[]{:S(2)}) %all-to-all-start) | async-done | bytes 229408 | tf_op jit(solution)/shard_map/all_to_all | solution.py:1076
  20.5 5.2 %all-to-all-start.1 = ((bf16[16,16,2304]{2,1,0:T(8,128)(2,1)}), bf16[16,16,2304]{2,1,0:T(8,128)(2,1)}, u32[]{:S(2)}, u32[]{:S(2)}) async-start(bf16[16,16,2304]{2,1,0:T(8,128)(2,1)} %get-tuple-element.61), calls=%async_computation.1 | async-start | bytes 2359296 | tf_op jit(solution)/shard_map/all_to_all | solution.py:1076
  25.8 0.1 collective-permute-start
  25.9 1.5 collective-permute-done
  27.4 0.1 pad_maximum_fusion
  27.5 0.0 copy-start.8
  27.5 0.8 reshape.63.s_ref
  28.3 0.0 copy-done.8
  28.3 22.1 %attend.1 = (bf16[8,688,256]{2,1,0:T(8,128)(2,1)}, bf16[8,688,256]{2,1,0:T(8,128)(2,1)}, bf16[8,14,112,384]{3,2,1,0:T(8,128)(2,1)}, bf16[8,14,112,512]{3,2,1,0:T...) custom-call(f32[5440,256]{1,0:T(8,128)} %get-tuple-element.58.x_ref, ...), custom_call_target="tpu_custom_call" | custom-call | tf_op jit(solution)/shard_map/attend/pallas_call | solution.py:847
  50.5 1.8 %all-to-all-done.1 = bf16[16,16,2304]{2,1,0:T(8,128)(2,1)} async-done(((bf16[16,16,2304]{2,1,0:T(8,128)(2,1)}), bf16[16,16,2304]{2,1,0:T(8,128)(2,1)}, u32[]{:S(2)}, u32[]{:S(2)}) %all-to-all-start.1) | async-done | bytes 1179680 | tf_op jit(solution)/shard_map/all_to_all | solution.py:1076
  52.3 34.1 %feed.1 = (f32[5440,256]{1,0:T(8,128)}, f32[5440,256]{1,0:T(8,128)}, bf16[8,688,256]{2,1,0:T(8,128)(2,1)}, bf16[256,2304]{1,0:T(8,128)(2,1)}, f32[5,8,256]{2,1,0:T(8,128)}, /*index=5*/f32[8,1024]{1,0:T(8,128)}) custom-call(s32[8]{0:T(128)} %cnt_ref.1, f32[5440,256]{1,0:T(8,128)} %x_ref.7, f32[5440,256]{1,0:T(8,128)} %c_ref.1, ...), custom_call_target="tpu_custom_call" | custom-call | tf_op jit(solution)/shard_map/feed/pallas_call | solution.py:866
  86.4 6.1 %all-to-all-start.2 = ((bf16[16,16,2304]{2,1,0:T(8,128)(2,1)}), bf16[16,16,2304]{2,1,0:T(8,128)(2,1)S(1)}, u32[]{:S(2)}, u32[]{:S(2)}) async-start(bf16[16,16,2304]{2,1,0:T(8,128)(2,1)} %bitcast.17), calls=%async_computation.2 | async-start | bytes 2359296 | tf_op jit(solution)/shard_map/all_to_all | solution.py:1076
  92.5 30.2 %back.1 = (bf16[8,688,768]{2,1,0:T(8,128)(2,1)}, bf16[256,896]{1,0:T(8,128)(2,1)}) custom-call(bf16[8,688,256]{2,1,0:T(8,128)(2,1)} %get-tuple-element.64.datt_ref, bf16[8,14,112,384]{3,2,1,0:T(8,128)(2,1)} %get-tuple-element.65.win_ref, bf16[8,14,112,512]{3,2,1,0:T(8,128)(2,1)} %get-tuple-element.66.e_ref, f32[8,14,112,128]{3,2,1,0:T(8,128)} %get-tuple-element.67.il_ref, ...), custom_call_target="tpu_custom_call" | custom-call | tf_op jit(solution)/shard_map/back/pallas_call | solution.py:914
  122.8 0.0 all-to-all-done.2
  122.8 6.9 %all-to-all-start.3 = ((bf16[16,16,896]{2,1,0:T(8,128)(2,1)}), bf16[16,16,896]{2,1,0:T(8,128)(2,1)S(1)}, u32[]{:S(2)}, u32[]{:S(2)}) async-start(bf16[16,16,896]{2,1,0:T(8,128)(2,1)} %bitcast.18), calls=%async_computation.3 | async-start | bytes 917504 | tf_op jit(solution)/shard_map/all_to_all | solution.py:1076
  129.7 0.2 convert_reduce_fusion.gl_ref
  129.9 0.1 collective-permute-start.1
  130.0 1.4 collective-permute-done.1.gl_other_ref
  131.3 0.0 copy-start
  131.3 0.0 copy-start.1
  131.3 0.0 copy-start.2
  131.3 0.0 copy-start.3
  131.3 0.0 copy-start.6
  131.3 0.0 copy-start.7
  131.3 0.0 copy-start.9
  131.4 0.0 copy-start.10
  131.4 0.0 copy-start.11
  131.4 0.0 copy-start.12
  131.4 9.4 %input_grad.2.out_refs_0_ = f32[5440,256]{1,0:T(8,128)} custom-call(f32[5440,256]{1,0:T(8,128)} %x_ref.7, bf16[8,688,768]{2,1,0:T(8,128)(2,1)} %get-tuple-element.76.dqkv_ref, f32[5440,256]{1,0:T(8,128)} %get-tuple-element.77.dx_ref, bf16[256,896]{1,0:T(8,128)(2,1)} %bitcast.15, f32[23,256]{1,0:T(8,128)} %reshape.63.s_ref), custom_call_target="tpu_custom_call" | custom-call | flops 1352663040 | bytes 15851520 | tf_op jit(solution)/shard_map/input_grad/pallas_call | solution.py:942
  140.8 1.5 all-to-all-done.3
  142.3 0.1 convert_reduce_fusion.1.gq_ref
  142.3 0.1 collective-permute-start.2
  142.4 1.2 collective-permute-done.2.gq_other_ref
  143.7 0.0 copy-done
  143.7 0.0 copy-done.1
  143.7 0.0 copy-done.2
  143.7 0.0 copy-done.3
  143.7 0.0 copy-done.6
  143.7 0.0 copy-done.7
  143.7 0.9 moment.1
  144.6 5.5 %all-to-all-start.4 = ((f32[16,8,128]{2,1,0:T(8,128)}), f32[16,8,128]{2,1,0:T(8,128)S(1)}, u32[]{:S(2)}, u32[]{:S(2)}) async-start(f32[16,8,128]{2,1,0:T(8,128)} %get-tuple-element.82), calls=%async_computation.4 | async-start | bytes 131072 | tf_op jit(solution)/shard_map/all_to_all | solution.py:1076
  150.1 0.0 copy-done.9
  150.1 0.0 copy-done.10
  150.1 0.0 copy-done.11
  150.1 0.0 copy-done.12
  150.1 0.7 multiply_add_fusion
  150.8 0.0 copy-start.4
  150.8 0.0 copy-start.5
  150.8 6.5 %input_grad.3 = f32[5440,256]{1,0:T(8,128)} custom-call(f32[5440,256]{1,0:T(8,128)} %x_ref.7, bf16[8,688,768]{2,1,0:T(8,128)(2,1)} %get-tuple-element.76.dqkv_ref, f32[5440,256]{1,0:T(8,128)} %get-tuple-element.77.dx_ref, bf16[256,896]{1,0:T(8,128)(2,1)} %bitcast.16, f32[23,256]{1,0:T(8,128)} %reshape.63.s_ref, ...), custom_call_target="tpu_custom_call", output_to_operand_aliasing={{}: (5, {})} | custom-call | flops 811597824 | bytes 9510912 | tf_op jit(solution)/shard_map/input_grad/pallas_call | solution.py:942
  157.3 0.3 all-to-all-done.4.sq_ref
  157.6 0.0 copy-done.4
  157.6 0.0 copy-done.5
  157.6 0.9 update.1
  (4 shorter events, 0.1 us)
Async XLA Ops:
  3.0 17.6 %all-to-all-start = ((bf16[16,8,896]{2,1,0:T(8,128)(2,1)}), bf16[16,8,896]{2,1,0:T(8,128)(2,1)S(1)}, u32[]{:S(2)}, u32[]{:S(2)}) async-start(bf16[16,8,896]{2,1,0:T(8,128)(2,1)} %broadcast_in_dim.2), calls=%async_computation | async-start | bytes 458752 | tf_op jit(solution)/shard_map/all_to_all | solution.py:1076
  20.5 31.7 %all-to-all-start.1 = ((bf16[16,16,2304]{2,1,0:T(8,128)(2,1)}), bf16[16,16,2304]{2,1,0:T(8,128)(2,1)}, u32[]{:S(2)}, u32[]{:S(2)}) async-start(bf16[16,16,2304]{2,1,0:T(8,128)(2,1)} %get-tuple-element.61), calls=%async_computation.1 | async-start | bytes 2359296 | tf_op jit(solution)/shard_map/all_to_all | solution.py:1076
  25.8 1.6 collective-permute-start
  27.5 0.8 copy-start.8
  86.4 36.4 %all-to-all-start.2 = ((bf16[16,16,2304]{2,1,0:T(8,128)(2,1)}), bf16[16,16,2304]{2,1,0:T(8,128)(2,1)S(1)}, u32[]{:S(2)}, u32[]{:S(2)}) async-start(bf16[16,16,2304]{2,1,0:T(8,128)(2,1)} %bitcast.17), calls=%async_computation.2 | async-start | bytes 2359296 | tf_op jit(solution)/shard_map/all_to_all | solution.py:1076
  122.8 19.5 %all-to-all-start.3 = ((bf16[16,16,896]{2,1,0:T(8,128)(2,1)}), bf16[16,16,896]{2,1,0:T(8,128)(2,1)S(1)}, u32[]{:S(2)}, u32[]{:S(2)}) async-start(bf16[16,16,896]{2,1,0:T(8,128)(2,1)} %bitcast.18), calls=%async_computation.3 | async-start | bytes 917504 | tf_op jit(solution)/shard_map/all_to_all | solution.py:1076
  129.9 1.4 collective-permute-start.1
  131.3 12.3 %copy-start = (f32[16,2048]{1,0:T(8,128)S(1)}, f32[16,2048]{1,0:T(8,128)}, u32[]{:S(2)}) copy-start(f32[16,2048]{1,0:T(8,128)} %ww_ref.3) | copy-start | bytes 393220
  131.3 12.3 %copy-start.1 = (f32[64,256]{1,0:T(8,128)S(1)}, f32[64,256]{1,0:T(8,128)}, u32[]{:S(2)}) copy-start(f32[64,256]{1,0:T(8,128)} %dw_ref.3) | copy-start | bytes 196612
  131.3 12.3 %copy-start.2 = (f32[16,2048]{1,0:T(8,128)S(1)}, f32[16,2048]{1,0:T(8,128)}, u32[]{:S(2)}) copy-start(f32[16,2048]{1,0:T(8,128)} %wm_ref.1) | copy-start | bytes 393220
  131.3 12.4 %copy-start.3 = (f32[16,2048]{1,0:T(8,128)S(1)}, f32[16,2048]{1,0:T(8,128)}, u32[]{:S(2)}) copy-start(f32[16,2048]{1,0:T(8,128)} %wv_ref.1) | copy-start | bytes 393220
  131.3 12.4 %copy-start.6 = (f32[64,256]{1,0:T(8,128)S(1)}, f32[64,256]{1,0:T(8,128)}, u32[]{:S(2)}) copy-start(f32[64,256]{1,0:T(8,128)} %dm_ref.1) | copy-start | bytes 196612
  131.3 12.4 %copy-start.7 = (f32[64,256]{1,0:T(8,128)S(1)}, f32[64,256]{1,0:T(8,128)}, u32[]{:S(2)}) copy-start(f32[64,256]{1,0:T(8,128)} %dv_ref.1) | copy-start | bytes 196612
  131.3 18.7 %copy-start.9 = (f32[368]{0:T(512)S(1)}, f32[368]{0:T(512)}, u32[]{:S(2)}) copy-start(f32[368]{0:T(512)} %param.30) | copy-start | bytes 4420
  131.4 18.7 %copy-start.10 = (f32[368]{0:T(512)S(1)}, f32[368]{0:T(512)}, u32[]{:S(2)}) copy-start(f32[368]{0:T(512)} %param.33) | copy-start | bytes 4420
  131.4 18.7 %copy-start.11 = (f32[368]{0:T(512)S(1)}, f32[368]{0:T(512)}, u32[]{:S(2)}) copy-start(f32[368]{0:T(512)} %param.31) | copy-start | bytes 4420
  131.4 18.7 %copy-start.12 = (f32[368]{0:T(512)S(1)}, f32[368]{0:T(512)}, u32[]{:S(2)}) copy-start(f32[368]{0:T(512)} %param.32) | copy-start | bytes 4420
  142.3 1.3 collective-permute-start.2
  144.6 13.0 %all-to-all-start.4 = ((f32[16,8,128]{2,1,0:T(8,128)}), f32[16,8,128]{2,1,0:T(8,128)S(1)}, u32[]{:S(2)}, u32[]{:S(2)}) async-start(f32[16,8,128]{2,1,0:T(8,128)} %get-tuple-element.82), calls=%async_computation.4 | async-start | bytes 131072 | tf_op jit(solution)/shard_map/all_to_all | solution.py:1076
  150.8 6.8 %copy-start.4 = (f32[16,2048]{1,0:T(8,128)S(1)}, f32[16,2048]{1,0:T(8,128)}, u32[]{:S(2)}) copy-start(f32[16,2048]{1,0:T(8,128)} %we_ref.1) | copy-start | bytes 393220
  150.8 6.8 %copy-start.5 = (f32[64,256]{1,0:T(8,128)S(1)}, f32[64,256]{1,0:T(8,128)}, u32[]{:S(2)}) copy-start(f32[64,256]{1,0:T(8,128)} %de_ref.1) | copy-start | bytes 196612

commit v8 on v7

--- a/solution.py
+++ b/solution.py
@@ -35,8 +35,6 @@
 HEADS = 4
 SCALE = HEAD**-0.5
 LOG2E = 1.4426950408889634
-LN2 = 0.6931471805599453
-ROOT = 2**-0.5
 CHUNKS = ((0, 240), (240, 464), (464, 688))
 LONG = 744
 EDGE = 16
@@ -193,21 +191,19 @@
     return jnp.concatenate([first, second], axis=0)
 
 
-def by_two_heads(left, other, turned, added):
+def by_two_heads(left, other, turned, added, rest=None):
     low, high = lane_half(False), lane_half(True)
-    first = dot(
-        left * low + other[0], jnp.concatenate([two_heads(turned, 0), added], axis=0)
-    )
-    second = dot(
-        left * high + other[1], jnp.concatenate([added, two_heads(turned, 1)], axis=0)
-    )
+    none = jnp.zeros_like(added)
+    first = [two_heads(turned, 0), added, none, added]
+    second = [added, two_heads(turned, 1), added, none]
+    lefts = [left * low + other[0], left * high + other[1]]
+    if rest is None:
+        first, second = first[:2], second[:2]
+    else:
+        lefts = [jnp.concatenate([part, rest], axis=1) for part in lefts]
+    first = dot(lefts[0], jnp.concatenate(first, axis=0))
+    second = dot(lefts[1], jnp.concatenate(second, axis=0))
     return [first[:, :WIN], first[:, WIN:], second[:, :WIN], second[:, WIN:]]
-
-
-def head_block(rows):
-    return jnp.concatenate(
-        [jnp.broadcast_to(head_lanes(h), (rows, HALF)) for h in range(HEADS)], axis=0
-    )
 
 
 def taps_of(table, branch):
@@ -283,7 +279,9 @@
         att_scr[TOK_IMG:, :] = jnp.zeros((ROWS - TOK_IMG, D), F32)
 
     gain, shift = s_ref[0:1, :], s_ref[1:2, :]
-    ones = head_block(WIN)
+    ones = jnp.concatenate(
+        [jnp.broadcast_to(head_lanes(h), (WIN, HALF)) for h in range(HEADS)], axis=0
+    )
 
     def project(chunk):
         low, high = CHUNKS[chunk]
@@ -293,8 +291,6 @@
         for part in range(3):
             lanes = slice(part * D, (part + 1) * D)
             piece = dot(a, w_ref[:, lanes]) + s_ref[2 + part : 3 + part, :]
-            if part == 0:
-                piece = piece * (SCALE * LOG2E)
             for branch in range(2):
                 qkv_scr[branch, low:high, part * HALF : (part + 1) * HALF] = piece[
                     :, branch * HALF : (branch + 1) * HALF
@@ -334,7 +330,7 @@
             exps = []
             for part in scores:
                 peak = jnp.max(part, axis=-1, keepdims=True)
-                exps.append(jnp.exp2(part - peak).astype(BF))
+                exps.append(jnp.exp2((part - peak) * (SCALE * LOG2E)).astype(BF))
             e = jnp.concatenate(exps, axis=1)
             e_ref[0, 2 * pair + member] = e
             state[member] = v, e
@@ -361,7 +357,7 @@
             inv = 1.0 / both[:, HALF:]
             o = both[:, :HALF] * inv
             il_ref[0, at] = inv
-            o_ref[0, at] = o.astype(BF)
+            o_ref[0, at] = o
             conv = state[2][:, member * HALF : (member + 1) * HALF]
             piece = o + s_ref[14:15, lanes] + conv
             if kind_of(pair) == 1:
@@ -382,10 +378,10 @@
     att_ref[0] = att_scr[...].astype(BF)
 
 
-def gelu_parts(v):
-    above = lax.erf(v) + 1.0
-    decay = jnp.exp2((v * v) * -LOG2E)
-    return v * above, above + (v * decay) * (2 / np.sqrt(np.pi))
+def gelu_parts(u):
+    above = lax.erf(u * 2**-0.5) + 1.0
+    decay = jnp.exp2((u * u) * (-0.5 * LOG2E))
+    return u * above, above + (u * decay) * (2 / np.pi) ** 0.5
 
 
 def beside(*streams):
@@ -454,7 +450,7 @@
     lanes_of = [slice(part * D, (part + 1) * D) for part in range(FF // D)]
     count = 16
     rows = range(0, ROWS, count)
-    biases = [s_ref[18 + part : 19 + part, :] * ROOT for part in range(FF // D)]
+    biases = [s_ref[18 + part : 19 + part, :] for part in range(FF // D)]
     sums = {}
     held = {}
 
@@ -487,7 +483,7 @@
         hat, scale = normalise(x1)
         rs_scr[own, :] = scale
         keep("hat", at, hat.astype(BF))
-        keep("h2", at, (hat * (gain * ROOT) + shift * ROOT).astype(BF))
+        keep("h2", at, (hat * gain + shift).astype(BF))
 
     def hidden(part):
         cols = slice(D + part * D, D + (part + 1) * D)
@@ -528,7 +524,7 @@
 
     def out_store(at):
         own = slice(at, at + count)
-        out = x1_scr[own, :] + held["out"][own] * ROOT + s_ref[22:23, :]
+        out = x1_scr[own, :] + held["out"][own] * 0.5 + s_ref[22:23, :]
         store_rows(out_ref, at, at + count, out)
 
     def back_first():
@@ -574,7 +570,7 @@
 
     @pl.when(image == pl.num_programs(0) - 1)
     def _():
-        turn_scr[...] = gdn_scr[...].T * ROOT
+        turn_scr[...] = gdn_scr[...].T * 0.5
         for owner, part, low in down_blocks(shard):
             pack_scr[owner * shard : (owner + 1) * shard, part * D : (part + 1) * D] = turn_scr[
                 low : low + shard, :
@@ -661,12 +657,13 @@
             grad_scr[at * QROWS : (at + 1) * QROWS, :] = grad
             v = win_ref[0, at, :, 2 * HALF :]
             pad_scr[at, EDGE : EDGE + QROWS, :] = first_rows(v.astype(F32), tokens_of(pair))
-            dn = grad * il_ref[0, at]
-            z = pltpu.roll(dn * o_ref[0, at].astype(F32), HALF // 2, 1).astype(BF)
-            dn = dn.astype(BF)
-            rows = z * lane_half(True), z * lane_half(False)
+            dn = (grad * il_ref[0, at]).astype(BF)
+            z = pltpu.roll(dn.astype(F32) * o_ref[0, at], HALF // 2, 1)
+            high = z.astype(BF)
+            rows = high * lane_half(True), high * lane_half(False)
+            rest = (z - high.astype(F32)).astype(BF)
             v = jnp.concatenate([v, none], axis=0).T
-            state[member] = grad, dn, by_two_heads(dn, rows, v, minus)
+            state[member] = grad, dn, by_two_heads(dn, rows, v, minus, rest)
             yield
 
     def score(pair, state):
@@ -733,7 +730,7 @@
             at = 2 * pair + member
             branch = branch_of(pair, member)
             dq, dk, dv = state[member]
-            dk = jnp.concatenate(dk, axis=0).T[:QROWS] * LN2
+            dk = jnp.concatenate(dk, axis=0).T[:QROWS] * SCALE
             dv = jnp.concatenate(dv, axis=0).T[:QROWS]
             dv = dv + state[2][:, member * HALF : (member + 1) * HALF]
             for part, piece in enumerate((dq * SCALE, dk, dv)):
@@ -842,7 +839,7 @@
         ((2 * PAIRS, QROWS, 3 * HALF), BF),
         ((2 * PAIRS, QROWS, HEADS * WIN), BF),
         ((2 * PAIRS, QROWS, HALF), F32),
-        ((2 * PAIRS, QROWS, HALF), BF),
+        ((2 * PAIRS, QROWS, HALF), F32),
     ]
     return pl.pallas_call(
         attend_kernel,

time: 159 us -> 161 us (1.013)
  no operation moved by 1% of the time
where the time goes in v8:
time: 161 us; the launch traced here: 160 us
  Pallas kernels  113 us (70%)
  starting transfers between devices  32.1 us (20%)
  waiting for transfers between devices  9.35 us (6%)
  local copies, waits for them, and re-layouts  2.49 us (2%)
  other arithmetic  1.72 us (1%)
    pallas_call x1, Pallas kernels, run_feed(): pl.pallas_call(functools.partial(feed_kernel, shard), grid_spec=pltpu.Pre...  34.6 us
    all_to_all x5, starting transfers between devices, send_terms(): lax.all_to_all(values.reshape(count, -1, values.shape[-1]), 'fsdp', 0, 0)  31.9 us
    pallas_call x1, Pallas kernels, run_back(): pl.pallas_call(functools.partial(back_kernel, spans, places), grid=(image...  31.3 us
    pallas_call x1, Pallas kernels, run_attend(): pl.pallas_call(attend_kernel, grid=(images,), in_specs=[tokens(), whole(w...  22.2 us
    pallas_call x2, Pallas kernels, run_input(): pl.pallas_call(input_kernel, grid=(high - low,), in_specs=[own, rows, own...  15.9 us
    pallas_call x1, Pallas kernels, run_norm(): pl.pallas_call(norm_kernel, grid=(tokens_in.shape[0] // rows,), in_specs=...  7.53 us
    all_to_all x5, waiting for transfers between devices, send_terms(): lax.all_to_all(values.reshape(count, -1, values.shape[-1]), 'fsdp', 0, 0)  5.31 us
    ppermute x3, waiting for transfers between devices, to_other(): return lax.ppermute(values, 'dp', [(0, 1), (1, 0)])  4.04 us
  transfers between devices with their start and end apart: 8, of which 7 were waited for; matrix products, arithmetic and copies ran while one was open for 1% of the time, Pallas kernels for 48%

profile of v8, /device:TPU:0, one launch (start us, length us, event | category | flops | bytes accessed | tf_op | source)
XLA Modules:
  0.0 160.0 jit_solution(5093953106355620341)
XLA Ops:
  0.6 0.7 convert_element_type.13
  1.3 0.1 reshape.54
  1.4 0.8 slice.23
  2.2 0.7 broadcast_in_dim.2
  3.0 8.3 %all-to-all-start = ((bf16[16,8,896]{2,1,0:T(8,128)(2,1)}), bf16[16,8,896]{2,1,0:T(8,128)(2,1)S(1)}, u32[]{:S(2)}, u32[]{:S(2)}) async-start(bf16[16,8,896]{2,1,0:T(8,128)(2,1)} %broadcast_in_dim.2), calls=%async_computation | async-start | bytes 458752 | tf_op jit(solution)/shard_map/all_to_all | solution.py:1073
  11.3 7.5 %norm.1 = (f32[5440,256]{1,0:T(8,128)}, bf16[16,16,2304]{2,1,0:T(8,128)(2,1)}) custom-call(f32[5440,256]{1,0:T(8,128)} %x_ref.7, f32[16,2048]{1,0:T(8,128)} %ww_ref.3, f32[64,256]{1,0:T(8,128)} %dw_ref.3), custom_call_target="tpu_custom_call" | custom-call | tf_op jit(solution)/shard_map/norm/pallas_call | solution.py:821
  18.8 1.7 %all-to-all-done = bf16[16,8,896]{2,1,0:T(8,128)(2,1)S(1)} async-done(((bf16[16,8,896]{2,1,0:T(8,128)(2,1)}), bf16[16,8,896]{2,1,0:T(8,128)(2,1)S(1)}, u32[]{:S(2)}, u32[]{:S(2)}) %all-to-all-start) | async-done | bytes 229408 | tf_op jit(solution)/shard_map/all_to_all | solution.py:1073
  20.5 5.2 %all-to-all-start.1 = ((bf16[16,16,2304]{2,1,0:T(8,128)(2,1)}), bf16[16,16,2304]{2,1,0:T(8,128)(2,1)}, u32[]{:S(2)}, u32[]{:S(2)}) async-start(bf16[16,16,2304]{2,1,0:T(8,128)(2,1)} %get-tuple-element.61), calls=%async_computation.1 | async-start | bytes 2359296 | tf_op jit(solution)/shard_map/all_to_all | solution.py:1073
  25.8 0.1 collective-permute-start
  25.9 1.5 collective-permute-done
  27.4 0.1 pad_maximum_fusion
  27.5 0.0 copy-start.8
  27.5 0.8 reshape.63.s_ref
  28.3 0.0 copy-done.8
  28.3 22.2 %attend.1 = (bf16[8,688,256]{2,1,0:T(8,128)(2,1)}, bf16[8,688,256]{2,1,0:T(8,128)(2,1)}, bf16[8,14,112,384]{3,2,1,0:T(8,128)(2,1)}, bf16[8,14,112,512]{3,2,1,0:T...) custom-call(f32[5440,256]{1,0:T(8,128)} %get-tuple-element.58.x_ref, bf16[256,896]{1,0:T(8,128)(2,1)} %bitcast.13, ...), custom_call_target="tpu_custom_call" | custom-call | tf_op jit(solution)/shard_map/attend/pallas_call | solution.py:844
  50.5 1.7 %all-to-all-done.1 = bf16[16,16,2304]{2,1,0:T(8,128)(2,1)} async-done(((bf16[16,16,2304]{2,1,0:T(8,128)(2,1)}), bf16[16,16,2304]{2,1,0:T(8,128)(2,1)}, u32[]{:S(2)}, u32[]{:S(2)}) %all-to-all-start.1) | async-done | bytes 1179680 | tf_op jit(solution)/shard_map/all_to_all | solution.py:1073
  52.3 34.6 %feed.1 = (f32[5440,256]{1,0:T(8,128)}, f32[5440,256]{1,0:T(8,128)}, bf16[8,688,256]{2,1,0:T(8,128)(2,1)}, bf16[256,2304]{1,0:T(8,128)(2,1)}, f32[5,8,256]{2,1,0:T(8,128)}, /*index=5*/f32[8,1024]{1,0:T(8,128)}) custom-call(s32[8]{0:T(128)} %cnt_ref.1, f32[5440,256]{1,0:T(8,128)} %x_ref.7, f32[5440,256]{1,0:T(8,128)} %c_ref.1, ...), custom_call_target="tpu_custom_call" | custom-call | tf_op jit(solution)/shard_map/feed/pallas_call | solution.py:863
  86.9 6.1 %all-to-all-start.2 = ((bf16[16,16,2304]{2,1,0:T(8,128)(2,1)}), bf16[16,16,2304]{2,1,0:T(8,128)(2,1)S(1)}, u32[]{:S(2)}, u32[]{:S(2)}) async-start(bf16[16,16,2304]{2,1,0:T(8,128)(2,1)} %bitcast.17), calls=%async_computation.2 | async-start | bytes 2359296 | tf_op jit(solution)/shard_map/all_to_all | solution.py:1073
  93.0 31.3 %back.1 = (bf16[8,688,768]{2,1,0:T(8,128)(2,1)}, bf16[256,896]{1,0:T(8,128)(2,1)}) custom-call(bf16[8,688,256]{2,1,0:T(8,128)(2,1)} %get-tuple-element.64.datt_ref, bf16[8,14,112,384]{3,2,1,0:T(8,128)(2,1)} %get-tuple-element.65.win_ref, bf16[8,14,112,512]{3,2,1,0:T(8,128)(2,1)} %get-tuple-element.66.e_ref, f32[8,14,112,128]{3,2,1,0:T(8,128)} %get-tuple-element.67.il_ref, ...), custom_call_target="tpu_custom_call" | custom-call | tf_op jit(solution)/shard_map/back/pallas_call | solution.py:911
  124.3 0.0 all-to-all-done.2
  124.4 6.9 %all-to-all-start.3 = ((bf16[16,16,896]{2,1,0:T(8,128)(2,1)}), bf16[16,16,896]{2,1,0:T(8,128)(2,1)S(1)}, u32[]{:S(2)}, u32[]{:S(2)}) async-start(bf16[16,16,896]{2,1,0:T(8,128)(2,1)} %bitcast.18), calls=%async_computation.3 | async-start | bytes 917504 | tf_op jit(solution)/shard_map/all_to_all | solution.py:1073
  131.3 0.2 convert_reduce_fusion.gl_ref
  131.4 0.1 collective-permute-start.1
  131.5 1.4 collective-permute-done.1.gl_other_ref
  132.9 0.0 copy-start
  132.9 0.0 copy-start.1
  132.9 0.0 copy-start.2
  132.9 0.0 copy-start.3
  132.9 0.0 copy-start.6
  132.9 0.0 copy-start.7
  132.9 0.0 copy-start.9
  132.9 0.0 copy-start.10
  132.9 0.0 copy-start.11
  132.9 0.0 copy-start.12
  133.0 9.4 %input_grad.2.out_refs_0_ = f32[5440,256]{1,0:T(8,128)} custom-call(f32[5440,256]{1,0:T(8,128)} %x_ref.7, bf16[8,688,768]{2,1,0:T(8,128)(2,1)} %get-tuple-element.76.dqkv_ref, f32[5440,256]{1,0:T(8,128)} %get-tuple-element.77.dx_ref, bf16[256,896]{1,0:T(8,128)(2,1)} %bitcast.15, f32[23,256]{1,0:T(8,128)} %reshape.63.s_ref), custom_call_target="tpu_custom_call" | custom-call | flops 1352663040 | bytes 15851520 | tf_op jit(solution)/shard_map/input_grad/pallas_call | solution.py:939
  142.4 1.5 all-to-all-done.3
  143.9 0.1 convert_reduce_fusion.1.gq_ref
  144.0 0.1 collective-permute-start.2
  144.1 1.2 collective-permute-done.2.gq_other_ref
  145.3 0.0 copy-done
  145.3 0.0 copy-done.1
  145.3 0.0 copy-done.2
  145.3 0.0 copy-done.3
  145.3 0.0 copy-done.6
  145.3 0.0 copy-done.7
  145.3 0.9 moment.1
  146.2 5.4 %all-to-all-start.4 = ((f32[16,8,128]{2,1,0:T(8,128)}), f32[16,8,128]{2,1,0:T(8,128)S(1)}, u32[]{:S(2)}, u32[]{:S(2)}) async-start(f32[16,8,128]{2,1,0:T(8,128)} %get-tuple-element.82), calls=%async_computation.4 | async-start | bytes 131072 | tf_op jit(solution)/shard_map/all_to_all | solution.py:1073
  151.6 0.0 copy-done.9
  151.6 0.0 copy-done.10
  151.6 0.0 copy-done.11
  151.6 0.0 copy-done.12
  151.7 0.7 multiply_add_fusion
  152.3 0.0 copy-start.4
  152.3 0.0 copy-start.5
  152.3 6.5 %input_grad.3 = f32[5440,256]{1,0:T(8,128)} custom-call(f32[5440,256]{1,0:T(8,128)} %x_ref.7, bf16[8,688,768]{2,1,0:T(8,128)(2,1)} %get-tuple-element.76.dqkv_ref, f32[5440,256]{1,0:T(8,128)} %get-tuple-element.77.dx_ref, bf16[256,896]{1,0:T(8,128)(2,1)} %bitcast.16, f32[23,256]{1,0:T(8,128)} %reshape.63.s_ref, ...), custom_call_target="tpu_custom_call", output_to_operand_aliasing={{}: (5, {})} | custom-call | flops 811597824 | bytes 9510912 | tf_op jit(solution)/shard_map/input_grad/pallas_call | solution.py:939
  158.8 0.3 all-to-all-done.4.sq_ref
  159.1 0.0 copy-done.4
  159.1 0.0 copy-done.5
  159.1 0.9 update.1
  (4 shorter events, 0.1 us)
Async XLA Ops:
  3.0 17.6 %all-to-all-start = ((bf16[16,8,896]{2,1,0:T(8,128)(2,1)}), bf16[16,8,896]{2,1,0:T(8,128)(2,1)S(1)}, u32[]{:S(2)}, u32[]{:S(2)}) async-start(bf16[16,8,896]{2,1,0:T(8,128)(2,1)} %broadcast_in_dim.2), calls=%async_computation | async-start | bytes 458752 | tf_op jit(solution)/shard_map/all_to_all | solution.py:1073
  20.5 31.7 %all-to-all-start.1 = ((bf16[16,16,2304]{2,1,0:T(8,128)(2,1)}), bf16[16,16,2304]{2,1,0:T(8,128)(2,1)}, u32[]{:S(2)}, u32[]{:S(2)}) async-start(bf16[16,16,2304]{2,1,0:T(8,128)(2,1)} %get-tuple-element.61), calls=%async_computation.1 | async-start | bytes 2359296 | tf_op jit(solution)/shard_map/all_to_all | solution.py:1073
  25.8 1.6 collective-permute-start
  27.5 0.8 copy-start.8
  86.9 37.5 %all-to-all-start.2 = ((bf16[16,16,2304]{2,1,0:T(8,128)(2,1)}), bf16[16,16,2304]{2,1,0:T(8,128)(2,1)S(1)}, u32[]{:S(2)}, u32[]{:S(2)}) async-start(bf16[16,16,2304]{2,1,0:T(8,128)(2,1)} %bitcast.17), calls=%async_computation.2 | async-start | bytes 2359296 | tf_op jit(solution)/shard_map/all_to_all | solution.py:1073
  124.4 19.6 %all-to-all-start.3 = ((bf16[16,16,896]{2,1,0:T(8,128)(2,1)}), bf16[16,16,896]{2,1,0:T(8,128)(2,1)S(1)}, u32[]{:S(2)}, u32[]{:S(2)}) async-start(bf16[16,16,896]{2,1,0:T(8,128)(2,1)} %bitcast.18), calls=%async_computation.3 | async-start | bytes 917504 | tf_op jit(solution)/shard_map/all_to_all | solution.py:1073
  131.4 1.4 collective-permute-start.1
  132.9 12.4 %copy-start = (f32[16,2048]{1,0:T(8,128)S(1)}, f32[16,2048]{1,0:T(8,128)}, u32[]{:S(2)}) copy-start(f32[16,2048]{1,0:T(8,128)} %ww_ref.3) | copy-start | bytes 393220
  132.9 12.4 %copy-start.1 = (f32[64,256]{1,0:T(8,128)S(1)}, f32[64,256]{1,0:T(8,128)}, u32[]{:S(2)}) copy-start(f32[64,256]{1,0:T(8,128)} %dw_ref.3) | copy-start | bytes 196612
  132.9 12.4 %copy-start.2 = (f32[16,2048]{1,0:T(8,128)S(1)}, f32[16,2048]{1,0:T(8,128)}, u32[]{:S(2)}) copy-start(f32[16,2048]{1,0:T(8,128)} %wm_ref.1) | copy-start | bytes 393220
  132.9 12.4 %copy-start.3 = (f32[16,2048]{1,0:T(8,128)S(1)}, f32[16,2048]{1,0:T(8,128)}, u32[]{:S(2)}) copy-start(f32[16,2048]{1,0:T(8,128)} %wv_ref.1) | copy-start | bytes 393220
  132.9 12.4 %copy-start.6 = (f32[64,256]{1,0:T(8,128)S(1)}, f32[64,256]{1,0:T(8,128)}, u32[]{:S(2)}) copy-start(f32[64,256]{1,0:T(8,128)} %dm_ref.1) | copy-start | bytes 196612
  132.9 12.4 %copy-start.7 = (f32[64,256]{1,0:T(8,128)S(1)}, f32[64,256]{1,0:T(8,128)}, u32[]{:S(2)}) copy-start(f32[64,256]{1,0:T(8,128)} %dv_ref.1) | copy-start | bytes 196612
  132.9 18.7 %copy-start.9 = (f32[368]{0:T(512)S(1)}, f32[368]{0:T(512)}, u32[]{:S(2)}) copy-start(f32[368]{0:T(512)} %param.30) | copy-start | bytes 4420
  132.9 18.7 %copy-start.10 = (f32[368]{0:T(512)S(1)}, f32[368]{0:T(512)}, u32[]{:S(2)}) copy-start(f32[368]{0:T(512)} %param.33) | copy-start | bytes 4420
  132.9 18.7 %copy-start.11 = (f32[368]{0:T(512)S(1)}, f32[368]{0:T(512)}, u32[]{:S(2)}) copy-start(f32[368]{0:T(512)} %param.31) | copy-start | bytes 4420
  132.9 18.7 %copy-start.12 = (f32[368]{0:T(512)S(1)}, f32[368]{0:T(512)}, u32[]{:S(2)}) copy-start(f32[368]{0:T(512)} %param.32) | copy-start | bytes 4420
  144.0 1.3 collective-permute-start.2
  146.2 12.9 %all-to-all-start.4 = ((f32[16,8,128]{2,1,0:T(8,128)}), f32[16,8,128]{2,1,0:T(8,128)S(1)}, u32[]{:S(2)}, u32[]{:S(2)}) async-start(f32[16,8,128]{2,1,0:T(8,128)} %get-tuple-element.82), calls=%async_computation.4 | async-start | bytes 131072 | tf_op jit(solution)/shard_map/all_to_all | solution.py:1073
  152.3 6.8 %copy-start.4 = (f32[16,2048]{1,0:T(8,128)S(1)}, f32[16,2048]{1,0:T(8,128)}, u32[]{:S(2)}) copy-start(f32[16,2048]{1,0:T(8,128)} %we_ref.1) | copy-start | bytes 393220
  152.3 6.8 %copy-start.5 = (f32[64,256]{1,0:T(8,128)S(1)}, f32[64,256]{1,0:T(8,128)}, u32[]{:S(2)}) copy-start(f32[64,256]{1,0:T(8,128)} %de_ref.1) | copy-start | bytes 196612

commit v9 on v8

--- a/solution.py
+++ b/solution.py
@@ -178,11 +178,6 @@
     return jnp.concatenate([values * head_lanes(h) for h in range(HEADS)], axis=0)
 
 
-def lane_half(upper):
-    lanes = lax.broadcasted_iota(jnp.int32, (1, HALF), 1)
-    return jnp.where((lanes >= HALF // 2) == upper, 1.0, 0.0).astype(BF)
-
-
 def two_heads(turned, pair):
     low = pair * 2 * HEAD
     none = jnp.zeros((HEAD, WIN), turned.dtype)
@@ -192,11 +187,11 @@
 
 
 def by_two_heads(left, other, turned, added, rest=None):
-    low, high = lane_half(False), lane_half(True)
     none = jnp.zeros_like(added)
     first = [two_heads(turned, 0), added, none, added]
     second = [added, two_heads(turned, 1), added, none]
-    lefts = [left * low + other[0], left * high + other[1]]
+    upper = lax.broadcasted_iota(jnp.int32, left.shape, 1) >= HALF // 2
+    lefts = [jnp.where(upper, other[0], left), jnp.where(upper, left, other[1])]
     if rest is None:
         first, second = first[:2], second[:2]
     else:
@@ -660,7 +655,7 @@
             dn = (grad * il_ref[0, at]).astype(BF)
             z = pltpu.roll(dn.astype(F32) * o_ref[0, at], HALF // 2, 1)
             high = z.astype(BF)
-            rows = high * lane_half(True), high * lane_half(False)
+            rows = high, high
             rest = (z - high.astype(F32)).astype(BF)
             v = jnp.concatenate([v, none], axis=0).T
             state[member] = grad, dn, by_two_heads(dn, rows, v, minus, rest)

time: 161 us -> 161 us (level)
  no operation moved by 1% of the time
where the time goes in v9:
time: 161 us; the launch traced here: 160 us
  Pallas kernels  114 us (71%)
  starting transfers between devices  31.7 us (20%)
  waiting for transfers between devices  9.38 us (6%)
  local copies, waits for them, and re-layouts  2.49 us (2%)
  other arithmetic  1.72 us (1%)
    pallas_call x1, Pallas kernels, run_feed(): pl.pallas_call(functools.partial(feed_kernel, shard), grid_spec=pltpu.Pre...  34.6 us
    all_to_all x5, starting transfers between devices, send_terms(): lax.all_to_all(values.reshape(count, -1, values.shape[-1]), 'fsdp', 0, 0)  31.5 us
    pallas_call x1, Pallas kernels, run_back(): pl.pallas_call(functools.partial(back_kernel, spans, places), grid=(image...  31.3 us
    pallas_call x1, Pallas kernels, run_attend(): pl.pallas_call(attend_kernel, grid=(images,), in_specs=[tokens(), whole(w...  22.7 us
    pallas_call x2, Pallas kernels, run_input(): pl.pallas_call(input_kernel, grid=(high - low,), in_specs=[own, rows, own...  15.9 us
    pallas_call x1, Pallas kernels, run_norm(): pl.pallas_call(norm_kernel, grid=(tokens_in.shape[0] // rows,), in_specs=...  7.53 us
    all_to_all x5, waiting for transfers between devices, send_terms(): lax.all_to_all(values.reshape(count, -1, values.shape[-1]), 'fsdp', 0, 0)  5.34 us
    ppermute x3, waiting for transfers between devices, to_other(): return lax.ppermute(values, 'dp', [(0, 1), (1, 0)])  4.04 us
  transfers between devices with their start and end apart: 8, of which 7 were waited for; matrix products, arithmetic and copies ran while one was open for 1% of the time, Pallas kernels for 48%

profile of v9, /device:TPU:0, one launch (start us, length us, event | category | flops | bytes accessed | tf_op | source)
XLA Modules:
  0.0 160.0 jit_solution(12452921954227760377)
XLA Ops:
  0.6 0.7 convert_element_type.13
  1.3 0.1 reshape.54
  1.4 0.8 slice.23
  2.2 0.7 broadcast_in_dim.2
  3.0 8.3 %all-to-all-start = ((bf16[16,8,896]{2,1,0:T(8,128)(2,1)}), bf16[16,8,896]{2,1,0:T(8,128)(2,1)S(1)}, u32[]{:S(2)}, u32[]{:S(2)}) async-start(bf16[16,8,896]{2,1,0:T(8,128)(2,1)} %broadcast_in_dim.2), calls=%async_computation | async-start | bytes 458752 | tf_op jit(solution)/shard_map/all_to_all | solution.py:1068
  11.3 7.5 %norm.1 = (f32[5440,256]{1,0:T(8,128)}, bf16[16,16,2304]{2,1,0:T(8,128)(2,1)}) custom-call(f32[5440,256]{1,0:T(8,128)} %x_ref.7, f32[16,2048]{1,0:T(8,128)} %ww_ref.3, f32[64,256]{1,0:T(8,128)} %dw_ref.3), custom_call_target="tpu_custom_call" | custom-call | tf_op jit(solution)/shard_map/norm/pallas_call | solution.py:816
  18.8 1.7 %all-to-all-done = bf16[16,8,896]{2,1,0:T(8,128)(2,1)S(1)} async-done(((bf16[16,8,896]{2,1,0:T(8,128)(2,1)}), bf16[16,8,896]{2,1,0:T(8,128)(2,1)S(1)}, u32[]{:S(2)}, u32[]{:S(2)}) %all-to-all-start) | async-done | bytes 229408 | tf_op jit(solution)/shard_map/all_to_all | solution.py:1068
  20.5 5.2 %all-to-all-start.1 = ((bf16[16,16,2304]{2,1,0:T(8,128)(2,1)}), bf16[16,16,2304]{2,1,0:T(8,128)(2,1)}, u32[]{:S(2)}, u32[]{:S(2)}) async-start(bf16[16,16,2304]{2,1,0:T(8,128)(2,1)} %get-tuple-element.61), calls=%async_computation.1 | async-start | bytes 2359296 | tf_op jit(solution)/shard_map/all_to_all | solution.py:1068
  25.8 0.1 collective-permute-start
  25.9 1.5 collective-permute-done
  27.4 0.1 pad_maximum_fusion
  27.5 0.0 copy-start.8
  27.5 0.8 reshape.63.s_ref
  28.3 0.0 copy-done.8
  28.3 22.7 %attend.1 = (bf16[8,688,256]{2,1,0:T(8,128)(2,1)}, bf16[8,688,256]{2,1,0:T(8,128)(2,1)}, bf16[8,14,112,384]{3,2,1,0:T(8,128)(2,1)}, bf16[8,14,112,512]{3,2,1,0:T...) custom-call(f32[5440,256]{1,0:T(8,128)} %get-tuple-element.58.x_ref, bf16[256,896]{1,0:T(8,128)(2,1)} %bitcast.13, ...), custom_call_target="tpu_custom_call" | custom-call | tf_op jit(solution)/shard_map/attend/pallas_call | solution.py:839
  51.0 1.3 all-to-all-done.1
  52.3 34.6 %feed.1 = (f32[5440,256]{1,0:T(8,128)}, f32[5440,256]{1,0:T(8,128)}, bf16[8,688,256]{2,1,0:T(8,128)(2,1)}, bf16[256,2304]{1,0:T(8,128)(2,1)}, f32[5,8,256]{2,1,0:T(8,128)}, /*index=5*/f32[8,1024]{1,0:T(8,128)}) custom-call(s32[8]{0:T(128)} %cnt_ref.1, f32[5440,256]{1,0:T(8,128)} %x_ref.7, f32[5440,256]{1,0:T(8,128)} %c_ref.1, ...), custom_call_target="tpu_custom_call" | custom-call | tf_op jit(solution)/shard_map/feed/pallas_call | solution.py:858
  86.9 6.1 %all-to-all-start.2 = ((bf16[16,16,2304]{2,1,0:T(8,128)(2,1)}), bf16[16,16,2304]{2,1,0:T(8,128)(2,1)S(1)}, u32[]{:S(2)}, u32[]{:S(2)}) async-start(bf16[16,16,2304]{2,1,0:T(8,128)(2,1)} %bitcast.17), calls=%async_computation.2 | async-start | bytes 2359296 | tf_op jit(solution)/shard_map/all_to_all | solution.py:1068
  93.0 31.3 %back.1 = (bf16[8,688,768]{2,1,0:T(8,128)(2,1)}, bf16[256,896]{1,0:T(8,128)(2,1)}) custom-call(bf16[8,688,256]{2,1,0:T(8,128)(2,1)} %get-tuple-element.64.datt_ref, bf16[8,14,112,384]{3,2,1,0:T(8,128)(2,1)} %get-tuple-element.65.win_ref, bf16[8,14,112,512]{3,2,1,0:T(8,128)(2,1)} %get-tuple-element.66.e_ref, f32[8,14,112,128]{3,2,1,0:T(8,128)} %get-tuple-element.67.il_ref, ...), custom_call_target="tpu_custom_call" | custom-call | tf_op jit(solution)/shard_map/back/pallas_call | solution.py:906
  124.3 0.0 all-to-all-done.2
  124.3 6.9 %all-to-all-start.3 = ((bf16[16,16,896]{2,1,0:T(8,128)(2,1)}), bf16[16,16,896]{2,1,0:T(8,128)(2,1)S(1)}, u32[]{:S(2)}, u32[]{:S(2)}) async-start(bf16[16,16,896]{2,1,0:T(8,128)(2,1)} %bitcast.18), calls=%async_computation.3 | async-start | bytes 917504 | tf_op jit(solution)/shard_map/all_to_all | solution.py:1068
  131.2 0.2 convert_reduce_fusion.gl_ref
  131.4 0.1 collective-permute-start.1
  131.5 1.4 collective-permute-done.1.gl_other_ref
  132.8 0.0 copy-start
  132.8 0.0 copy-start.1
  132.8 0.0 copy-start.2
  132.8 0.0 copy-start.3
  132.8 0.0 copy-start.6
  132.9 0.0 copy-start.7
  132.9 0.0 copy-start.9
  132.9 0.0 copy-start.10
  132.9 0.0 copy-start.11
  132.9 0.0 copy-start.12
  132.9 9.4 %input_grad.2.out_refs_0_ = f32[5440,256]{1,0:T(8,128)} custom-call(f32[5440,256]{1,0:T(8,128)} %x_ref.7, bf16[8,688,768]{2,1,0:T(8,128)(2,1)} %get-tuple-element.76.dqkv_ref, f32[5440,256]{1,0:T(8,128)} %get-tuple-element.77.dx_ref, bf16[256,896]{1,0:T(8,128)(2,1)} %bitcast.15, f32[23,256]{1,0:T(8,128)} %reshape.63.s_ref), custom_call_target="tpu_custom_call" | custom-call | flops 1352663040 | bytes 15851520 | tf_op jit(solution)/shard_map/input_grad/pallas_call | solution.py:934
  142.3 2.0 %all-to-all-done.3 = bf16[16,16,896]{2,1,0:T(8,128)(2,1)S(1)} async-done(((bf16[16,16,896]{2,1,0:T(8,128)(2,1)}), bf16[16,16,896]{2,1,0:T(8,128)(2,1)S(1)}, u32[]{:S(2)}, u32[]{:S(2)}) %all-to-all-start.3) | async-done | bytes 458784 | tf_op jit(solution)/shard_map/all_to_all | solution.py:1068
  144.3 0.1 convert_reduce_fusion.1.gq_ref
  144.4 0.1 collective-permute-start.2
  144.5 1.2 collective-permute-done.2.gq_other_ref
  145.7 0.0 copy-done
  145.7 0.0 copy-done.1
  145.7 0.0 copy-done.2
  145.7 0.0 copy-done.3
  145.7 0.0 copy-done.6
  145.7 0.0 copy-done.7
  145.7 0.9 moment.1
  146.6 5.0 %all-to-all-start.4 = ((f32[16,8,128]{2,1,0:T(8,128)}), f32[16,8,128]{2,1,0:T(8,128)S(1)}, u32[]{:S(2)}, u32[]{:S(2)}) async-start(f32[16,8,128]{2,1,0:T(8,128)} %get-tuple-element.82), calls=%async_computation.4 | async-start | bytes 131072 | tf_op jit(solution)/shard_map/all_to_all | solution.py:1068
  151.6 0.0 copy-done.9
  151.6 0.0 copy-done.10
  151.6 0.0 copy-done.11
  151.6 0.0 copy-done.12
  151.6 0.7 multiply_add_fusion
  152.3 0.0 copy-start.4
  152.3 0.0 copy-start.5
  152.3 6.5 %input_grad.3 = f32[5440,256]{1,0:T(8,128)} custom-call(f32[5440,256]{1,0:T(8,128)} %x_ref.7, bf16[8,688,768]{2,1,0:T(8,128)(2,1)} %get-tuple-element.76.dqkv_ref, f32[5440,256]{1,0:T(8,128)} %get-tuple-element.77.dx_ref, bf16[256,896]{1,0:T(8,128)(2,1)} %bitcast.16, f32[23,256]{1,0:T(8,128)} %reshape.63.s_ref, ...), custom_call_target="tpu_custom_call", output_to_operand_aliasing={{}: (5, {})} | custom-call | flops 811597824 | bytes 9510912 | tf_op jit(solution)/shard_map/input_grad/pallas_call | solution.py:934
  158.8 0.3 all-to-all-done.4.sq_ref
  159.1 0.0 copy-done.4
  159.1 0.0 copy-done.5
  159.1 0.9 update.1
  (4 shorter events, 0.1 us)
Async XLA Ops:
  3.0 17.6 %all-to-all-start = ((bf16[16,8,896]{2,1,0:T(8,128)(2,1)}), bf16[16,8,896]{2,1,0:T(8,128)(2,1)S(1)}, u32[]{:S(2)}, u32[]{:S(2)}) async-start(bf16[16,8,896]{2,1,0:T(8,128)(2,1)} %broadcast_in_dim.2), calls=%async_computation | async-start | bytes 458752 | tf_op jit(solution)/shard_map/all_to_all | solution.py:1068
  20.5 31.7 %all-to-all-start.1 = ((bf16[16,16,2304]{2,1,0:T(8,128)(2,1)}), bf16[16,16,2304]{2,1,0:T(8,128)(2,1)}, u32[]{:S(2)}, u32[]{:S(2)}) async-start(bf16[16,16,2304]{2,1,0:T(8,128)(2,1)} %get-tuple-element.61), calls=%async_computation.1 | async-start | bytes 2359296 | tf_op jit(solution)/shard_map/all_to_all | solution.py:1068
  25.8 1.6 collective-permute-start
  27.5 0.8 copy-start.8
  86.9 37.4 %all-to-all-start.2 = ((bf16[16,16,2304]{2,1,0:T(8,128)(2,1)}), bf16[16,16,2304]{2,1,0:T(8,128)(2,1)S(1)}, u32[]{:S(2)}, u32[]{:S(2)}) async-start(bf16[16,16,2304]{2,1,0:T(8,128)(2,1)} %bitcast.17), calls=%async_computation.2 | async-start | bytes 2359296 | tf_op jit(solution)/shard_map/all_to_all | solution.py:1068
  124.3 20.0 %all-to-all-start.3 = ((bf16[16,16,896]{2,1,0:T(8,128)(2,1)}), bf16[16,16,896]{2,1,0:T(8,128)(2,1)S(1)}, u32[]{:S(2)}, u32[]{:S(2)}) async-start(bf16[16,16,896]{2,1,0:T(8,128)(2,1)} %bitcast.18), calls=%async_computation.3 | async-start | bytes 917504 | tf_op jit(solution)/shard_map/all_to_all | solution.py:1068
  131.4 1.4 collective-permute-start.1
  132.8 12.8 %copy-start = (f32[16,2048]{1,0:T(8,128)S(1)}, f32[16,2048]{1,0:T(8,128)}, u32[]{:S(2)}) copy-start(f32[16,2048]{1,0:T(8,128)} %ww_ref.3) | copy-start | bytes 393220
  132.8 12.8 %copy-start.1 = (f32[64,256]{1,0:T(8,128)S(1)}, f32[64,256]{1,0:T(8,128)}, u32[]{:S(2)}) copy-start(f32[64,256]{1,0:T(8,128)} %dw_ref.3) | copy-start | bytes 196612
  132.8 12.8 %copy-start.2 = (f32[16,2048]{1,0:T(8,128)S(1)}, f32[16,2048]{1,0:T(8,128)}, u32[]{:S(2)}) copy-start(f32[16,2048]{1,0:T(8,128)} %wm_ref.1) | copy-start | bytes 393220
  132.8 12.8 %copy-start.3 = (f32[16,2048]{1,0:T(8,128)S(1)}, f32[16,2048]{1,0:T(8,128)}, u32[]{:S(2)}) copy-start(f32[16,2048]{1,0:T(8,128)} %wv_ref.1) | copy-start | bytes 393220
  132.8 12.9 %copy-start.6 = (f32[64,256]{1,0:T(8,128)S(1)}, f32[64,256]{1,0:T(8,128)}, u32[]{:S(2)}) copy-start(f32[64,256]{1,0:T(8,128)} %dm_ref.1) | copy-start | bytes 196612
  132.9 12.8 %copy-start.7 = (f32[64,256]{1,0:T(8,128)S(1)}, f32[64,256]{1,0:T(8,128)}, u32[]{:S(2)}) copy-start(f32[64,256]{1,0:T(8,128)} %dv_ref.1) | copy-start | bytes 196612
  132.9 18.7 %copy-start.9 = (f32[368]{0:T(512)S(1)}, f32[368]{0:T(512)}, u32[]{:S(2)}) copy-start(f32[368]{0:T(512)} %param.30) | copy-start | bytes 4420
  132.9 18.7 %copy-start.10 = (f32[368]{0:T(512)S(1)}, f32[368]{0:T(512)}, u32[]{:S(2)}) copy-start(f32[368]{0:T(512)} %param.33) | copy-start | bytes 4420
  132.9 18.7 %copy-start.11 = (f32[368]{0:T(512)S(1)}, f32[368]{0:T(512)}, u32[]{:S(2)}) copy-start(f32[368]{0:T(512)} %param.31) | copy-start | bytes 4420
  132.9 18.7 %copy-start.12 = (f32[368]{0:T(512)S(1)}, f32[368]{0:T(512)}, u32[]{:S(2)}) copy-start(f32[368]{0:T(512)} %param.32) | copy-start | bytes 4420
  144.4 1.3 collective-permute-start.2
  146.6 12.5 %all-to-all-start.4 = ((f32[16,8,128]{2,1,0:T(8,128)}), f32[16,8,128]{2,1,0:T(8,128)S(1)}, u32[]{:S(2)}, u32[]{:S(2)}) async-start(f32[16,8,128]{2,1,0:T(8,128)} %get-tuple-element.82), calls=%async_computation.4 | async-start | bytes 131072 | tf_op jit(solution)/shard_map/all_to_all | solution.py:1068
  152.3 6.8 %copy-start.4 = (f32[16,2048]{1,0:T(8,128)S(1)}, f32[16,2048]{1,0:T(8,128)}, u32[]{:S(2)}) copy-start(f32[16,2048]{1,0:T(8,128)} %we_ref.1) | copy-start | bytes 393220
  152.3 6.8 %copy-start.5 = (f32[64,256]{1,0:T(8,128)S(1)}, f32[64,256]{1,0:T(8,128)}, u32[]{:S(2)}) copy-start(f32[64,256]{1,0:T(8,128)} %de_ref.1) | copy-start | bytes 196612
